TPU v7x, 32 devices: a whole 2x2x4 slice. The times are simulated.
32 devices in a mesh: dp: 16 (over z, x, core), tensor: 2 (over y).
Axes of the slice: x: 2, y: 2, z: 4, core: 2. Of those that a mesh axis runs over, the one named last changes fastest.
Arguments:
- hidden_in: bfloat16 [32768, 512], P(('dp', 'tensor')), may hold values from -6 to 6
- w_qkv: bfloat16 [3, 512, 512], P(None, None, 'tensor'), may hold values from -0.25 to 0.25
- qv_bias: float32 [2, 512], P(None, 'tensor'), may hold values from -3 to 3
- w_out: bfloat16 [512, 512], P('tensor'), may hold values from -1 to 1
- out_bias: float32 [512], replicated, may hold values from -3 to 3
- gain1: float32 [512], replicated, may hold values from 0.5 to 1.5
- shift1: float32 [512], replicated, may hold values from -3 to 3
- w_up: bfloat16 [512, 2048], P(None, 'tensor'), may hold values from -0.25 to 0.25
- up_bias: float32 [2048], P('tensor'), may hold values from -3 to 3
- w_down: bfloat16 [2048, 512], P('tensor'), may hold values from -0.125 to 0.125
- down_bias: float32 [512], replicated, may hold values from -3 to 3
- gain2: float32 [512], replicated, may hold values from 0.5 to 1.5
- shift2: float32 [512], replicated, may hold values from -3 to 3
- lengths: int32 [32], P('dp'), may hold values from 640 to 1024, as said below
- head_perm: int32 [8], P('tensor'), may hold values from 0 to 1
- cotangent: bfloat16 [32768, 512], P(('dp', 'tensor')), may hold values from -6 to 6
Outputs:
- out: bfloat16 [32768, 512], P(('dp', 'tensor'))
- x_grad: float32 [32768, 512], P(('dp', 'tensor'))
- w_qkv_grad: float32 [3, 512, 512], P(None, None, 'tensor')
- qv_bias_grad: float32 [2, 512], P(None, 'tensor')
- w_out_grad: float32 [512, 512], P('tensor')
- out_bias_grad: float32 [512], replicated
- gain1_grad: float32 [512], replicated
- shift1_grad: float32 [512], replicated
- w_up_grad: float32 [512, 2048], P(None, 'tensor')
- up_bias_grad: float32 [2048], P('tensor')
- w_down_grad: float32 [2048, 512], P('tensor')
- down_bias_grad: float32 [512], replicated
- gain2_grad: float32 [512], replicated
- shift2_grad: float32 [512], replicated
Inputs may be any that keep to these rules, and one draw needn't show every extreme that they name: `lengths`: slots from a sequence's length up to 1024 are padding; some sequence has all 1024 slots real.
All inputs are finite; a program needn't handle non-finite values.
Results may differ from a plain program's by a relative error of at most 0.013.
The roundings to bfloat16 on the way count: a program that leaves them out, or rounds other values in their place, can miss the bound.
Values may be sent and summed in bfloat16 or wider, within the bound.
No kernel may reach another device: no remote copies, remote signals or barrier semaphores. Data moves between devices by JAX's collectives and lax.ppermute only.
A program may use at most 128 MiB of HBM per device.

v0:
```python
from functools import partial
import math

import jax
import jax.numpy as jnp
from jax import lax
from jax.sharding import PartitionSpec as P

EPSILON = 1e-05


def norm_rows(inputs, norm_gain, norm_shift):
    centre = inputs - jnp.mean(inputs, axis=-1, keepdims=True)
    spread = jnp.mean(centre * centre, axis=-1, keepdims=True)
    return centre * lax.rsqrt(spread + EPSILON) * norm_gain + norm_shift


def swap_halves(blocks, head_perm):
    flipped = jnp.flip(blocks, axis=1)
    chosen = (head_perm == 1).reshape((1, 1, 1, -1) + (1,) * (blocks.ndim - 4))
    return jnp.where(chosen, flipped, blocks)


def block_scores(queries, keys_perm, allowed):
    scaling = 1.0 / math.sqrt(queries.shape[-1])
    scores = (
        jnp.einsum("ahd,bhd->hab", queries, keys_perm, preferred_element_type=jnp.float32) * scaling
    )
    return (jnp.where(allowed.T[:, None, :], scores, -1e30), scaling)


def attend_block(block_items):
    queries, keys_perm, values_perm, allowed = block_items
    scores, scaling = block_scores(queries, keys_perm, allowed)
    row_max = jnp.max(scores, axis=-1, keepdims=True)
    exponent = jnp.exp(scores - row_max)
    row_total = jnp.sum(exponent, axis=-1, keepdims=True)
    attn_probs = (exponent / row_total).astype(jnp.bfloat16)
    context = jnp.einsum(
        "hab,bhd->ahd", attn_probs, values_perm, preferred_element_type=jnp.float32
    )
    return (context.astype(jnp.bfloat16), (row_max + jnp.log(row_total))[..., 0])


def attend_back(block_items):
    queries, keys_perm, values_perm, allowed, log_total, grad_ctx = block_items
    scores, scaling = block_scores(queries, keys_perm, allowed)
    attn_probs = jnp.exp(scores - log_total[..., None])
    probs_low = attn_probs.astype(jnp.bfloat16)
    grad_values = jnp.einsum(
        "hab,ahd->bhd", probs_low, grad_ctx, preferred_element_type=jnp.float32
    )
    grad_probs = jnp.einsum(
        "ahd,bhd->hab", grad_ctx, values_perm, preferred_element_type=jnp.float32
    )
    row_inner = jnp.sum(attn_probs * grad_probs, axis=-1, keepdims=True)
    grad_scores = (attn_probs * (grad_probs - row_inner)).astype(jnp.bfloat16)
    grad_queries = (
        jnp.einsum("hab,bhd->ahd", grad_scores, keys_perm, preferred_element_type=jnp.float32)
        * scaling
    )
    grad_keys = (
        jnp.einsum("hab,ahd->bhd", grad_scores, queries, preferred_element_type=jnp.float32)
        * scaling
    )
    return (grad_queries, grad_keys, grad_values)


def batch_total(members):
    flattened = jnp.concatenate([member.reshape(-1) for member in members])
    summed = lax.psum(flattened, "dp")
    results = []
    offset_at = 0
    for member in members:
        results.append(summed[offset_at : offset_at + member.size].reshape(member.shape))
        offset_at = offset_at + member.size
    return tuple(results)


def local(
    hidden_in,
    w_qkv,
    qv_bias,
    w_out,
    out_bias,
    gain1,
    shift1,
    w_up,
    up_bias,
    w_down,
    down_bias,
    gain2,
    shift2,
    lengths,
    head_perm,
    cotangent,
):
    tensor_count = lax.axis_size("tensor")
    own_rows = hidden_in.shape[0]
    seq_count = lengths.shape[0]
    seq_len = own_rows * tensor_count // seq_count
    half_len = seq_len // 2
    own_seqs = seq_count // tensor_count
    positions = lax.broadcasted_iota(jnp.int32, (seq_count, seq_len), 1)
    valid_every = positions < lengths[:, None]
    own_first = lax.axis_index("tensor") * own_seqs
    own_valid = lax.dynamic_slice_in_dim(valid_every, own_first, own_seqs, 0)
    row_valid = own_valid.reshape(own_rows, 1).astype(jnp.float32)
    rows_all = lax.all_gather(hidden_in, "tensor", axis=0, tiled=True)
    work_seqs = valid_every.shape[0]
    heads_local = head_perm.shape[0]
    local_width = w_qkv.shape[2]
    head_size = local_width // heads_local
    zero_bias = jnp.zeros_like(qv_bias[0])
    bias_all = jnp.stack([qv_bias[0], zero_bias, qv_bias[1]])
    projected = jnp.einsum("rd,cde->rce", rows_all, w_qkv, preferred_element_type=jnp.float32)
    projected = (projected + bias_all[None]).astype(jnp.bfloat16)
    split_qkv = projected.reshape(work_seqs, 2, half_len, 3, heads_local, head_size)
    block_shape = (work_seqs, 2, half_len, heads_local, head_size)
    blocks = work_seqs * 2
    queries = split_qkv[:, :, :, 0]
    keys_perm = swap_halves(split_qkv[:, :, :, 1], head_perm)
    values_perm = swap_halves(split_qkv[:, :, :, 2], head_perm)
    key_valid = swap_halves(
        jnp.broadcast_to(
            valid_every.reshape(work_seqs, 2, half_len, 1), (work_seqs, 2, half_len, heads_local)
        ),
        head_perm,
    )
    flat_items = (
        queries.reshape(blocks, half_len, heads_local, head_size),
        keys_perm.reshape(blocks, half_len, heads_local, head_size),
        values_perm.reshape(blocks, half_len, heads_local, head_size),
        key_valid.reshape(blocks, half_len, heads_local),
    )
    context, log_total = lax.map(attend_block, flat_items)
    context_rows = context.reshape(work_seqs * seq_len, local_width)
    attn_own = lax.psum_scatter(
        jnp.dot(context_rows, w_out, preferred_element_type=jnp.float32),
        "tensor",
        scatter_dimension=0,
        tiled=True,
    )
    sum_z1 = hidden_in.astype(jnp.float32) + attn_own + out_bias
    normed1, norm1_back = jax.vjp(norm_rows, sum_z1, gain1, shift1)
    normed_all = lax.all_gather(normed1.astype(jnp.bfloat16), "tensor", axis=0, tiled=True)
    pre_act = jnp.dot(normed_all, w_up, preferred_element_type=jnp.float32) + up_bias
    act_full, gelu_back = jax.vjp(partial(jax.nn.gelu, approximate=False), pre_act)
    act_low = act_full.astype(jnp.bfloat16)
    ffn_own = lax.psum_scatter(
        jnp.dot(
            lax.slice_in_dim(act_low, 0, own_rows * lax.axis_size("tensor"), axis=0),
            w_down,
            preferred_element_type=jnp.float32,
        ),
        "tensor",
        scatter_dimension=0,
        tiled=True,
    )
    sum_z2 = normed1 + ffn_own + down_bias
    out_full, norm2_back = jax.vjp(norm_rows, sum_z2, gain2, shift2)
    out_rows = (out_full * row_valid).astype(jnp.bfloat16)
    grad_z2, grad_gain2, grad_shift2 = norm2_back(cotangent.astype(jnp.float32) * row_valid)
    grad_ffn = grad_z2.astype(jnp.bfloat16)
    grad_down_bias = jnp.sum(grad_ffn, axis=0, dtype=jnp.float32)
    grad_ffn_all = lax.all_gather(grad_ffn, "tensor", axis=0, tiled=True)
    grad_w_down = jnp.einsum("rf,rd->fd", act_low, grad_ffn_all, preferred_element_type=jnp.float32)
    grad_act = jnp.einsum("rd,fd->rf", grad_ffn_all, w_down, preferred_element_type=jnp.float32)
    grad_pre = gelu_back(grad_act)[0].astype(jnp.bfloat16)
    grad_up_bias = jnp.sum(grad_pre, axis=0, dtype=jnp.float32)
    grad_w_up = jnp.einsum("rd,rf->df", normed_all, grad_pre, preferred_element_type=jnp.float32)
    grad_normed_part = lax.psum_scatter(
        jnp.einsum("rf,df->rd", grad_pre, w_up, preferred_element_type=jnp.float32),
        "tensor",
        scatter_dimension=0,
        tiled=True,
    )
    grad_normed1 = grad_z2 + grad_normed_part
    grad_z1, grad_gain1, grad_shift1 = norm1_back(grad_normed1)
    grad_attn = grad_z1.astype(jnp.bfloat16)
    grad_out_bias = jnp.sum(grad_attn, axis=0, dtype=jnp.float32)
    grad_attn_all = lax.all_gather(grad_attn, "tensor", axis=0, tiled=True)
    grad_w_out = jnp.einsum(
        "rc,rd->cd", context_rows, grad_attn_all, preferred_element_type=jnp.float32
    )
    grad_context = jnp.einsum(
        "rd,cd->rc", grad_attn_all, w_out, preferred_element_type=jnp.float32
    ).astype(jnp.bfloat16)
    back_items = flat_items + (
        log_total,
        grad_context.reshape(blocks, half_len, heads_local, head_size),
    )
    grad_q, grad_k_perm, grad_v_perm = lax.map(attend_back, back_items)
    grad_keys = swap_halves(grad_k_perm.reshape(block_shape), head_perm)
    grad_values = swap_halves(grad_v_perm.reshape(block_shape), head_perm)
    grad_qkv = jnp.stack([grad_q.reshape(block_shape), grad_keys, grad_values], axis=3)
    grad_qkv = grad_qkv.reshape(work_seqs * seq_len, 3, local_width).astype(jnp.bfloat16)
    column_sums = jnp.sum(grad_qkv, axis=0, dtype=jnp.float32)
    grad_qv_bias = jnp.stack([column_sums[0], column_sums[2]])
    grad_w_qkv = jnp.einsum("rd,rce->cde", rows_all, grad_qkv, preferred_element_type=jnp.float32)
    input_part = lax.psum_scatter(
        jnp.einsum("rce,cde->rd", grad_qkv, w_qkv, preferred_element_type=jnp.float32).astype(
            jnp.bfloat16
        ),
        "tensor",
        scatter_dimension=0,
        tiled=True,
    ).astype(jnp.float32)
    x_grad = grad_z1 + input_part
    grad_w_qkv, grad_qv_bias, grad_w_out, grad_w_up, grad_up_bias, grad_w_down = batch_total(
        [grad_w_qkv, grad_qv_bias, grad_w_out, grad_w_up, grad_up_bias, grad_w_down]
    )
    grad_out_bias, grad_gain1, grad_shift1, grad_down_bias, grad_gain2, grad_shift2 = lax.psum(
        (grad_out_bias, grad_gain1, grad_shift1, grad_down_bias, grad_gain2, grad_shift2),
        ("dp", "tensor"),
    )
    return (
        out_rows,
        x_grad,
        grad_w_qkv,
        grad_qv_bias,
        grad_w_out,
        grad_out_bias,
        grad_gain1,
        grad_shift1,
        grad_w_up,
        grad_up_bias,
        grad_w_down,
        grad_down_bias,
        grad_gain2,
        grad_shift2,
    )


def solution(mesh):
    return jax.shard_map(
        local,
        mesh=mesh,
        in_specs=(
            P(("dp", "tensor"), None),
            P(None, None, "tensor"),
            P(None, "tensor"),
            P("tensor", None),
            P(),
            P(),
            P(),
            P(None, "tensor"),
            P("tensor"),
            P("tensor", None),
            P(),
            P(),
            P(),
            P("dp"),
            P("tensor"),
            P(("dp", "tensor"), None),
        ),
        out_specs=(
            P(("dp", "tensor"), None),
            P(("dp", "tensor"), None),
            P(None, None, "tensor"),
            P(None, "tensor"),
            P("tensor", None),
            P(),
            P(),
            P(),
            P(None, "tensor"),
            P("tensor"),
            P("tensor", None),
            P(),
            P(),
            P(),
        ),
        check_vma=False,
    )
```

profile of v0, /device:TPU:5, one launch (start us, length us, event | category | flops | bytes accessed | tf_op | source)
XLA Modules:
  0.0 758.7 jit_solution(13257469692317642926)
XLA Ops:
  10.4 32.5 %all-gather.5.cloned.1.call-done = bf16[2048,512]{1,0:T(8,128)(2,1)} async-done(((bf16[1024,512]{1,0:T(8,128)(2,1)}), bf16[2048,512]{1,0:T(8,128)(2,1)}) %all-gather.5.cloned.1.call-update) | async-done | bytes 2097168 | tf_op jit(solution)/shard_map/all_gather | solution.py:109
  42.9 5.2 add_convert_fusion.1
  48.2 4.7 copy.48
  52.9 6.2 reshape.242
  59.0 4.5 slice_bitcast_fusion
  63.5 5.5 rev.18
  69.1 9.4 %rev.20 = bf16[2,2,512,4,64]{2,1,0,4,3:T(2,128)(2,1)S(1)} reverse(bf16[2,2,512,4,64]{2,1,0,4,3:T(2,128)(2,1)} %get-tuple-element.207), dimensions={1} | reverse | bytes 2097152 | tf_op jit(solution)/shard_map/jit(_flip)/rev | solution.py:19
  78.5 3.7 broadcast_select_fusion
  83.8 21.9 %while.26 = (s32[]{:T(128)}, bf16[4,512,4,64]{1,3,2,0:T(8,128)(2,1)}, f32[4,4,512]{2,1,0:T(4,128)S(1)}, bf16[4,512,4,64]{1,3,2,0:T(8,128)(2,1)}, pred[4,512,4]{1...) while((s32[]{:T(128)}, ...), condition=%wide.region_3.4_spmd, body=%wide.region_0.3_spmd.sunk | while | flops 281147392 | bytes 13709405 | solution.py:136
  86.5 2.9 fusion.123
  91.9 2.9 fusion.123
  97.4 2.9 fusion.123
  102.9 2.9 fusion.123
  105.8 2.8 copy.52
  109.8 2.7 fusion.79
  112.7 54.4 %reduce-scatter.5.cloned.1.call-done = f32[1024,512]{1,0:T(8,128)} async-done(((f32[2048,512]{1,0:T(8,128)}), f32[1024,512]{1,0:T(8,128)}) %reduce-scatter.5.cloned.1.call-update) | async-done | bytes 2097168 | tf_op jit(solution)/shard_map/reduce_scatter | solution.py:138
  167.0 2.2 fusion.75
  171.6 32.8 %all-gather.7.cloned.1.call-done = bf16[2048,512]{1,0:T(8,128)(2,1)} async-done(((bf16[1024,512]{1,0:T(8,128)(2,1)}), bf16[2048,512]{1,0:T(8,128)(2,1)}) %all-gather.7.cloned.1.call-update) | async-done | bytes 2097168 | tf_op jit(solution)/shard_map/all_gather | solution.py:146
  204.4 22.7 %multiply_convert_fusion.1 = (bf16[2048,1024]{1,0:T(8,128)(2,1)S(1)}, f32[2048,1024]{1,0:T(8,128)}, f32[2048,1024]{1,0:T(8,128)}) fusion(f32[1024]{0:T(1024)S(1)} %copy-done.39, bf16[2048,512]{1,0:T(8,128)(2,1)} %all-gather.7.cloned.1.call-done, bf16[512,1024]{1,0:T(8,128)(2,1)S(1)} %copy-done), kind=kOutput, calls=%fused_computation.65 | convolution fusion | flops 2285895680 | bytes 24121344 | tf_op jit(solution)/shard_map/dot_general | solution.py:147
  227.0 2.0 copy-done.17
  229.0 4.4 fusion.80
  235.3 52.6 %reduce-scatter.7.cloned.1.call-done = f32[1024,512]{1,0:T(8,128)} async-done(((f32[2048,512]{1,0:T(8,128)}), f32[1024,512]{1,0:T(8,128)}) %reduce-scatter.7.cloned.1.call-update) | async-done | bytes 2097168 | tf_op jit(solution)/shard_map/reduce_scatter | solution.py:150
  287.9 2.4 fusion.73
  291.9 2.1 fusion.72
  296.8 33.1 %all-gather.9.cloned.1.call-done = bf16[2048,512]{1,0:T(8,128)(2,1)} async-done(((bf16[1024,512]{1,0:T(8,128)(2,1)}), bf16[2048,512]{1,0:T(8,128)(2,1)}) %all-gather.9.cloned.1.call-update) | async-done | bytes 2097168 | tf_op jit(solution)/shard_map/all_gather | solution.py:166
  329.9 10.3 %convert_reduce_fusion = (f32[1024]{0:T(1024)S(1)}, bf16[2048,1024]{1,0:T(8,128)(2,1)S(1)}) fusion(f32[2048,1024]{1,0:T(8,128)} %get-tuple-element.196, bf16[2048,512]{1,0:T(8,128)(2,1)} %all-gather.9.cloned.1.call-done, bf16[1024,512]{1,0:T(8,128)(2,1)} %param.29, f32[2048,1024]{1,0:T(8,128)} %get-tuple-element.217, f32[1024]{0:T(1024)S(1)} %copy-done.39), kind=kOutput, calls=%fused_computation.63 | convolution fusion | flops 2183134208 | bytes 24125440 | tf_op jit(solution)/shard_map/rd,fd->rf/dot_general | solution.py:168
  342.2 4.4 fusion.81
  346.6 54.4 %reduce-scatter.9.cloned.1.call-done = f32[1024,512]{1,0:T(8,128)} async-done(((f32[2048,512]{1,0:T(8,128)}), f32[1024,512]{1,0:T(8,128)}) %reduce-scatter.9.cloned.1.call-update) | async-done | bytes 2097168 | tf_op jit(solution)/shard_map/reduce_scatter | solution.py:172
  401.0 2.8 multiply_reduce_fusion.2
  407.3 4.7 convolution_bitcast_fusion.1
  415.0 2.4 convolution_bitcast_fusion
  419.2 21.3 %all-gather.11.cloned.1.call-done = bf16[2048,512]{1,0:T(8,128)(2,1)} async-done(((bf16[1024,512]{1,0:T(8,128)(2,1)}), bf16[2048,512]{1,0:T(8,128)(2,1)}) %all-gather.11.cloned.1.call-update) | async-done | bytes 2097168 | tf_op jit(solution)/shard_map/all_gather | solution.py:182
  440.5 2.3 convolution_convert_fusion
  442.9 2.0 reshape.260
  444.9 2.9 copy.56
  447.8 38.3 %while.27 = (s32[]{:T(128)}, bf16[4,512,4,64]{1,3,2,0:T(8,128)(2,1)}, bf16[4,512,4,64]{1,3,2,0:T(8,128)(2,1)}, bf16[4,512,4,64]{1,3,2,0:T(8,128)(2,1)}, bf16[4,5...) while((s32[]{:T(128)}, ...), condition=%wide.region_17.18_spmd, body=%wide.region_15.17_spmd.sunk | while | flops 687077376 | bytes 51715300 | solution.py:193
  448.6 2.5 multiply_reduce_fusion.8
  455.2 2.2 fusion.135
  458.2 2.5 multiply_reduce_fusion.8
  464.7 2.2 fusion.135
  467.7 2.5 multiply_reduce_fusion.8
  474.3 2.2 fusion.135
  477.3 2.5 multiply_reduce_fusion.8
  483.9 2.2 fusion.135
  486.1 2.4 copy.74
  488.5 5.5 rev.21
  494.0 2.3 copy.75
  496.4 7.7 %rev.22 = bf16[2,2,512,4,64]{2,1,0,4,3:T(2,128)(2,1)} reverse(bf16[2,2,512,4,64]{2,1,0,4,3:T(2,128)(2,1)S(1)} %copy.75), dimensions={1} | reverse | bytes 2097152 | tf_op jit(solution)/shard_map/jit(_flip)/rev | solution.py:19
  504.0 4.8 select_convert_fusion.1
  514.1 2.9 copy.73
  518.7 2.4 convert_reduce_fusion.1
  521.1 5.2 fusion.66
  526.3 2.0 copy.65
  534.5 19.0 %dynamic-update-slice.3 = f32[1574400]{0:T(1024)} dynamic-update-slice(f32[1574400]{0:T(1024)} %constant_dynamic-update-slice_fusion.1, f32[524288]{0:T(1024)} %bitcast.188, s32[]{} %constant.144) | dynamic-update-slice | bytes 4194308
  554.8 17.9 %dynamic-update-slice.5 = f32[1574400]{0:T(1024)} dynamic-update-slice(f32[1574400]{0:T(1024)} %constant_dynamic-update-slice_fusion, f32[524288]{0:T(1024)S(1)} %bitcast.187, s32[]{} %constant.146) | dynamic-update-slice | bytes 4194308 | tf_op jit(solution)/shard_map/concatenate | solution.py:70
  572.8 42.8 %all-reduce = (f32[512]{0:T(512)}, f32[512]{0:T(512)}, f32[512]{0:T(512)}, f32[512]{0:T(512)}, f32[512]{0:T(512)}, /*index=5*/f32[512]{0:T(512)}) all-reduce(f32[512]{0:T(512)S(1)} %get-tuple-element.186, f32[512]{0:T(512)S(1)} %get-tuple-element.138, ...), channel_id=1, replica_groups=mesh['dp'=16,'tensor'=2] {'dp','tensor'}, use_global_device_ids=true, to_apply=%region_23.24 | all-reduce | flops 3072 | bytes 24576 | tf_op jit(solution)/shard_map/psum | solution.py:213
  615.6 4.3 bitcast_convert_fusion
  619.9 95.6 %all-reduce.3.cloned.1.call-done = f32[1574400]{0:T(1024)} async-done(((f32[1574400]{0:T(1024)}), f32[1574400]{0:T(1024)}) %all-reduce.3.cloned.1.call-update) | async-done | bytes 6297616 | tf_op jit(solution)/shard_map/psum | solution.py:71
  715.6 3.8 fusion.76
  719.4 2.7 reshape.256
  723.6 3.2 slice.90
  726.8 2.8 reshape.255
  735.3 13.6 %reduce-scatter.11.cloned.1.call-done = bf16[1024,512]{1,0:T(8,128)(2,1)} async-done(((bf16[2048,512]{1,0:T(8,128)(2,1)}), bf16[1024,512]{1,0:T(8,128)(2,1)}) %reduce-scatter.11.cloned.1.call-update) | async-done | bytes 1048592 | tf_op jit(solution)/shard_map/reduce_scatter | solution.py:201
  748.9 2.8 convert_add_fusion
  (221 shorter events, 76.1 us)
Async XLA Ops:
  7.2 197.2 %copy-start = (bf16[512,1024]{1,0:T(8,128)(2,1)S(1)}, bf16[512,1024]{1,0:T(8,128)(2,1)}, u32[]{:S(2)}) copy-start(bf16[512,1024]{1,0:T(8,128)(2,1)} %param.27) | copy-start | bytes 3145732
  7.2 35.7 %all-gather.5.cloned.1.call-start = ((), (), s32[]{:S(2)}) async-start(), calls=%async_computation.4 | async-start | bytes 3145728 | tf_op jit(solution)/shard_map/all_gather | solution.py:109
  7.9 159.1 %reduce-scatter.5.cloned.1.call-start = ((), (), s32[]{:S(2)}) async-start(), calls=%async_computation.5 | async-start | bytes 6291456 | tf_op jit(solution)/shard_map/reduce_scatter | solution.py:138
  8.7 69.8 %copy-start.31 = (pred[4]{0:T(512)(128)(4,1)}, pred[4]{0:T(512)(128)(4,1)S(1)}, u32[]{:S(2)}) copy-start(pred[4]{0:T(512)(128)(4,1)S(1)} %broadcast_compare_fusion.1) | copy-start | bytes 16
  78.5 5.1 copy-start.22
  105.8 6.8 copy-start.2
  105.8 6.8 copy-start.4
  105.8 4.1 copy-start.27
  108.8 1.0 copy-start.10
  112.6 54.5 %copy-start.33 = (f32[512]{0:T(512)S(1)}, f32[512]{0:T(512)}, u32[]{:S(2)}) copy-start(f32[512]{0:T(512)} %param.24) | copy-start | bytes 6148
  112.6 57.1 %copy-start.28 = (f32[512]{0:T(512)S(1)}, f32[512]{0:T(512)}, u32[]{:S(2)}) copy-start(f32[512]{0:T(512)} %param.25) | copy-start | bytes 6148
  112.6 57.1 %copy-start.29 = (f32[512]{0:T(512)S(1)}, f32[512]{0:T(512)}, u32[]{:S(2)}) copy-start(f32[512]{0:T(512)} %param.26) | copy-start | bytes 6148
  112.6 91.8 %all-gather.7.cloned.1.call-start = ((), (), s32[]{:S(2)}) async-start(), calls=%async_computation.6 | async-start | bytes 3145728 | tf_op jit(solution)/shard_map/all_gather | solution.py:146
  169.2 35.1 %copy-start.39 = (f32[1024]{0:T(1024)S(1)}, f32[1024]{0:T(1024)}, u32[]{:S(2)}) copy-start(f32[1024]{0:T(1024)} %param.28) | copy-start | bytes 12292
  171.1 116.8 %reduce-scatter.7.cloned.1.call-start = ((), (), s32[]{:S(2)}) async-start(), calls=%async_computation.7 | async-start | bytes 6291456 | tf_op jit(solution)/shard_map/reduce_scatter | solution.py:150
  204.4 24.6 %copy-start.38 = (bf16[1024,512]{1,0:T(8,128)(2,1)S(1)}, bf16[1024,512]{1,0:T(8,128)(2,1)}, u32[]{:S(2)}) copy-start(bf16[1024,512]{1,0:T(8,128)(2,1)} %param.29) | copy-start | bytes 3145732
  227.0 2.0 copy-start.17
  233.4 0.7 copy-start.36
  233.4 54.5 %copy-start.34 = (f32[512]{0:T(512)S(1)}, f32[512]{0:T(512)}, u32[]{:S(2)}) copy-start(f32[512]{0:T(512)} %param.30) | copy-start | bytes 6148
  233.4 96.5 %all-gather.9.cloned.1.call-start = ((), (), s32[]{:S(2)}) async-start(), calls=%async_computation.8 | async-start | bytes 3145728 | tf_op jit(solution)/shard_map/all_gather | solution.py:166
  235.3 55.4 %copy-start.30 = (f32[512]{0:T(512)S(1)}, f32[512]{0:T(512)}, u32[]{:S(2)}) copy-start(f32[512]{0:T(512)} %param.31) | copy-start | bytes 6148
  287.9 2.9 copy-start.21
  290.3 1.7 copy-start.35
  294.1 1.3 copy-start.8
  296.6 104.4 %reduce-scatter.9.cloned.1.call-start = ((), (), s32[]{:S(2)}) async-start(), calls=%async_computation.9 | async-start | bytes 6291456 | tf_op jit(solution)/shard_map/reduce_scatter | solution.py:172
  340.2 2.0 copy-start.40
  346.6 93.9 %all-gather.11.cloned.1.call-start = ((), (), s32[]{:S(2)}) async-start(), calls=%async_computation.10 | async-start | bytes 3145728 | tf_op jit(solution)/shard_map/all_gather | solution.py:182
  404.7 1.3 copy-start.6
  404.7 2.7 copy-start.37
  407.3 308.3 %all-reduce.3.cloned.1.call-start = ((), (), s32[]{:S(2)}) async-start(), calls=%async_computation.12 | async-start | bytes 12599296 | tf_op jit(solution)/shard_map/psum | solution.py:71
  407.3 6.5 copy-start.24
  412.0 3.0 copy-start.18
  419.2 28.6 %copy-start.3 = (bf16[4,512,4,64]{1,3,2,0:T(8,128)(2,1)S(1)}, bf16[4,512,4,64]{1,3,2,0:T(8,128)(2,1)}, u32[]{:S(2)}) copy-start(bf16[4,512,4,64]{1,3,2,0:T(8,128)(2,1)} %copy-done.2) | copy-start | bytes 3145732
  419.2 28.6 %copy-start.5 = (bf16[4,512,4,64]{1,3,2,0:T(8,128)(2,1)S(1)}, bf16[4,512,4,64]{1,3,2,0:T(8,128)(2,1)}, u32[]{:S(2)}) copy-start(bf16[4,512,4,64]{1,3,2,0:T(8,128)(2,1)} %copy-done.4) | copy-start | bytes 3145732
  451.1 1.3 copy-start.14
  451.1 2.1 copy-start.25
  453.2 1.0 copy-start.15
  454.2 1.0 copy-start.26
  460.6 1.3 copy-start.14
  460.7 2.1 copy-start.25
  462.7 1.0 copy-start.15
  463.7 1.0 copy-start.26
  470.2 1.3 copy-start.14
  470.2 2.1 copy-start.25
  472.3 1.0 copy-start.15
  473.3 1.0 copy-start.26
  479.8 1.3 copy-start.14
  479.8 2.1 copy-start.25
  481.9 1.0 copy-start.15
  482.9 1.0 copy-start.26
  486.1 17.9 %copy-start.16 = (bf16[4,512,4,64]{1,3,2,0:T(8,128)(2,1)S(1)}, bf16[4,512,4,64]{1,3,2,0:T(8,128)(2,1)}, u32[]{:S(2)}) copy-start(bf16[4,512,4,64]{1,3,2,0:T(8,128)(2,1)} %get-tuple-element.109) | copy-start | bytes 3145732
  486.1 17.9 %copy-start.32 = (pred[4]{0:T(512)(128)(4,1)S(1)}, pred[4]{0:T(512)(128)(4,1)}, u32[]{:S(2)}) copy-start(pred[4]{0:T(512)(128)(4,1)} %copy-done.31) | copy-start | bytes 16
  518.6 2.4 copy-start.12
  526.3 4.0 copy-start.11
  528.3 2.1 copy-start.23
  530.4 24.4 %copy-start.9 = (f32[128,4,8,128]{3,1,2,0:T(4,128)S(1)}, f32[128,4,8,128]{3,1,2,0:T(4,128)}, u32[]{:S(2)}) copy-start(f32[128,4,8,128]{3,1,2,0:T(4,128)} %copy.85) | copy-start | bytes 6291460
  572.7 42.9 %copy-start.13 = (bf16[2048,1,256]{2,0,1:T(8,128)(2,1)S(1)}, bf16[2048,1,256]{2,0,1:T(8,128)(2,1)}, u32[]{:S(2)}) copy-start(bf16[2048,1,256]{2,0,1:T(8,128)(2,1)} %copy-done.12) | copy-start | bytes 3145732
  572.7 42.9 %copy-start.19 = (bf16[2048,1,256]{2,0,1:T(8,128)(2,1)S(1)}, bf16[2048,1,256]{2,0,1:T(8,128)(2,1)}, u32[]{:S(2)}) copy-start(bf16[2048,1,256]{2,0,1:T(8,128)(2,1)} %copy.62) | copy-start | bytes 3145732
  572.7 42.9 %copy-start.20 = (bf16[2048,1,256]{2,0,1:T(8,128)(2,1)S(1)}, bf16[2048,1,256]{2,0,1:T(8,128)(2,1)}, u32[]{:S(2)}) copy-start(bf16[2048,1,256]{2,0,1:T(8,128)(2,1)} %copy.63) | copy-start | bytes 3145732
  572.7 176.1 %reduce-scatter.11.cloned.1.call-start = ((), (), s32[]{:S(2)}) async-start(), calls=%async_computation.11 | async-start | bytes 3145728 | tf_op jit(solution)/shard_map/reduce_scatter | solution.py:201
  723.6 9.8 %slice-start = ((f32[1574400]{0:T(1024)}), f32[512]{0:T(512)S(1)}, s32[]{:S(2)}) async-start(f32[1574400]{0:T(1024)} %all-reduce.3.cloned.1.call-done), calls=%async_computation.13 | async-start | bytes 4096 | tf_op jit(solution)/shard_map/slice | solution.py:75
  723.6 25.3 %copy-start.7 = (f32[1024,512]{1,0:T(8,128)S(1)}, f32[1024,512]{1,0:T(8,128)}, u32[]{:S(2)}) copy-start(f32[1024,512]{1,0:T(8,128)} %copy-done.6) | copy-start | bytes 6291460
  726.8 24.9 %copy-start.1 = (bf16[512,1024]{1,0:T(8,128)(2,1)S(1)}, bf16[512,1024]{1,0:T(8,128)(2,1)}, u32[]{:S(2)}) copy-start(bf16[512,1024]{1,0:T(8,128)(2,1)} %param.27) | copy-start | bytes 3145732
Sparse Core Ops, SparseCore 0:
  9.6 33.3 all-gather.4
  112.7 54.2 reduce-scatter.4
  171.2 33.1 all-gather.6
  233.5 54.3 reduce-scatter.6
  296.7 33.1 all-gather.8
  346.7 54.2 reduce-scatter.8
  407.4 33.1 all-gather.10
  572.8 142.6 all-reduce.2
  718.5 30.3 reduce-scatter.10
where the time goes:
time: 774 us; the launch traced here: 759 us
  waiting for transfers between devices  391 us (51%)
  local copies, waits for them, and re-layouts  154 us (20%)
  matrix products  113 us (15%)
  blocking collectives  42.8 us (6%)
  other arithmetic  41.4 us (5%)
  between operations  14.9 us (2%)
    psum x1, waiting for transfers between devices, batch_total(): summed = lax.psum(flattened, 'dp')  95.6 us
    reduce_scatter x1, waiting for transfers between devices, local(): lax.psum_scatter(jnp.einsum('rf,df->rd', grad_pre, w_up, preferred_elemen...  54.4 us
    reduce_scatter x1, waiting for transfers between devices, local(): lax.psum_scatter(jnp.dot(context_rows, w_out, preferred_element_type=jnp....  54.4 us
    reduce_scatter x1, waiting for transfers between devices, local(): lax.psum_scatter(jnp.dot(lax.slice_in_dim(act_low, 0, own_rows * lax.axis...  52.6 us
    psum x1, blocking collectives, local(): lax.psum((grad_out_bias, grad_gain1, grad_shift1, grad_down_bias, grad_ga...  42.8 us
    unnamed x85, local copies, waits for them, and re-layouts  39.1 us
    all_gather x1, waiting for transfers between devices, local(): grad_ffn_all = lax.all_gather(grad_ffn, 'tensor', axis=0, tiled=True)  33.1 us
    all_gather x1, waiting for transfers between devices, local(): lax.all_gather(normed1.astype(jnp.bfloat16), 'tensor', axis=0, tiled=True)  32.8 us
  transfers between devices with their start and end apart: 9, of which 9 were waited for; matrix products, arithmetic and copies ran while one was open for 5% of the time, Pallas kernels for 0%

commit v1 on v0

v1 whole, which is shorter than its diff:
```python
import math

import jax
import jax.numpy as jnp
from jax import lax
from jax.sharding import PartitionSpec as P

EPSILON = 1e-05
BF = jnp.bfloat16
F32 = jnp.float32


def ein(spec, a, b):
    return jnp.einsum(spec, a, b, preferred_element_type=F32)


def send_tensor(v):
    n = lax.axis_size("tensor")
    return jax.tree.map(lambda a: lax.ppermute(a, "tensor", [(i, (i + 1) % n) for i in range(n)]), v)


def send_bit(v, bit):
    n = lax.axis_size("dp")
    pairs = [(i, i ^ (1 << bit)) for i in range(n)]
    return jax.tree.map(lambda a: lax.ppermute(a, "dp", pairs), v)


def pick(a, axis, index):
    return lax.dynamic_index_in_dim(a, index, axis, keepdims=False)


def total_chips(buf):
    me = lax.axis_index("dp")
    bits = list(range(1, lax.axis_size("dp").bit_length() - 1))
    split, rest = bits[:3], bits[3:]
    for bit in split:
        side = (me >> bit) & 1
        half = buf.shape[0] // 2
        away = lax.dynamic_slice_in_dim(buf, (1 - side) * half, half, 0)
        kept = lax.dynamic_slice_in_dim(buf, side * half, half, 0)
        buf = (kept.astype(F32) + send_bit(away, bit).astype(F32)).astype(BF)
    for bit in rest:
        buf = (buf.astype(F32) + send_bit(buf, bit).astype(F32)).astype(BF)
    for bit in reversed(split):
        side = (me >> bit) & 1
        got = send_bit(buf, bit)
        first = jnp.where(side == 0, buf, got)
        second = jnp.where(side == 0, got, buf)
        buf = jnp.concatenate([first, second], axis=0)
    return buf


def norm_parts(v):
    centre = v - jnp.mean(v, axis=-1, keepdims=True)
    spread = jnp.mean(centre * centre, axis=-1, keepdims=True)
    inv = lax.rsqrt(spread + EPSILON)
    return centre * inv, inv


def norm_back(g, hat, inv, gain):
    gg = g * gain
    mean_g = jnp.mean(gg, axis=-1, keepdims=True)
    mean_gh = jnp.mean(gg * hat, axis=-1, keepdims=True)
    return (gg - mean_g - hat * mean_gh) * inv


def local(hidden_in, w_qkv, qv_bias, w_out, out_bias, gain1, shift1, w_up, up_bias, w_down,
          down_bias, gain2, shift2, lengths, head_perm, cotangent):
    rows, width = hidden_in.shape
    half = rows // 2
    core = lax.axis_index("dp") % 2
    length = lengths[lax.axis_index("tensor")]
    valid = jnp.arange(rows, dtype=jnp.int32) < length
    row_valid = valid.astype(F32)[:, None]
    pair = w_qkv.shape[2] // 2
    heads = head_perm.shape[0] // 2
    size = pair // heads
    units = up_bias.shape[0] // 2

    def slot(i):
        small = jnp.concatenate([
            pick(qv_bias.reshape(2, 2, pair), 1, i).reshape(-1),
            pick(up_bias.reshape(2, units), 0, i),
            pick(head_perm.reshape(2, heads), 0, i).astype(F32)])
        return (pick(w_qkv.reshape(3, width, 2, pair), 2, i), small,
                pick(w_out.reshape(2, pair, width), 0, i),
                pick(w_up.reshape(width, 2, units), 1, i),
                pick(w_down.reshape(2, units, width), 0, i))

    own_m = slot(core)
    own_p = slot(1 - core)
    other_m = send_tensor(own_m)
    other_p = send_bit(other_m, 0)
    slots = [own_m, own_p, other_m, other_p]

    def flip(a, perm):
        chosen = (perm == 1).reshape((1, 1, heads) + (1,) * (a.ndim - 3))
        return jnp.where(chosen, a[::-1], a)

    scaling = 1.0 / math.sqrt(size)
    kept = []
    attn = 0.0
    for wq, small, wo, _, _ in slots:
        bias = small[: 2 * pair].reshape(2, pair)
        perm = small[2 * pair + units:]
        bias3 = jnp.stack([bias[0], jnp.zeros_like(bias[0]), bias[1]])
        qkv = (ein("rd,cde->cre", hidden_in, wq) + bias3[:, None]).astype(BF)
        qkv = qkv.reshape(3, 2, half, heads, size)
        q, k, v = qkv[0], flip(qkv[1], perm), flip(qkv[2], perm)
        ok = flip(jnp.broadcast_to(valid.reshape(2, half, 1), (2, half, heads)), perm)
        s = ein("iahd,ibhd->ihab", q, k) * scaling
        s = jnp.where(jnp.transpose(ok, (0, 2, 1))[:, :, None, :], s, -1e30)
        m = jnp.max(s, axis=-1, keepdims=True)
        e = jnp.exp(s - m)
        p = e / jnp.sum(e, axis=-1, keepdims=True)
        p_low = p.astype(BF)
        ctx = ein("ihab,ibhd->iahd", p_low, v)
        ctx = ctx.astype(BF).reshape(rows, pair)
        kept.append((q, k, v, p_low, ctx, perm))
        attn = attn + jnp.dot(ctx, wo, preferred_element_type=F32)

    z1 = hidden_in.astype(F32) + attn + out_bias
    hat1, inv1 = norm_parts(z1)
    n1 = hat1 * gain1 + shift1
    n1_low = n1.astype(BF)
    ffn = 0.0
    pres = []
    for _, small, _, wu, wd in slots:
        pre = jnp.dot(n1_low, wu, preferred_element_type=F32) + small[2 * pair: 2 * pair + units]
        cdf = 0.5 * (1.0 + lax.erf(pre * math.sqrt(0.5)))
        act = (pre * cdf).astype(BF)
        slope = cdf + pre * jnp.exp(-0.5 * pre * pre) * (1.0 / math.sqrt(2.0 * math.pi))
        pres.append((act, slope))
        ffn = ffn + jnp.dot(act, wd, preferred_element_type=F32)
    z2 = n1 + ffn + down_bias
    hat2, inv2 = norm_parts(z2)
    out = ((hat2 * gain2 + shift2) * row_valid).astype(BF)
    g_out = cotangent.astype(F32) * row_valid
    d_gain2 = jnp.sum(g_out * hat2, axis=0)
    d_shift2 = jnp.sum(g_out, axis=0)
    g_z2 = norm_back(g_out, hat2, inv2, gain2)
    g_ffn = g_z2.astype(BF)
    d_down_bias = jnp.sum(g_ffn, axis=0, dtype=F32)
    g_n1 = g_z2
    d_ffn = []
    for (_, _, _, wu, wd), (act, slope) in zip(slots, pres):
        d_wd = ein("rf,rd->fd", act, g_ffn)
        g_pre = (ein("rd,fd->rf", g_ffn, wd) * slope).astype(BF)
        d_ub = jnp.sum(g_pre, axis=0, dtype=F32)
        d_wu = ein("rd,rf->df", n1_low, g_pre)
        g_n1 = g_n1 + ein("rf,df->rd", g_pre, wu)
        d_ffn.append((d_wu, d_ub, d_wd))
    d_gain1 = jnp.sum(g_n1 * hat1, axis=0)
    d_shift1 = jnp.sum(g_n1, axis=0)
    g_z1 = norm_back(g_n1, hat1, inv1, gain1)
    g_attn = g_z1.astype(BF)
    d_out_bias = jnp.sum(g_attn, axis=0, dtype=F32)
    x_grad = g_z1
    d_attn = []
    for (wq, _, wo, _, _), (q, k, v, p_low, ctx, perm) in zip(slots, kept):
        d_wo = ein("rc,rd->cd", ctx, g_attn)
        g_ctx = ein("rd,cd->rc", g_attn, wo).astype(BF).reshape(2, half, heads, size)
        dv = flip(ein("ihab,iahd->ibhd", p_low, g_ctx), perm)
        dp = ein("iahd,ibhd->ihab", g_ctx, v)
        p = p_low.astype(F32)
        ds = (p * (dp - jnp.sum(p * dp, axis=-1, keepdims=True))).astype(BF)
        dq = ein("ihab,ibhd->iahd", ds, k) * scaling
        dk = flip(ein("ihab,iahd->ibhd", ds, q) * scaling, perm)
        g_qkv = jnp.stack([dq, dk, dv]).astype(BF).reshape(3, rows, pair)
        sums = jnp.sum(g_qkv, axis=1, dtype=F32)
        d_wq = ein("rd,cre->cde", hidden_in, g_qkv)
        x_grad = x_grad + ein("cre,cde->rd", g_qkv, wq)
        d_attn.append((d_wq, jnp.stack([sums[0], sums[2]]), d_wo))

    common = jnp.stack([d_out_bias, d_gain1, d_shift1, d_down_bias, d_gain2, d_shift2]).astype(BF)

    def flat(i):
        d_wu, d_ub, d_wd = d_ffn[i]
        d_wq, d_b, d_wo = d_attn[i]
        return [d_wu.astype(BF), d_wd.astype(BF), d_wq.astype(BF), d_wo.astype(BF), d_ub.astype(BF), d_b.astype(BF)]

    def plus(a, b):
        return jax.tree.map(lambda u, v: (u.astype(F32) + v.astype(F32)).astype(BF), a, b)

    got = send_bit((flat(1), flat(3), common), 0)
    own, other, common = plus((flat(0), flat(2), common), got)
    own, common = plus((own, common), send_tensor((other, common)))
    parts = own + [common]
    shapes = [a.shape for a in parts]
    line = jnp.concatenate([a.reshape(-1) for a in parts])
    unit = 512 * 8 * 16
    pad = -line.size % unit
    line = jnp.pad(line, (0, pad)).reshape(-1, 512)
    line = total_chips(line)
    mate = send_bit(line, 0)
    both = [line, mate]
    first = jnp.where(core == 0, line, mate).reshape(-1)
    second = jnp.where(core == 0, mate, line).reshape(-1)

    def unpack(v):
        out, at = [], 0
        for s in shapes:
            n = math.prod(s)
            out.append(v[at: at + n].reshape(s).astype(F32))
            at += n
        return out

    a, b = unpack(first), unpack(second)
    d_wu = jnp.concatenate([a[0], b[0]], axis=1)
    d_wd = jnp.concatenate([a[1], b[1]], axis=0)
    d_wq = jnp.concatenate([a[2], b[2]], axis=2)
    d_wo = jnp.concatenate([a[3], b[3]], axis=0)
    d_ub = jnp.concatenate([a[4], b[4]], axis=0)
    d_qvb = jnp.concatenate([a[5], b[5]], axis=1)
    com = a[6]
    return (out, x_grad, d_wq, d_qvb, d_wo, com[0], com[1], com[2], d_wu, d_ub, d_wd, com[3], com[4], com[5])


def solution(mesh):
    whole = P()
    rows = P(("dp", "tensor"), None)
    return jax.shard_map(
        local,
        mesh=mesh,
        in_specs=(rows, P(None, None, "tensor"), P(None, "tensor"), P("tensor", None), whole, whole, whole,
                  P(None, "tensor"), P("tensor"), P("tensor", None), whole, whole, whole, P("dp"), P("tensor"), rows),
        out_specs=(rows, rows, P(None, None, "tensor"), P(None, "tensor"), P("tensor", None), whole, whole, whole,
                   P(None, "tensor"), P("tensor"), P("tensor", None), whole, whole, whole),
        check_vma=False,
    )
```

time: 774 us -> 519 us (0.67)
  waiting for transfers between devices: 391 us -> 103 us
  blocking collectives: 42.8 us -> 0 us
  other arithmetic: 41.4 us -> 72.5 us
  starting transfers between devices: 1.01 us -> 30.4 us
  matrix products: 113 us -> 140 us
  between operations: 14.9 us -> 3.02 us
    reduce_scatter x4 -> x0, waiting for transfers between devices: 175 us -> none  [the longest x1 54.4 us: local(): lax.psum_scatter(jnp.einsum('rf,df->rd', grad_pre, w_up, preferred_elemen...]
    all_gather x4 -> x0, waiting for transfers between devices: 120 us -> none  [the longest x1 33.1 us: local(): grad_ffn_all = lax.all_gather(grad_ffn, 'tensor', axis=0, tiled=True)]
    ppermute x0 -> x37, waiting for transfers between devices: none -> 103 us  [the longest x25 80 us: send_bit(): return jax.tree.map(lambda a: lax.ppermute(a, 'dp', pairs), v)]
    psum x1 -> x0, waiting for transfers between devices: 95.6 us -> none  [batch_total(): summed = lax.psum(flattened, 'dp')]
    another operation x7 -> x36, local copies, waits for them, and re-layouts: 9.83 us -> 55.9 us  [the longest x28 55.1 us: local(): g_qkv = jnp.stack([dq, dk, dv]).astype(BF).reshape(3, rows, pair)]
    psum x1 -> x0, blocking collectives: 42.8 us -> none  [local(): lax.psum((grad_out_bias, grad_gain1, grad_shift1, grad_down_bias, grad_ga...]
    ppermute x0 -> x37, starting transfers between devices: none -> 30.4 us  [the longest x25 17.8 us: send_bit(): return jax.tree.map(lambda a: lax.ppermute(a, 'dp', pairs), v)]
    rev x4 -> x0, local copies, waits for them, and re-layouts: 28.2 us -> none  [swap_halves(): flipped = jnp.flip(blocks, axis=1)]
  transfers between devices with their start and end apart: 9 -> 37, of which waited for: 9 -> 13; matrix products, arithmetic and copies ran while one was open for 5% -> 27% of each run, Pallas kernels for 0% -> 0%
where the time goes in v1:
time: 519 us; the launch traced here: 510 us
  local copies, waits for them, and re-layouts  161 us (31%)
  matrix products  140 us (27%)
  waiting for transfers between devices  103 us (20%)
  other arithmetic  72.5 us (14%)
  starting transfers between devices  30.4 us (6%)
    dot_general x56, matrix products, ein(): return jnp.einsum(spec, a, b, preferred_element_type=F32)  99.8 us
    ppermute x25, waiting for transfers between devices, send_bit(): return jax.tree.map(lambda a: lax.ppermute(a, 'dp', pairs), v)  80 us
    another operation x28, local copies, waits for them, and re-layouts, local(): g_qkv = jnp.stack([dq, dk, dv]).astype(BF).reshape(3, rows, pair)  55.1 us
    unnamed x337, local copies, waits for them, and re-layouts  46.5 us
    ppermute x12, waiting for transfers between devices, send_tensor(): lax.ppermute(a, 'tensor', [(i, (i + 1) % n) for i in range(n)])  22.5 us
    ppermute x25, starting transfers between devices, send_bit(): return jax.tree.map(lambda a: lax.ppermute(a, 'dp', pairs), v)  17.8 us
    reshape x8, local copies, waits for them, and re-layouts, local(): ein('rd,cd->rc', g_attn, wo).astype(BF).reshape(2, half, heads, size)  15.8 us
    sub x4, matrix products, local(): e = jnp.exp(s - m)  14.6 us
  transfers between devices with their start and end apart: 37, of which 13 were waited for; matrix products, arithmetic and copies ran while one was open for 27% of the time, Pallas kernels for 0%

profile of v1, /device:TPU:5, one launch (start us, length us, event | category | flops | bytes accessed | tf_op | source)
XLA Modules:
  0.0 509.5 jit_solution(5276814482374528116)
XLA Ops:
  6.1 2.5 constant_dynamic-slice_fusion.10
  11.8 2.3 copy.242
  20.5 2.2 copy.394
  24.1 2.3 copy.249
  36.4 3.3 fusion.212
  39.8 2.8 divide_convert_fusion.3
  45.1 4.7 fusion.222
  49.9 2.8 divide_convert_fusion.2
  60.7 3.2 fusion.217
  63.9 2.8 divide_convert_fusion.1
  67.8 2.7 fusion.239
  73.4 3.4 fusion.227
  76.8 3.0 divide_convert_fusion
  85.8 2.7 multiply_convert_fusion.4
  88.6 2.2 fusion.240
  90.8 2.7 multiply_convert_fusion.3
  93.5 2.4 multiply_convert_fusion.2
  95.9 2.2 fusion.241
  100.8 2.8 fusion.233
  104.8 2.7 multiply_reduce_fusion
  108.9 3.6 fusion.237
  113.3 2.1 fusion.236
  116.2 3.2 fusion.234
  119.4 3.6 fusion.235
  123.0 2.1 fusion.243
  125.1 3.9 multiply_reduce_fusion.1
  135.6 3.3 convolution_bitcast_fusion.4
  145.0 2.1 convolution_convert_fusion.12
  149.1 2.1 copy.300
  151.2 2.7 fusion.10
  159.6 2.1 convolution_convert_fusion.13
  165.5 3.3 convolution_bitcast_fusion.2
  180.1 2.7 fusion.4
  204.5 2.2 copy.371
  212.1 2.8 fusion.71
  216.2 2.1 select_convert_fusion.3
  238.5 3.0 fusion.69
  244.3 2.0 reshape.412
  246.3 2.1 select_convert_fusion.2
  262.7 3.0 fusion.70
  265.7 3.0 convolution_convert_fusion
  282.4 2.0 reshape.415
  284.4 2.1 select_convert_fusion.1
  290.5 2.4 copy.365
  318.6 2.4 collective-permute-start.11
  322.7 2.1 add_convert_fusion.12
  326.7 3.2 fusion.62
  332.9 2.8 collective-permute-done.18
  337.2 9.9 %collective-permute-done.15 = bf16[512,512]{1,0:T(8,128)(2,1)} collective-permute-done((bf16[512,512]{1,0:T(8,128)(2,1)}, bf16[512,512]{1,0:T(8,128)(2,1)}, u32[]{:S(2)}, u32[]{:S(2)}) %collective-permute-start.15) | collective-permute-done | bytes 524320 | tf_op jit(solution)/shard_map/ppermute | solution.py:19
  349.0 9.3 %collective-permute-done.12 = bf16[512,512]{1,0:T(8,128)(2,1)} collective-permute-done((bf16[512,512]{1,0:T(8,128)(2,1)}, bf16[512,512]{1,0:T(8,128)(2,1)}, u32[]{:S(2)}, u32[]{:S(2)}) %collective-permute-start.12) | collective-permute-done | bytes 524320 | tf_op jit(solution)/shard_map/ppermute | solution.py:19
  367.4 2.7 pad.4
  370.1 3.8 reshape.400
  376.3 18.4 %collective-permute-done.30 = bf16[832,512]{1,0:T(8,128)(2,1)} collective-permute-done((bf16[832,512]{1,0:T(8,128)(2,1)S(1)}, bf16[832,512]{1,0:T(8,128)(2,1)}, u32[]{:S(2)}, u32[]{:S(2)}) %collective-permute-start.30) | collective-permute-done | bytes 852000 | tf_op jit(solution)/shard_map/ppermute | solution.py:25
  398.1 8.7 %collective-permute-done.31 = bf16[416,512]{1,0:T(8,128)(2,1)} collective-permute-done((bf16[416,512]{1,0:T(8,128)(2,1)}, bf16[416,512]{1,0:T(8,128)(2,1)}, u32[]{:S(2)}, u32[]{:S(2)}) %collective-permute-start.31) | collective-permute-done | bytes 426016 | tf_op jit(solution)/shard_map/ppermute | solution.py:25
  410.4 10.0 %collective-permute-done.32 = bf16[208,512]{1,0:T(8,128)(2,1)S(1)} collective-permute-done((bf16[208,512]{1,0:T(8,128)(2,1)S(1)}, bf16[208,512]{1,0:T(8,128)(2,1)S(1)}, u32[]{:S(2)}, u32[]{:S(2)}) %collective-permute-start.32) | collective-permute-done | bytes 213024 | tf_op jit(solution)/shard_map/ppermute | solution.py:25
  421.4 12.4 %collective-permute-done.33 = bf16[208,512]{1,0:T(8,128)(2,1)S(1)} collective-permute-done((bf16[208,512]{1,0:T(8,128)(2,1)S(1)}, bf16[208,512]{1,0:T(8,128)(2,1)S(1)}, u32[]{:S(2)}, u32[]{:S(2)}) %collective-permute-start.33) | collective-permute-done | bytes 213024 | tf_op jit(solution)/shard_map/ppermute | solution.py:25
  434.5 10.4 %collective-permute-done.34 = bf16[416,512]{1,0:T(8,128)(2,1)} collective-permute-done((bf16[416,512]{1,0:T(8,128)(2,1)S(1)}, bf16[416,512]{1,0:T(8,128)(2,1)}, u32[]{:S(2)}, u32[]{:S(2)}) %collective-permute-start.34) | collective-permute-done | bytes 426016 | tf_op jit(solution)/shard_map/ppermute | solution.py:25
  447.1 19.4 %collective-permute-done.35 = bf16[832,512]{1,0:T(8,128)(2,1)} collective-permute-done((bf16[832,512]{1,0:T(8,128)(2,1)}, bf16[832,512]{1,0:T(8,128)(2,1)}, u32[]{:S(2)}, u32[]{:S(2)}) %collective-permute-start.35) | collective-permute-done | bytes 852000 | tf_op jit(solution)/shard_map/ppermute | solution.py:25
  470.2 2.3 collective-permute-start.36
  476.2 2.1 fusion.244
  478.4 2.6 bitcast_add_fusion
  480.9 3.0 copy.320
  485.4 2.3 broadcast_select_fusion.1
  492.8 3.8 slice.269
  (611 shorter events, 256.1 us)
Async XLA Ops:
  0.6 17.1 %copy-start = (bf16[1024,512]{1,0:T(8,128)(2,1)S(1)}, bf16[1024,512]{1,0:T(8,128)(2,1)}, u32[]{:S(2)}) copy-start(bf16[1024,512]{1,0:T(8,128)(2,1)} %param.25) | copy-start | bytes 3145732
  2.9 32.8 %copy-start.117 = (pred[2]{0:T(512)(128)(4,1)}, pred[2]{0:T(512)(128)(4,1)S(1)}, u32[]{:S(2)}) copy-start(pred[2]{0:T(512)(128)(4,1)S(1)} %get-tuple-element.68) | copy-start | bytes 10
  4.1 22.3 %collective-permute-start = (f32[770]{0:T(1024)S(1)}, f32[770]{0:T(1024)S(1)}, u32[]{:S(2)}, u32[]{:S(2)}) collective-permute-start(f32[770]{0:T(1024)S(1)} %pad_maximum_fusion.3), channel_id=1, source_target_pairs={{0,1},{1,0},{2,3},{3,2},{4,5},{5,4},{6,7},{7,6},{8,9},{9,8},{10,11... | collective-permute-start | bytes 9248 | tf_op jit(solution)/shard_map/ppermute | solution.py:19
  6.1 5.6 %copy-start.96 = (bf16[256,512]{1,0:T(8,128)(2,1)S(1)}, bf16[256,512]{1,0:T(8,128)(2,1)}, u32[]{:S(2)}) copy-start(bf16[256,512]{1,0:T(8,128)(2,1)} %param.19) | copy-start | bytes 786436
  10.2 47.8 %collective-permute-start.1 = (bf16[3,512,128]{1,2,0:T(8,128)(2,1)}, bf16[3,512,128]{1,2,0:T(8,128)(2,1)}, u32[]{:S(2)}, u32[]{:S(2)}) collective-permute-start(bf16[3,512,128]{1,2,0:T(8,128)(2,1)} %bitcast.1), channel_id=1, source_target_pairs={{0,1},{1,0},{2,3},{3,2},{4,5},{5,4},{6,7},{7,6},{8,9},{9,8},{10,11... | collective-permute-start | bytes 1179656 | tf_op jit(solution)/shard_map/ppermute | solution.py:19
  11.7 46.0 %collective-permute-start.2 = (bf16[128,512]{1,0:T(8,128)(2,1)S(1)}, bf16[128,512]{1,0:T(8,128)(2,1)}, u32[]{:S(2)}, u32[]{:S(2)}) collective-permute-start(bf16[128,512]{1,0:T(8,128)(2,1)S(1)} %dynamic-slice_bitcast_fusion.1), channel_id=1, source_target_pairs={{0,1},{1,0},{2,3},{3,2},{4,5},{5,4},{6,7},{7,6},{8,9},{9,8},{10,11... | collective-permute-start | bytes 393224 | tf_op jit(solution)/shard_map/ppermute | solution.py:19
  14.1 8.6 %copy-start.10 = (bf16[1024,512]{1,0:T(8,128)(2,1)S(1)}, bf16[1024,512]{1,0:T(8,128)(2,1)}, u32[]{:S(2)}) copy-start(bf16[1024,512]{1,0:T(8,128)(2,1)} %param.16) | copy-start | bytes 3145732
  15.3 8.8 %copy-start.31 = (bf16[512,1,512]{0,2,1:T(8,128)(2,1)}, bf16[512,1,512]{0,2,1:T(8,128)(2,1)S(1)}, u32[]{:S(2)}) copy-start(bf16[512,1,512]{0,2,1:T(8,128)(2,1)S(1)} %constant_dynamic-slice_fusion.7) | copy-start | bytes 1572868
  16.3 54.2 %collective-permute-start.6 = (bf16[512,512]{1,0:T(8,128)(2,1)}, bf16[512,512]{1,0:T(8,128)(2,1)}, u32[]{:S(2)}, u32[]{:S(2)}) collective-permute-start(bf16[512,512]{1,0:T(8,128)(2,1)} %bitcast.32), channel_id=1, source_target_pairs={{0,1},{1,0},{2,3},{3,2},{4,5},{5,4},{6,7},{7,6},{8,9},{9,8},{10,11... | collective-permute-start | bytes 1572872 | tf_op jit(solution)/shard_map/ppermute | solution.py:19
  18.6 52.3 %collective-permute-start.7 = (bf16[512,512]{1,0:T(8,128)(2,1)}, bf16[512,512]{1,0:T(8,128)(2,1)}, u32[]{:S(2)}, u32[]{:S(2)}) collective-permute-start(bf16[512,512]{1,0:T(8,128)(2,1)} %dynamic-slice_bitcast_fusion), channel_id=1, source_target_pairs={{0,1},{1,0},{2,3},{3,2},{4,5},{5,4},{6,7},{7,6},{8,9},{9,8},{10,11... | collective-permute-start | bytes 1572872 | tf_op jit(solution)/shard_map/ppermute | solution.py:19
  20.5 15.2 %copy-start.126 = (pred[2]{0:T(512)(128)(4,1)}, pred[2]{0:T(512)(128)(4,1)S(1)}, u32[]{:S(2)}) copy-start(pred[2]{0:T(512)(128)(4,1)S(1)} %compare_bitcast_fusion) | copy-start | bytes 10
  22.7 7.0 %copy-start.61 = (bf16[3,512,1,128]{1,3,0,2:T(8,128)(2,1)}, bf16[3,512,1,128]{1,3,0,2:T(8,128)(2,1)S(1)}, u32[]{:S(2)}) copy-start(bf16[3,512,1,128]{1,3,0,2:T(8,128)(2,1)S(1)} %copy.394) | copy-start | bytes 1179652
  26.4 2.6 collective-permute-start.3
  28.2 32.2 %copy-start.124 = (pred[2]{0:T(512)(128)(4,1)}, pred[2]{0:T(512)(128)(4,1)S(1)}, u32[]{:S(2)}) copy-start(pred[2]{0:T(512)(128)(4,1)S(1)} %slice_compare_fusion.1) | copy-start | bytes 10
  29.0 6.6 %copy-start.141 = (f32[770]{0:T(1024)}, f32[770]{0:T(1024)S(1)}, u32[]{:S(2)}) copy-start(f32[770]{0:T(1024)S(1)} %collective-permute-done.3) | copy-start | bytes 9244
  35.7 6.9 %copy-start.50 = (bf16[2,512,2,64]{1,3,2,0:T(8,128)(2,1)}, bf16[2,512,2,64]{1,3,2,0:T(8,128)(2,1)S(1)}, u32[]{:S(2)}) copy-start(bf16[2,512,2,64]{1,3,2,0:T(8,128)(2,1)S(1)} %get-tuple-element.134) | copy-start | bytes 786436
  44.0 9.2 %copy-start.40 = (bf16[16,8,2,512]{3,1,2,0:T(8,128)(2,1)}, bf16[16,8,2,512]{3,1,2,0:T(8,128)(2,1)S(1)}, u32[]{:S(2)}) copy-start(bf16[16,8,2,512]{3,1,2,0:T(8,128)(2,1)S(1)} %copy.395) | copy-start | bytes 786436
  57.7 22.9 %collective-permute-start.5 = (bf16[128,512]{1,0:T(8,128)(2,1)}, bf16[128,512]{1,0:T(8,128)(2,1)}, u32[]{:S(2)}, u32[]{:S(2)}) collective-permute-start(bf16[128,512]{1,0:T(8,128)(2,1)} %collective-permute-done.2), channel_id=1, source_target_pairs={{0,2},{2,0},{4,6},{6,4},{8,10},{10,8},{12,14},{14,12},{16,18},{18,... | collective-permute-start | bytes 393224 | tf_op jit(solution)/shard_map/ppermute | solution.py:25
  60.7 6.3 %copy-start.53 = (bf16[2,512,2,64]{1,3,2,0:T(8,128)(2,1)}, bf16[2,512,2,64]{1,3,2,0:T(8,128)(2,1)S(1)}, u32[]{:S(2)}) copy-start(bf16[2,512,2,64]{1,3,2,0:T(8,128)(2,1)S(1)} %get-tuple-element.136) | copy-start | bytes 786436
  66.7 4.3 collective-permute-start.4
  70.5 28.4 %collective-permute-start.8 = (bf16[512,512]{1,0:T(8,128)(2,1)}, bf16[512,512]{1,0:T(8,128)(2,1)}, u32[]{:S(2)}, u32[]{:S(2)}) collective-permute-start(bf16[512,512]{1,0:T(8,128)(2,1)} %collective-permute-done.6), channel_id=1, source_target_pairs={{0,2},{2,0},{4,6},{6,4},{8,10},{10,8},{12,14},{14,12},{16,18},{18,... | collective-permute-start | bytes 1572872 | tf_op jit(solution)/shard_map/ppermute | solution.py:25
  70.8 29.9 %collective-permute-start.9 = (bf16[512,512]{1,0:T(8,128)(2,1)}, bf16[512,512]{1,0:T(8,128)(2,1)}, u32[]{:S(2)}, u32[]{:S(2)}) collective-permute-start(bf16[512,512]{1,0:T(8,128)(2,1)} %collective-permute-done.7), channel_id=1, source_target_pairs={{0,2},{2,0},{4,6},{6,4},{8,10},{10,8},{12,14},{14,12},{16,18},{18,... | collective-permute-start | bytes 1572872 | tf_op jit(solution)/shard_map/ppermute | solution.py:25
  85.8 13.1 %copy-start.33 = (bf16[1024,512]{0,1:T(8,128)(2,1)}, bf16[1024,512]{0,1:T(8,128)(2,1)S(1)}, u32[]{:S(2)}) copy-start(bf16[1024,512]{0,1:T(8,128)(2,1)S(1)} %fusion.55) | copy-start | bytes 3145732
  100.8 15.4 %copy-start.26 = (f32[1024,512]{1,0:T(8,128)}, f32[1024,512]{1,0:T(8,128)S(1)}, u32[]{:S(2)}) copy-start(f32[1024,512]{1,0:T(8,128)S(1)} %fusion.242) | copy-start | bytes 6291460
  108.9 10.4 %copy-start.64 = (bf16[1024,512]{0,1:T(8,128)(2,1)}, bf16[1024,512]{0,1:T(8,128)(2,1)S(1)}, u32[]{:S(2)}) copy-start(bf16[1024,512]{0,1:T(8,128)(2,1)S(1)} %get-tuple-element.65) | copy-start | bytes 3145732
  119.4 5.7 %copy-start.72 = (bf16[1024,512]{1,0:T(8,128)(2,1)}, bf16[1024,512]{1,0:T(8,128)(2,1)S(1)}, u32[]{:S(2)}) copy-start(bf16[1024,512]{1,0:T(8,128)(2,1)S(1)} %get-tuple-element.165) | copy-start | bytes 3145732
  123.0 6.1 %copy-start.66 = (bf16[1024,512]{1,0:T(8,128)(2,1)}, bf16[1024,512]{1,0:T(8,128)(2,1)S(1)}, u32[]{:S(2)}) copy-start(bf16[1024,512]{1,0:T(8,128)(2,1)S(1)} %get-tuple-element.167) | copy-start | bytes 3145732
  208.7 7.5 %copy-start.118 = (pred[2]{0:T(512)(128)(4,1)S(1)}, pred[2]{0:T(512)(128)(4,1)}, u32[]{:S(2)}) copy-start(pred[2]{0:T(512)(128)(4,1)} %copy-done.117) | copy-start | bytes 10
  235.5 6.0 %copy-start.128 = (pred[2]{0:T(512)(128)(4,1)S(1)}, pred[2]{0:T(512)(128)(4,1)}, u32[]{:S(2)}) copy-start(pred[2]{0:T(512)(128)(4,1)} %copy-done.126) | copy-start | bytes 10
  258.0 7.7 %copy-start.121 = (f32[512]{0:T(512)S(1)}, f32[512]{0:T(512)}, u32[]{:S(2)}) copy-start(f32[512]{0:T(512)} %slice.256) | copy-start | bytes 6148
  277.5 33.4 %collective-permute-start.28 = (bf16[6,512]{1,0:T(8,128)(2,1)}, bf16[6,512]{1,0:T(8,128)(2,1)}, u32[]{:S(2)}, u32[]{:S(2)}) collective-permute-start(bf16[6,512]{1,0:T(8,128)(2,1)} %stack.134), channel_id=1, source_target_pairs={{0,2},{2,0},{4,6},{6,4},{8,10},{10,8},{12,14},{14,12},{16,18},{18,... | collective-permute-start | bytes 18440 | tf_op jit(solution)/shard_map/ppermute | solution.py:25
  277.9 26.3 %collective-permute-start.25 = (bf16[2,128]{1,0:T(2,128)(2,1)S(1)}, bf16[2,128]{1,0:T(2,128)(2,1)}, u32[]{:S(2)}, u32[]{:S(2)}) collective-permute-start(bf16[2,128]{1,0:T(2,128)(2,1)S(1)} %pad_maximum_fusion.8), channel_id=1, source_target_pairs={{0,2},{2,0},{4,6},{6,4},{8,10},{10,8},{12,14},{14,12},{16,18},{18,... | collective-permute-start | bytes 1544 | tf_op jit(solution)/shard_map/ppermute | solution.py:25
  278.1 23.7 %collective-permute-start.26 = (bf16[2,128]{1,0:T(2,128)(2,1)S(1)}, bf16[2,128]{1,0:T(2,128)(2,1)S(1)}, u32[]{:S(2)}, u32[]{:S(2)}) collective-permute-start(bf16[2,128]{1,0:T(2,128)(2,1)S(1)} %pad_maximum_fusion.9), channel_id=1, source_target_pairs={{0,2},{2,0},{4,6},{6,4},{8,10},{10,8},{12,14},{14,12},{16,18},{18,... | collective-permute-start | bytes 1544 | tf_op jit(solution)/shard_map/ppermute | solution.py:25
  290.5 10.7 %copy-start.152 = (bf16[512]{0:T(512)(128)(2,1)S(1)}, bf16[512]{0:T(512)(128)(2,1)}, u32[]{:S(2)}) copy-start(bf16[512]{0:T(512)(128)(2,1)} %get-tuple-element.164) | copy-start | bytes 3076
  290.5 13.6 %copy-start.151 = (bf16[512]{0:T(512)(128)(2,1)S(1)}, bf16[512]{0:T(512)(128)(2,1)}, u32[]{:S(2)}) copy-start(bf16[512]{0:T(512)(128)(2,1)} %get-tuple-element.166) | copy-start | bytes 3076
  301.2 1.2 collective-permute-start.23
  301.4 6.2 %collective-permute-start.22 = (bf16[512]{0:T(512)(128)(2,1)}, bf16[512]{0:T(512)(128)(2,1)S(1)}, u32[]{:S(2)}, u32[]{:S(2)}) collective-permute-start(bf16[512]{0:T(512)(128)(2,1)} %get-tuple-element.168), channel_id=1, source_target_pairs={{0,2},{2,0},{4,6},{6,4},{8,10},{10,8},{12,14},{14,12},{16,18},{18,... | collective-permute-start | bytes 3080 | tf_op jit(solution)/shard_map/ppermute | solution.py:25
  301.8 9.9 %collective-permute-start.20 = (bf16[128,512]{1,0:T(8,128)(2,1)}, bf16[128,512]{1,0:T(8,128)(2,1)S(1)}, u32[]{:S(2)}, u32[]{:S(2)}) collective-permute-start(bf16[128,512]{1,0:T(8,128)(2,1)} %convolution_convert_fusion.20), channel_id=1, source_target_pairs={{0,2},{2,0},{4,6},{6,4},{8,10},{10,8},{12,14},{14,12},{16,18},{18,... | collective-permute-start | bytes 393224 | tf_op jit(solution)/shard_map/ppermute | solution.py:25
  302.4 2.7 collective-permute-start.27
  304.1 12.4 %collective-permute-start.19 = (bf16[128,512]{1,0:T(8,128)(2,1)}, bf16[128,512]{1,0:T(8,128)(2,1)S(1)}, u32[]{:S(2)}, u32[]{:S(2)}) collective-permute-start(bf16[128,512]{1,0:T(8,128)(2,1)} %convolution_convert_fusion.22), channel_id=1, source_target_pairs={{0,2},{2,0},{4,6},{6,4},{8,10},{10,8},{12,14},{14,12},{16,18},{18,... | collective-permute-start | bytes 393224 | tf_op jit(solution)/shard_map/ppermute | solution.py:25
  305.1 4.2 collective-permute-start.24
  307.6 15.1 %collective-permute-start.17 = (bf16[3,512,128]{1,2,0:T(8,128)(2,1)}, bf16[3,512,128]{1,2,0:T(8,128)(2,1)}, u32[]{:S(2)}, u32[]{:S(2)}) collective-permute-start(bf16[3,512,128]{1,2,0:T(8,128)(2,1)} %fusion.71), channel_id=1, source_target_pairs={{0,2},{2,0},{4,6},{6,4},{8,10},{10,8},{12,14},{14,12},{16,18},{18,... | collective-permute-start | bytes 1179656 | tf_op jit(solution)/shard_map/ppermute | solution.py:25
  309.2 22.4 %collective-permute-start.16 = (bf16[3,512,128]{1,2,0:T(8,128)(2,1)}, bf16[3,512,128]{1,2,0:T(8,128)(2,1)}, u32[]{:S(2)}, u32[]{:S(2)}) collective-permute-start(bf16[3,512,128]{1,2,0:T(8,128)(2,1)} %fusion.70), channel_id=1, source_target_pairs={{0,2},{2,0},{4,6},{6,4},{8,10},{10,8},{12,14},{14,12},{16,18},{18,... | collective-permute-start | bytes 1179656 | tf_op jit(solution)/shard_map/ppermute | solution.py:25
  310.9 14.0 %collective-permute-start.14 = (bf16[512,512]{1,0:T(8,128)(2,1)}, bf16[512,512]{1,0:T(8,128)(2,1)}, u32[]{:S(2)}, u32[]{:S(2)}) collective-permute-start(bf16[512,512]{1,0:T(8,128)(2,1)} %convolution_convert_fusion), channel_id=1, source_target_pairs={{0,2},{2,0},{4,6},{6,4},{8,10},{10,8},{12,14},{14,12},{16,18},{18,... | collective-permute-start | bytes 1572872 | tf_op jit(solution)/shard_map/ppermute | solution.py:25
  311.7 2.9 collective-permute-start.29
  314.6 4.0 collective-permute-start.21
  316.5 20.6 %collective-permute-start.13 = (bf16[512,512]{1,0:T(8,128)(2,1)}, bf16[512,512]{1,0:T(8,128)(2,1)}, u32[]{:S(2)}, u32[]{:S(2)}) collective-permute-start(bf16[512,512]{1,0:T(8,128)(2,1)} %convolution_convert_fusion.2), channel_id=1, source_target_pairs={{0,2},{2,0},{4,6},{6,4},{8,10},{10,8},{12,14},{14,12},{16,18},{18,... | collective-permute-start | bytes 1572872 | tf_op jit(solution)/shard_map/ppermute | solution.py:25
  318.6 11.3 %collective-permute-start.11 = (bf16[512,512]{1,0:T(8,128)(2,1)}, bf16[512,512]{1,0:T(8,128)(2,1)S(1)}, u32[]{:S(2)}, u32[]{:S(2)}) collective-permute-start(bf16[512,512]{1,0:T(8,128)(2,1)} %convolution_convert_fusion.4), channel_id=1, source_target_pairs={{0,2},{2,0},{4,6},{6,4},{8,10},{10,8},{12,14},{14,12},{16,18},{18,... | collective-permute-start | bytes 1572872 | tf_op jit(solution)/shard_map/ppermute | solution.py:25
  322.7 26.3 %collective-permute-start.10 = (bf16[512,512]{1,0:T(8,128)(2,1)}, bf16[512,512]{1,0:T(8,128)(2,1)}, u32[]{:S(2)}, u32[]{:S(2)}) collective-permute-start(bf16[512,512]{1,0:T(8,128)(2,1)} %convolution_convert_fusion.6), channel_id=1, source_target_pairs={{0,2},{2,0},{4,6},{6,4},{8,10},{10,8},{12,14},{14,12},{16,18},{18,... | collective-permute-start | bytes 1572872 | tf_op jit(solution)/shard_map/ppermute | solution.py:25
  324.9 5.2 %copy-start.35 = (bf16[1024,512]{0,1:T(8,128)(2,1)S(1)}, bf16[1024,512]{0,1:T(8,128)(2,1)}, u32[]{:S(2)}) copy-start(bf16[1024,512]{0,1:T(8,128)(2,1)} %copy-done.33) | copy-start | bytes 3145732
  324.9 5.2 %copy-start.67 = (bf16[1024,512]{1,0:T(8,128)(2,1)S(1)}, bf16[1024,512]{1,0:T(8,128)(2,1)}, u32[]{:S(2)}) copy-start(bf16[1024,512]{1,0:T(8,128)(2,1)} %copy-done.66) | copy-start | bytes 3145732
  324.9 10.8 %collective-permute-start.18 = (bf16[3,512,128]{1,2,0:T(8,128)(2,1)S(1)}, bf16[3,512,128]{1,2,0:T(8,128)(2,1)S(1)}, u32[]{:S(2)}, u32[]{:S(2)}) collective-permute-start(bf16[3,512,128]{1,2,0:T(8,128)(2,1)S(1)} %add_convert_fusion.12), channel_id=1, source_target_pairs={{0,1},{1,0},{2,3},{3,2},{4,5},{5,4},{6,7},{7,6},{8,9},{9,8},{10,11... | collective-permute-start | bytes 1179656 | tf_op jit(solution)/shard_map/ppermute | solution.py:19
  329.9 5.8 %copy-start.39 = (f32[3,512,128]{1,2,0:T(8,128)S(1)}, f32[3,512,128]{1,2,0:T(8,128)}, u32[]{:S(2)}) copy-start(f32[3,512,128]{1,2,0:T(8,128)} %fusion.69) | copy-start | bytes 2359300
  329.9 17.1 %collective-permute-start.15 = (bf16[512,512]{1,0:T(8,128)(2,1)}, bf16[512,512]{1,0:T(8,128)(2,1)}, u32[]{:S(2)}, u32[]{:S(2)}) collective-permute-start(bf16[512,512]{1,0:T(8,128)(2,1)} %fusion.62), channel_id=1, source_target_pairs={{0,1},{1,0},{2,3},{3,2},{4,5},{5,4},{6,7},{7,6},{8,9},{9,8},{10,11... | collective-permute-start | bytes 1572872 | tf_op jit(solution)/shard_map/ppermute | solution.py:19
  331.6 26.7 %collective-permute-start.12 = (bf16[512,512]{1,0:T(8,128)(2,1)}, bf16[512,512]{1,0:T(8,128)(2,1)}, u32[]{:S(2)}, u32[]{:S(2)}) collective-permute-start(bf16[512,512]{1,0:T(8,128)(2,1)} %add_convert_fusion.8), channel_id=1, source_target_pairs={{0,1},{1,0},{2,3},{3,2},{4,5},{5,4},{6,7},{7,6},{8,9},{9,8},{10,11... | collective-permute-start | bytes 1572872 | tf_op jit(solution)/shard_map/ppermute | solution.py:19
  337.1 21.2 %copy-start.75 = (f32[512,512]{1,0:T(8,128)S(1)}, f32[512,512]{1,0:T(8,128)}, u32[]{:S(2)}) copy-start(f32[512,512]{1,0:T(8,128)} %fusion.65) | copy-start | bytes 3145732
  360.0 6.0 %copy-start.115 = (bf16[3072]{0:T(1024)(128)(2,1)S(1)}, bf16[3072]{0:T(1024)(128)(2,1)}, u32[]{:S(2)}) copy-start(bf16[3072]{0:T(1024)(128)(2,1)} %reshape.399) | copy-start | bytes 18436
  375.1 19.6 %collective-permute-start.30 = (bf16[832,512]{1,0:T(8,128)(2,1)S(1)}, bf16[832,512]{1,0:T(8,128)(2,1)}, u32[]{:S(2)}, u32[]{:S(2)}) collective-permute-start(bf16[832,512]{1,0:T(8,128)(2,1)S(1)} %constant_dynamic-slice_fusion.5), channel_id=1, source_target_pairs={{0,4},{2,6},{4,0},{6,2},{8,12},{10,14},{12,8},{14,10},{16,20},{18,... | collective-permute-start | bytes 2555912 | tf_op jit(solution)/shard_map/ppermute | solution.py:25
  397.1 9.7 %collective-permute-start.31 = (bf16[416,512]{1,0:T(8,128)(2,1)}, bf16[416,512]{1,0:T(8,128)(2,1)}, u32[]{:S(2)}, u32[]{:S(2)}) collective-permute-start(bf16[416,512]{1,0:T(8,128)(2,1)} %constant_dynamic-slice_fusion.4), channel_id=1, source_target_pairs={{0,8},{2,10},{4,12},{6,14},{8,0},{10,2},{12,4},{14,6},{16,24},{18,... | collective-permute-start | bytes 1277960 | tf_op jit(solution)/shard_map/ppermute | solution.py:25
  408.7 11.7 %collective-permute-start.32 = (bf16[208,512]{1,0:T(8,128)(2,1)S(1)}, bf16[208,512]{1,0:T(8,128)(2,1)S(1)}, u32[]{:S(2)}, u32[]{:S(2)}) collective-permute-start(bf16[208,512]{1,0:T(8,128)(2,1)S(1)} %constant_dynamic-slice_fusion.3), channel_id=1, source_target_pairs={{0,16},{2,18},{4,20},{6,22},{8,24},{10,26},{12,28},{14,30},{16,0},... | collective-permute-start | bytes 638984 | tf_op jit(solution)/shard_map/ppermute | solution.py:25
  421.3 12.4 %collective-permute-start.33 = (bf16[208,512]{1,0:T(8,128)(2,1)S(1)}, bf16[208,512]{1,0:T(8,128)(2,1)S(1)}, u32[]{:S(2)}, u32[]{:S(2)}) collective-permute-start(bf16[208,512]{1,0:T(8,128)(2,1)S(1)} %add_convert_fusion.14), channel_id=1, source_target_pairs={{0,16},{2,18},{4,20},{6,22},{8,24},{10,26},{12,28},{14,30},{16,0},... | collective-permute-start | bytes 638984 | tf_op jit(solution)/shard_map/ppermute | solution.py:25
  433.9 11.1 %collective-permute-start.34 = (bf16[416,512]{1,0:T(8,128)(2,1)S(1)}, bf16[416,512]{1,0:T(8,128)(2,1)}, u32[]{:S(2)}, u32[]{:S(2)}) collective-permute-start(bf16[416,512]{1,0:T(8,128)(2,1)S(1)} %pad_maximum_fusion.2), channel_id=1, source_target_pairs={{0,8},{2,10},{4,12},{6,14},{8,0},{10,2},{12,4},{14,6},{16,24},{18,... | collective-permute-start | bytes 1277960 | tf_op jit(solution)/shard_map/ppermute | solution.py:25
  447.1 19.4 %collective-permute-start.35 = (bf16[832,512]{1,0:T(8,128)(2,1)}, bf16[832,512]{1,0:T(8,128)(2,1)}, u32[]{:S(2)}, u32[]{:S(2)}) collective-permute-start(bf16[832,512]{1,0:T(8,128)(2,1)} %pad_maximum_fusion.1), channel_id=1, source_target_pairs={{0,4},{2,6},{4,0},{6,2},{8,12},{10,14},{12,8},{14,10},{16,20},{18,... | collective-permute-start | bytes 2555912 | tf_op jit(solution)/shard_map/ppermute | solution.py:25
  470.2 15.1 %collective-permute-start.36 = (bf16[1664,512]{1,0:T(8,128)(2,1)}, bf16[1664,512]{1,0:T(8,128)(2,1)}, u32[]{:S(2)}, u32[]{:S(2)}) collective-permute-start(bf16[1664,512]{1,0:T(8,128)(2,1)} %pad_maximum_fusion), channel_id=1, source_target_pairs={{0,2},{2,0},{4,6},{6,4},{8,10},{10,8},{12,14},{14,12},{16,18},{18,... | collective-permute-start | bytes 5111816 | tf_op jit(solution)/shard_map/ppermute | solution.py:25
  (127 other events, 311.9 us)

commit v2 on v1

v2 whole, which is shorter than its diff:
```python
import math
from functools import partial
import jax
import jax.numpy as jnp
from jax import lax
from jax.experimental import pallas as pl
from jax.experimental.pallas import tpu as pltpu
from jax.sharding import PartitionSpec as P

EPSILON = 1e-05
BF = jnp.bfloat16
F32 = jnp.float32
VMEM_BYTES = 56 * 1024 * 1024


def dot(a, b, ca, cb):
    return lax.dot_general(a, b, (((ca,), (cb,)), ((), ())), preferred_element_type=F32)


def forward_kernel(scalars, x_ref, w_ref, bias_ref, qkv_ref, e_ref, inv_ref, ctx_ref):
    width, rows = qkv_ref.shape[1:]
    half = rows // 2
    heads = e_ref.shape[1]
    size = width // heads
    i = pl.program_id(0)

    @pl.when(i == 0)
    def _():
        for c in range(3):
            part = dot(w_ref[c], x_ref[...], 0, 1)
            if c != 1:
                part = part + bias_ref[c // 2]
            qkv_ref[c] = part.astype(BF)

    length = scalars[1]
    mine = pl.ds(pl.multiple_of(i * half, half), half)
    factor = math.log2(math.e) / math.sqrt(size)
    for h in range(heads):
        lanes = slice(h * size, (h + 1) * size)
        j = i ^ scalars[2 + h]
        theirs = pl.ds(pl.multiple_of(j * half, half), half)
        s = dot(qkv_ref[1, lanes, theirs], qkv_ref[0, lanes, mine], 0, 0)
        key = lax.broadcasted_iota(jnp.int32, (half, 1), 0) + j * half
        s = jnp.where(key < length, s, -1e30)
        top = jnp.max(s, axis=0, keepdims=True)
        e = jnp.exp2((s - top) * factor)
        inv = 1.0 / jnp.sum(e, axis=0, keepdims=True)
        low = e.astype(BF)
        e_ref[0, h] = low
        inv_ref[0, h] = inv
        ctx = dot(qkv_ref[2, lanes, theirs], low, 1, 0) * inv
        ctx_ref[lanes, mine] = ctx.astype(BF)


def attend_forward(x, w, bias, scalars):
    rows, width = x.shape
    heads = scalars.shape[0] - 2
    pair = bias.shape[1]
    half = rows // 2
    once = lambda *shape: pl.BlockSpec(shape, lambda i, s: (0,) * len(shape))
    return pl.pallas_call(
        forward_kernel,
        out_shape=(
            jax.ShapeDtypeStruct((3, pair, rows), BF),
            jax.ShapeDtypeStruct((2, heads, half, half), BF),
            jax.ShapeDtypeStruct((2, heads, 1, half), F32),
            jax.ShapeDtypeStruct((pair, rows), BF),
        ),
        grid_spec=pltpu.PrefetchScalarGridSpec(
            num_scalar_prefetch=1,
            grid=(2,),
            in_specs=[
                once(rows, width),
                pl.BlockSpec((3, width, pair), lambda i, s: (0, 0, s[0])),
                once(2, pair, 1),
            ],
            out_specs=(
                once(3, pair, rows),
                pl.BlockSpec((1, heads, half, half), lambda i, s: (i, 0, 0, 0)),
                pl.BlockSpec((1, heads, 1, half), lambda i, s: (i, 0, 0, 0)),
                once(pair, rows),
            ),
        ),
        compiler_params=pltpu.CompilerParams(vmem_limit_bytes=VMEM_BYTES),
        cost_estimate=pl.CostEstimate(flops=2_000_000_000, bytes_accessed=5_000_000, transcendentals=1_000_000),
        name="attend_forward",
    )(scalars, x, w, bias)


def backward_kernel(scalars, x_ref, wo_ref, qkv_ref, e_ref, inv_ref, ctx_ref, ga_ref,
                    g_ref, dw_ref, sums_ref, gc_ref):
    width, rows = gc_ref.shape
    half = rows // 2
    heads = e_ref.shape[1]
    size = width // heads
    i = pl.program_id(0)

    @pl.when(i == 0)
    def _():
        gc_ref[...] = dot(wo_ref[...], ga_ref[...], 1, 1).astype(BF)
        dw_ref[3 * width:] = dot(ctx_ref[...], ga_ref[...], 1, 0).astype(BF)

    mine = pl.ds(pl.multiple_of(i * half, half), half)
    scaling = 1.0 / math.sqrt(size)
    for h in range(heads):
        lanes = slice(h * size, (h + 1) * size)
        j = i ^ scalars[2 + h]
        theirs = pl.ds(pl.multiple_of(j * half, half), half)
        g = gc_ref[lanes, mine].astype(F32) * inv_ref[0, h]
        inner = jnp.sum(g * ctx_ref[lanes, mine].astype(F32), axis=0, keepdims=True)
        g = g.astype(BF)
        e = e_ref[0, h]
        dp = dot(qkv_ref[2, lanes, theirs], g, 0, 0)
        ds = (e.astype(F32) * (dp - inner)).astype(BF)
        g_ref[2, lanes, theirs] = dot(g, e, 1, 1).astype(BF)
        g_ref[1, lanes, theirs] = (dot(qkv_ref[0, lanes, mine], ds, 1, 1) * scaling).astype(BF)
        g_ref[0, lanes, mine] = (dot(qkv_ref[1, lanes, theirs], ds, 1, 0) * scaling).astype(BF)

    @pl.when(i == 1)
    def _():
        for c in range(3):
            dw_ref[c * width: (c + 1) * width] = dot(g_ref[c], x_ref[...], 1, 0).astype(BF)
            if c != 1:
                sums_ref[c // 2] = jnp.sum(g_ref[c].astype(F32), axis=1, keepdims=True)


def attend_backward(x, wo, qkv, e, inv, ctx, g_attn, scalars):
    rows, width = x.shape
    heads = e.shape[1]
    pair = ctx.shape[0]
    half = rows // 2
    once = lambda *shape: pl.BlockSpec(shape, lambda i, s: (0,) * len(shape))
    return pl.pallas_call(
        backward_kernel,
        out_shape=(
            jax.ShapeDtypeStruct((3, pair, rows), BF),
            jax.ShapeDtypeStruct((4 * pair, width), BF),
            jax.ShapeDtypeStruct((2, pair, 1), F32),
        ),
        grid_spec=pltpu.PrefetchScalarGridSpec(
            num_scalar_prefetch=1,
            grid=(2,),
            in_specs=[
                once(rows, width),
                pl.BlockSpec((pair, width), lambda i, s: (s[0], 0)),
                once(3, pair, rows),
                pl.BlockSpec((1, heads, half, half), lambda i, s: (i, 0, 0, 0)),
                pl.BlockSpec((1, heads, 1, half), lambda i, s: (i, 0, 0, 0)),
                once(pair, rows),
                once(rows, width),
            ],
            out_specs=(once(3, pair, rows), once(4 * pair, width), once(2, pair, 1)),
            scratch_shapes=[pltpu.VMEM((pair, rows), BF)],
        ),
        compiler_params=pltpu.CompilerParams(vmem_limit_bytes=VMEM_BYTES),
        cost_estimate=pl.CostEstimate(flops=4_000_000_000, bytes_accessed=6_000_000, transcendentals=0),
        name="attend_backward",
    )(scalars, x, wo, qkv, e, inv, ctx, g_attn)


def normed(v):
    centre = v - jnp.mean(v, axis=-1, keepdims=True)
    inv = lax.rsqrt(jnp.mean(centre * centre, axis=-1, keepdims=True) + EPSILON)
    return centre * inv, inv


def norm_back(g, hat, inv, gain):
    g = g * gain
    return (g - jnp.mean(g, axis=-1, keepdims=True) - hat * jnp.mean(g * hat, axis=-1, keepdims=True)) * inv


def gelu_parts(v):
    t = 1.0 / (1.0 + (0.3275911 * math.sqrt(0.5)) * jnp.abs(v))
    bell = jnp.exp2(v * v * (-0.5 * math.log2(math.e)))
    poly = ((((0.5 * 1.061405429 * t - 0.5 * 1.453152027) * t + 0.5 * 1.421413741) * t
             - 0.5 * 0.284496736) * t + 0.5 * 0.254829592) * t
    tail = poly * bell
    cdf = jnp.where(v < 0, tail, 1.0 - tail)
    return v * cdf, cdf + v * bell * (1.0 / math.sqrt(2.0 * math.pi))


def dense_kernel(scalars, x_ref, cot_ref, c0, c1, c2, c3, vec_ref, wo_own, wu_own, wd_own, ub_own, ub_m, ub_p,
                 pack_m, pack_p, out_ref, gz_ref, ga_ref, gm_ref, gp_ref, dub_ref, common_ref,
                 wo_all, n1_all, gf_all, act_all, gp_all, tile):
    rows, width = x_ref.shape
    pair = c0.shape[0]
    units = ub_m.shape[1]
    core, length = scalars[0], scalars[1]

    def at(i, n):
        return pl.ds(pl.multiple_of((core ^ i) * n, n), n)

    wo_all[0:pair] = wo_own[at(0, pair)]
    wo_all[pair: 2 * pair] = wo_own[at(1, pair)]
    wo_all[2 * pair: 3 * pair] = pack_m[2 * units:]
    wo_all[3 * pair:] = pack_p[2 * units:]
    ups = [wu_own.at[:, at(0, units)], wu_own.at[:, at(1, units)], pack_m.at[:units], pack_p.at[:units]]
    downs = [wd_own.at[at(0, units)], wd_own.at[at(1, units)], pack_m.at[units: 2 * units], pack_p.at[units: 2 * units]]
    biases = [ub_own.at[:, at(0, units)], ub_own.at[:, at(1, units)], ub_m, ub_p]
    out_bias, gain1, shift1, down_bias, gain2, shift2 = (vec_ref[k: k + 1] for k in range(6))
    dub_ref[...] = jnp.zeros_like(dub_ref)
    common_ref[...] = jnp.zeros_like(common_ref)

    @pl.loop(0, rows // tile)
    def _(r):
        here = pl.ds(pl.multiple_of(r * tile, tile), tile)
        ctx = jnp.concatenate([c[:, here] for c in (c0, c1, c2, c3)], axis=0)
        z1 = x_ref[here].astype(F32) + dot(ctx, wo_all[...], 0, 0) + out_bias
        hat1, inv1 = normed(z1)
        n1 = hat1 * gain1 + shift1
        low = n1.astype(BF)
        n1_all[here] = low
        z2 = n1 + down_bias
        for k in range(4):
            cols = slice(k * units, (k + 1) * units)
            act, slope = gelu_parts(dot(low, ups[k][...], 1, 0) + biases[k][...])
            act = act.astype(BF)
            act_all[here, cols] = act
            gp_all[here, cols] = slope.astype(BF)
            z2 = z2 + dot(act, downs[k][...], 1, 0)
        hat2, inv2 = normed(z2)
        row = lax.broadcasted_iota(jnp.int32, (tile, 1), 0) + r * tile
        valid = (row < length).astype(F32)
        out_ref[here] = ((hat2 * gain2 + shift2) * valid).astype(BF)
        g_out = cot_ref[here].astype(F32) * valid
        g_z2 = norm_back(g_out, hat2, inv2, gain2)
        g_ffn = g_z2.astype(BF)
        gf_all[here] = g_ffn
        g_n1 = g_z2
        for k in range(4):
            cols = slice(k * units, (k + 1) * units)
            g_pre = (dot(g_ffn, downs[k][...], 1, 1) * gp_all[here, cols].astype(F32)).astype(BF)
            gp_all[here, cols] = g_pre
            dub_ref[k: k + 1] += jnp.sum(g_pre.astype(F32), axis=0, keepdims=True)
            g_n1 = g_n1 + dot(g_pre, ups[k][...], 1, 1)
        g_z1 = norm_back(g_n1, hat1, inv1, gain1)
        gz_ref[here] = g_z1
        g_attn = g_z1.astype(BF)
        ga_ref[here] = g_attn
        sums = (g_attn.astype(F32), g_n1 * hat1, g_n1, g_ffn.astype(F32), g_out * hat2, g_out)
        for k, v in enumerate(sums):
            common_ref[k: k + 1] += jnp.sum(v, axis=0, keepdims=True)

    flipped = n1_all[...].T
    for k in range(4):
        cols = slice(k * units, (k + 1) * units)
        to = (gm_ref, gp_ref)[k % 2].at[k // 2]
        to[:width] = dot(flipped, gp_all[:, cols], 1, 0).astype(BF)
        to[width:] = dot(act_all[:, cols], gf_all[...], 0, 0).astype(BF)


def dense(scalars, x, cot, ctxs, vec, wo, wu, wd, biases, packs):
    rows, width = x.shape
    pair = ctxs[0].shape[0]
    units = biases[1].shape[1]
    tile = 256
    args = [x, cot, *ctxs, vec, wo, wu, wd, *biases, *packs]
    whole = lambda a: pl.BlockSpec(a.shape, lambda i, s: (0,) * len(a.shape))
    outs = (
        jax.ShapeDtypeStruct((rows, width), BF),
        jax.ShapeDtypeStruct((rows, width), F32),
        jax.ShapeDtypeStruct((rows, width), BF),
        jax.ShapeDtypeStruct((2, width + units, width), BF),
        jax.ShapeDtypeStruct((2, width + units, width), BF),
        jax.ShapeDtypeStruct((4, units), F32),
        jax.ShapeDtypeStruct((6, width), F32),
    )
    return pl.pallas_call(
        partial(dense_kernel, tile=tile),
        out_shape=outs,
        grid_spec=pltpu.PrefetchScalarGridSpec(
            num_scalar_prefetch=1,
            grid=(1,),
            in_specs=[whole(a) for a in args],
            out_specs=tuple(whole(a) for a in outs),
            scratch_shapes=[
                pltpu.VMEM((4 * pair, width), BF),
                pltpu.VMEM((rows, width), BF),
                pltpu.VMEM((rows, width), BF),
                pltpu.VMEM((rows, 4 * units), BF),
                pltpu.VMEM((rows, 4 * units), BF),
            ],
        ),
        compiler_params=pltpu.CompilerParams(vmem_limit_bytes=VMEM_BYTES),
        cost_estimate=pl.CostEstimate(flops=14_000_000_000, bytes_accessed=20_000_000, transcendentals=4_000_000),
        name="dense",
    )(scalars, *args)


def input_kernel(scalars, gz_ref, w_own, w_m, w_p, g0, g1, g2, g3, out_ref, tile):
    rows, width = gz_ref.shape
    pair = g0.shape[1]
    core = scalars[0]
    spots = [pl.ds(pl.multiple_of((core ^ i) * pair, pair), pair) for i in range(2)]

    @pl.loop(0, rows // tile)
    def _(r):
        here = pl.ds(pl.multiple_of(r * tile, tile), tile)
        total = gz_ref[here]
        for c in range(3):
            g = jnp.concatenate([g0[c, :, here], g1[c, :, here], g2[c, :, here], g3[c, :, here]], axis=0)
            w = jnp.concatenate([w_own[c, :, spots[0]], w_own[c, :, spots[1]], w_m[c], w_p[c]], axis=1)
            total = total + dot(g, w, 0, 1)
        out_ref[here] = total


def input_gradient(scalars, gz, w_own, w_m, w_p, gs):
    args = [gz, w_own, w_m, w_p, *gs]
    whole = lambda a: pl.BlockSpec(a.shape, lambda i, s: (0,) * len(a.shape))
    return pl.pallas_call(
        partial(input_kernel, tile=256),
        out_shape=jax.ShapeDtypeStruct(gz.shape, F32),
        grid_spec=pltpu.PrefetchScalarGridSpec(
            num_scalar_prefetch=1, grid=(1,), in_specs=[whole(a) for a in args], out_specs=whole(gz)),
        compiler_params=pltpu.CompilerParams(vmem_limit_bytes=VMEM_BYTES),
        cost_estimate=pl.CostEstimate(flops=1_600_000_000, bytes_accessed=9_000_000, transcendentals=0),
        name="input_gradient",
    )(scalars, *args)


def send_tensor(a):
    n = lax.axis_size("tensor")
    return lax.ppermute(a, "tensor", [(i, (i + 1) % n) for i in range(n)])


def send_bit(a, bit):
    return lax.ppermute(a, "dp", [(i, i ^ (1 << bit)) for i in range(lax.axis_size("dp"))])


def pick(a, axis, index):
    return lax.dynamic_index_in_dim(a, index, axis, keepdims=False)


def plus(*members):
    return sum(m.astype(F32) for m in members).astype(BF)


def total_chips(buf):
    me = lax.axis_index("dp")
    bits = list(range(1, lax.axis_size("dp").bit_length() - 1))
    split, rest = bits[:3], bits[3:]
    for bit in split:
        side = (me >> bit) & 1
        half = buf.shape[0] // 2
        away = lax.dynamic_slice_in_dim(buf, (1 - side) * half, half, 0)
        kept = lax.dynamic_slice_in_dim(buf, side * half, half, 0)
        buf = plus(kept, send_bit(away, bit))
    for bit in rest:
        buf = plus(buf, send_bit(buf, bit))
    for bit in reversed(split):
        side = (me >> bit) & 1
        got = send_bit(buf, bit)
        buf = jnp.concatenate([jnp.where(side == 0, buf, got), jnp.where(side == 0, got, buf)], axis=0)
    return buf


def local(hidden_in, w_qkv, qv_bias, w_out, out_bias, gain1, shift1, w_up, up_bias, w_down,
          down_bias, gain2, shift2, lengths, head_perm, cotangent):
    rows, width = hidden_in.shape
    core = lax.axis_index("dp") % 2
    length = lengths[lax.axis_index("tensor")]
    pair = w_qkv.shape[2] // 2
    heads = head_perm.shape[0] // 2
    units = up_bias.shape[0] // 2

    def small_of(i):
        return jnp.concatenate([
            pick(qv_bias.reshape(2, 2, pair), 1, i).reshape(-1),
            pick(up_bias.reshape(2, units), 0, i),
            pick(head_perm.reshape(2, heads), 0, i).astype(F32)])

    small_m = send_tensor(small_of(core))
    wq_m = send_tensor(pick(w_qkv.reshape(3, width, 2, pair), 2, core))
    pack_m = send_tensor(jnp.concatenate([
        pick(w_up.reshape(width, 2, units), 1, core),
        pick(w_down.reshape(2, units, width), 0, core),
        pick(w_out.reshape(2, pair, width), 0, core)], axis=0))
    small_p, wq_p, pack_p = (send_bit(a, 0) for a in (small_m, wq_m, pack_m))

    smalls = [small_of(core), small_of(1 - core), small_m, small_p]
    wqs = [w_qkv, w_qkv, wq_m, wq_p]
    where = [core, 1 - core, 0, 0]
    scalars = [jnp.concatenate([jnp.stack([jnp.int32(where[k]), length]), smalls[k][2 * pair + units:].astype(jnp.int32)])
               for k in range(4)]
    kept = []
    for k in range(4):
        kept.append(attend_forward(hidden_in, wqs[k], smalls[k][: 2 * pair].reshape(2, pair, 1), scalars[k]))
    vec = jnp.stack([out_bias, gain1, shift1, down_bias, gain2, shift2])
    base = jnp.stack([core, length])
    ubs = [up_bias.reshape(1, -1), small_m[2 * pair: 2 * pair + units].reshape(1, -1),
           small_p[2 * pair: 2 * pair + units].reshape(1, -1)]
    out, g_z1, g_attn, ffn_m, ffn_p, dub, common = dense(
        base, hidden_in, cotangent, [a[3] for a in kept], vec, w_out, w_up, w_down, ubs, [pack_m, pack_p])

    ffn_got = send_bit(ffn_p, 0)
    ffn_other = plus(ffn_m[1], ffn_got[1])
    ffn_own = plus(ffn_m[0], ffn_got[0], send_tensor(ffn_other))

    wos = [w_out, w_out, pack_m, pack_p]
    blocks = [core, 1 - core, 2 * units // pair, 2 * units // pair]
    back = {}

    def backward(k):
        qkv, e, inv, ctx = kept[k]
        sc = jnp.concatenate([jnp.stack([jnp.int32(blocks[k])]), scalars[k][1:]])
        back[k] = attend_backward(hidden_in, wos[k], qkv, e, inv, ctx, g_attn, sc)

    def tiny(k, shared):
        sums = back[k][2].reshape(-1)
        line = jnp.concatenate([dub[k], sums, jnp.zeros((-sums.size % width,), F32)]).reshape(-1, width)
        return jnp.concatenate([line, shared, jnp.zeros((16 - line.shape[0] - shared.shape[0], width), F32)], axis=0)

    for k in (1, 3, 2, 0):
        backward(k)
    nothing = jnp.zeros_like(common)
    got = {k: send_bit(jnp.concatenate([back[k][1], tiny(k, common if k == 1 else nothing).astype(BF)], axis=0), 0)
           for k in (1, 3)}
    att_other = plus(jnp.concatenate([back[2][1], tiny(2, common).astype(BF)], axis=0), got[3])
    att_other = jnp.concatenate([att_other[: 4 * pair + 2], plus(att_other[4 * pair + 2:], got[1][4 * pair + 2:])], axis=0)
    att_own = plus(jnp.concatenate([back[0][1], tiny(0, common).astype(BF)], axis=0), got[1], send_tensor(att_other))

    x_grad = input_gradient(base, g_z1, w_qkv, wq_m, wq_p, [back[k][0] for k in range(4)])

    merged = jnp.concatenate([ffn_own, att_own], axis=0)
    merged = jnp.pad(merged, ((0, -merged.shape[0] % 128), (0, 0)))
    line = total_chips(merged)
    mate = send_bit(line, 0)
    a = jnp.where(core == 0, line, mate).astype(F32)
    b = jnp.where(core == 0, mate, line).astype(F32)
    at = [0, width, width + units, width + units + 3 * pair, width + units + 4 * pair]
    d_wu = jnp.concatenate([a[:at[1]], b[:at[1]]], axis=1)
    d_wd = jnp.concatenate([a[at[1]: at[2]], b[at[1]: at[2]]], axis=0)
    turn = lambda v: jnp.swapaxes(v[at[2]: at[3]].reshape(3, pair, width), 1, 2)
    d_wq = jnp.concatenate([turn(a), turn(b)], axis=2)
    d_wo = jnp.concatenate([a[at[3]: at[4]], b[at[3]: at[4]]], axis=0)
    d_ub = jnp.concatenate([a[at[4]], b[at[4]]], axis=0)
    d_qvb = jnp.concatenate([v[at[4] + 1, : 2 * pair].reshape(2, pair) for v in (a, b)], axis=1)
    com = a[at[4] + 2: at[4] + 8]
    return (out, x_grad, d_wq, d_qvb, d_wo, com[0], com[1], com[2], d_wu, d_ub, d_wd, com[3], com[4], com[5])


def solution(mesh):
    whole = P()
    rows = P(("dp", "tensor"), None)
    return jax.shard_map(
        local,
        mesh=mesh,
        in_specs=(rows, P(None, None, "tensor"), P(None, "tensor"), P("tensor", None), whole, whole, whole,
                  P(None, "tensor"), P("tensor"), P("tensor", None), whole, whole, whole, P("dp"), P("tensor"), rows),
        out_specs=(rows, rows, P(None, None, "tensor"), P(None, "tensor"), P("tensor", None), whole, whole, whole,
                   P(None, "tensor"), P("tensor"), P("tensor", None), whole, whole, whole),
        check_vma=False,
    )
```

time: 519 us -> 288 us (0.55); the launches traced: 510 us -> 285 us
  matrix products: 140 us -> 0 us
  local copies, waits for them, and re-layouts: 161 us -> 22.6 us
  Pallas kernels: 0 us -> 96.7 us
  other arithmetic: 72.5 us -> 31.5 us
  starting transfers between devices: 30.4 us -> 17.6 us
  waiting for transfers between devices: 103 us -> 115 us
    dot_general x68 -> x0, matrix products: 125 us -> none  [the longest x56 99.8 us: ein(): return jnp.einsum(spec, a, b, preferred_element_type=F32)]
    pallas_call x0 -> x10, Pallas kernels: none -> 96.7 us  [the longest x1 32 us: dense(): pl.pallas_call(partial(dense_kernel, tile=tile), out_shape=outs, grid_spe...]
    another operation x36 -> x5, local copies, waits for them, and re-layouts: 55.9 us -> 2.23 us  [the longest x2 1.6 us: local(): smalls[k][:2 * pair].reshape(2, pair, 1)]
    unnamed x337 -> x44, local copies, waits for them, and re-layouts: 46.5 us -> 2.33 us
    reshape x14 -> x15, local copies, waits for them, and re-layouts: 24.4 us -> 7.31 us  [the longest x2 4.59 us: local(): turn = lambda v: jnp.swapaxes(v[at[2]:at[3]].reshape(3, pair, width), 1, 2)]
    convert_element_type x20 -> x12, other arithmetic: 23.9 us -> 8.52 us  [the longest x8 7.54 us: plus(): return sum((m.astype(F32) for m in members)).astype(BF)]
    sub x4 -> x0, matrix products: 14.6 us -> none  [local(): e = jnp.exp(s - m)]
    ppermute x37 -> x18, waiting for transfers between devices: 103 us -> 115 us  [the longest x13 75.7 us: send_bit(): lax.ppermute(a, 'dp', [(i, i ^ 1 << bit) for i in range(lax.axis_size('dp...]
  transfers between devices with their start and end apart: 37 -> 18, of which waited for: 13 -> 10; matrix products, arithmetic and copies ran while one was open for 27% -> 8% of each run, Pallas kernels for 0% -> 17%
where the time goes in v2:
time: 288 us; the launch traced here: 285 us
  waiting for transfers between devices  115 us (40%)
  Pallas kernels  96.7 us (34%)
  other arithmetic  31.5 us (11%)
  local copies, waits for them, and re-layouts  22.6 us (8%)
  starting transfers between devices  17.6 us (6%)
    ppermute x13, waiting for transfers between devices, send_bit(): lax.ppermute(a, 'dp', [(i, i ^ 1 << bit) for i in range(lax.axis_size('dp...  75.7 us
    ppermute x5, waiting for transfers between devices, send_tensor(): return lax.ppermute(a, 'tensor', [(i, (i + 1) % n) for i in range(n)])  39.8 us
    pallas_call x1, Pallas kernels, dense(): pl.pallas_call(partial(dense_kernel, tile=tile), out_shape=outs, grid_spe...  32 us
    pallas_call x4, Pallas kernels, attend_backward(): pl.pallas_call(backward_kernel, out_shape=(jax.ShapeDtypeStruct((3, pair,...  30.8 us
    pallas_call x4, Pallas kernels, attend_forward(): pl.pallas_call(forward_kernel, out_shape=(jax.ShapeDtypeStruct((3, pair,...  26.5 us
    ppermute x13, starting transfers between devices, send_bit(): lax.ppermute(a, 'dp', [(i, i ^ 1 << bit) for i in range(lax.axis_size('dp...  14.4 us
    convert_element_type x8, other arithmetic, plus(): return sum((m.astype(F32) for m in members)).astype(BF)  7.54 us
    pallas_call x1, Pallas kernels, input_gradient(): pl.pallas_call(partial(input_kernel, tile=256), out_shape=jax.ShapeDtypeS...  7.4 us
  transfers between devices with their start and end apart: 18, of which 10 were waited for; matrix products, arithmetic and copies ran while one was open for 8% of the time, Pallas kernels for 17%

profile of v2, /device:TPU:5, one launch (start us, length us, event | category | flops | bytes accessed | tf_op | source)
XLA Modules:
  0.0 285.2 jit_solution(8873152003305261752)
XLA Ops:
  0.7 1.0 dynamic-slice_bitcast_fusion.1
  1.7 1.1 dynamic-slice_bitcast_fusion
  3.6 1.1 constant_dynamic-slice_fusion.3
  5.5 1.2 collective-permute-start
  6.9 0.8 constant_dynamic-slice_fusion.4
  8.2 0.8 copy.37.bias_ref
  9.0 0.8 copy.39.bias_ref
  10.4 1.2 pad_add_fusion.1.scalars
  11.6 1.2 pad_add_fusion.2.scalars
  12.9 6.6 %attend_forward.4 = (bf16[3,128,1024]{2,1,0:T(8,128)(2,1)}, bf16[2,2,512,512]{3,2,1,0:T(8,128)(2,1)}, f32[2,2,1,512]{3,2,1,0:T(1,128)}, bf16[128,1024]{1,0:T(8,128)(2,1)}) custom-call(s32[4]{0:T(128)} %pad_add_fusion.1.scalars, bf16[1024,512]{1,0:T(8,128)(2,1)} %x_ref.17, bf16[3,512,256]{2,1,0:T(8,128)(2,1)} %w_own.1, f32[2,128,1]{2,1,0:T(8,128)} %copy.37.bias_ref), custom_call_target="tpu_custom_call" | custom-call | flops 2000000000 | bytes 5000000 | tf_op jit(solution)/shard_map/attend_forward/pallas_call | solution.py:61
  19.5 6.7 %attend_forward.5 = (bf16[3,128,1024]{2,1,0:T(8,128)(2,1)}, bf16[2,2,512,512]{3,2,1,0:T(8,128)(2,1)}, f32[2,2,1,512]{3,2,1,0:T(1,128)}, bf16[128,1024]{1,0:T(8,128)(2,1)}) custom-call(s32[4]{0:T(128)} %pad_add_fusion.2.scalars, bf16[1024,512]{1,0:T(8,128)(2,1)} %x_ref.17, bf16[3,512,256]{2,1,0:T(8,128)(2,1)} %w_own.1, f32[2,128,1]{2,1,0:T(8,128)} %copy.39.bias_ref), custom_call_target="tpu_custom_call" | custom-call | flops 2000000000 | bytes 5000000 | tf_op jit(solution)/shard_map/attend_forward/pallas_call | solution.py:61
  26.2 1.2 pad_add_fusion.scalars
  28.3 3.8 %collective-permute-done = f32[770]{0:T(1024)S(1)} collective-permute-done((f32[770]{0:T(1024)S(1)}, f32[770]{0:T(1024)S(1)}, u32[]{:S(2)}, u32[]{:S(2)}) %collective-permute-start) | collective-permute-done | bytes 3112 | tf_op jit(solution)/shard_map/ppermute | solution.py:323
  32.0 2.6 collective-permute-start.5
  34.7 1.2 pad_add_fusion.5
  36.0 0.8 copy.41.bias_ref
  37.3 3.0 %collective-permute-done.1.w_ref.w_m = bf16[3,512,128]{2,1,0:T(8,128)(2,1)S(1)} collective-permute-done((bf16[3,512,128]{2,1,0:T(8,128)(2,1)S(1)}, bf16[3,512,128]{2,1,0:T(8,128)(2,1)S(1)}, u32[]{:S(2)}, u32[]{:S(2)}) %collective-permute-start.1) | collective-permute-done | bytes 393248 | tf_op jit(solution)/shard_map/ppermute | solution.py:323
  40.4 1.5 collective-permute-start.3
  41.9 0.8 copy.42.bias_ref
  43.3 1.3 pad_add_fusion.7
  44.6 6.6 %attend_forward.6 = (bf16[3,128,1024]{2,1,0:T(8,128)(2,1)}, bf16[2,2,512,512]{3,2,1,0:T(8,128)(2,1)}, f32[2,2,1,512]{3,2,1,0:T(1,128)}, bf16[128,1024]{1,0:T(8,128)(2,1)}) custom-call(s32[4]{0:T(128)} %get-tuple-element.122.scalars, bf16[1024,512]{1,0:T(8,128)(2,1)} %x_ref.17, bf16[3,512,128]{2,1,0:T(8,128)(2,1)} %copy-done.6, f32[2,128,1]{2,1,0:T(8,128)} %copy.41.bias_ref), custom_call_target="tpu_custom_call" | custom-call | flops 2000000000 | bytes 5000000 | tf_op jit(solution)/shard_map/attend_forward/pallas_call | solution.py:61
  51.9 6.7 %attend_forward.7 = (bf16[3,128,1024]{2,1,0:T(8,128)(2,1)}, bf16[2,2,512,512]{3,2,1,0:T(8,128)(2,1)}, f32[2,2,1,512]{3,2,1,0:T(1,128)}, bf16[128,1024]{1,0:T(8,128)(2,1)}) custom-call(s32[4]{0:T(128)} %get-tuple-element.120.scalars, bf16[1024,512]{1,0:T(8,128)(2,1)} %x_ref.17, bf16[3,512,128]{2,1,0:T(8,128)(2,1)} %copy-done.7, f32[2,128,1]{2,1,0:T(8,128)} %copy.42.bias_ref), custom_call_target="tpu_custom_call" | custom-call | flops 2000000000 | bytes 5000000 | tf_op jit(solution)/shard_map/attend_forward/pallas_call | solution.py:61
  58.6 1.0 copy-done.18
  59.6 32.0 %dense.1 = (bf16[1024,512]{1,0:T(8,128)(2,1)}, f32[1024,512]{1,0:T(8,128)}, bf16[1024,512]{1,0:T(8,128)(2,1)}, bf16[2,1024,512]{2,1,0:T(8,128)(2,1)}, bf16[2,102...) custom-call(s32[2]{0:T(128)} %pad_add_fusion.scalars, bf16[1024,512]{1,0:T(8,128)(2,1)} %x_ref.17, ...), custom_call_target="tpu_custom_call" | custom-call | flops 14000000000 | bytes 20000000 | tf_op jit(solution)/shard_map/dense/pallas_call | solution.py:268
  91.6 7.7 %attend_backward.4 = (bf16[3,128,1024]{2,1,0:T(8,128)(2,1)}, bf16[512,512]{1,0:T(8,128)(2,1)}, f32[2,128,1]{2,1,0:T(8,128)}) custom-call(s32[4]{0:T(128)} %pad_add_fusion.1.scalars, bf16[1024,512]{1,0:T(8,128)(2,1)} %x_ref.17, bf16[256,512]{1,0:T(8,128)(2,1)} %wo_ref.3, bf16[3,128,1024]{2,1,0:T(8,128)(2,1)} %get-tuple-element.55.qkv_ref, ...), custom_call_target="tpu_custom_call" | custom-call | flops 4000000000 | bytes 6000000 | tf_op jit(solution)/shard_map/attend_backward/pallas_call | solution.py:133
  99.3 1.0 convert_reduce_fusion.3
  100.4 7.6 %attend_backward.5 = (bf16[3,128,1024]{2,1,0:T(8,128)(2,1)}, bf16[512,512]{1,0:T(8,128)(2,1)}, f32[2,128,1]{2,1,0:T(8,128)}) custom-call(s32[4]{0:T(128)} %pad_add_fusion.2.scalars, bf16[1024,512]{1,0:T(8,128)(2,1)} %x_ref.17, bf16[256,512]{1,0:T(8,128)(2,1)} %wo_ref.3, bf16[3,128,1024]{2,1,0:T(8,128)(2,1)} %get-tuple-element.60.qkv_ref, ...), custom_call_target="tpu_custom_call" | custom-call | flops 4000000000 | bytes 6000000 | tf_op jit(solution)/shard_map/attend_backward/pallas_call | solution.py:133
  108.0 1.0 convert_reduce_fusion.2
  109.1 7.8 %attend_backward.6 = (bf16[3,128,1024]{2,1,0:T(8,128)(2,1)}, bf16[512,512]{1,0:T(8,128)(2,1)}, f32[2,128,1]{2,1,0:T(8,128)}) custom-call(s32[4]{0:T(128)} %get-tuple-element.121.scalars, bf16[1024,512]{1,0:T(8,128)(2,1)} %x_ref.17, bf16[1152,512]{1,0:T(8,128)(2,1)} %collective-permute-done.4.pack_m.wo_ref, bf16[3,128,1024]{2,1,0:T(8,128)(2,1)} %get-tuple-element.64.qkv_ref, ...), custom_call_target="tpu_custom_call" | custom-call | flops 4000000000 | bytes 6000000 | tf_op jit(solution)/shard_map/attend_backward/pallas_call | solution.py:133
  116.9 1.0 convert_reduce_fusion.1
  117.9 7.7 %attend_backward.7 = (bf16[3,128,1024]{2,1,0:T(8,128)(2,1)}, bf16[512,512]{1,0:T(8,128)(2,1)}, f32[2,128,1]{2,1,0:T(8,128)}) custom-call(s32[4]{0:T(128)} %get-tuple-element.119.scalars, bf16[1024,512]{1,0:T(8,128)(2,1)} %x_ref.17, bf16[1152,512]{1,0:T(8,128)(2,1)} %copy-done.18, bf16[3,128,1024]{2,1,0:T(8,128)(2,1)} %get-tuple-element.68.qkv_ref, ...), custom_call_target="tpu_custom_call" | custom-call | flops 4000000000 | bytes 6000000 | tf_op jit(solution)/shard_map/attend_backward/pallas_call | solution.py:133
  125.6 1.0 convert_reduce_fusion
  126.7 2.1 maximum_maximum_fusion
  129.4 1.8 collective-permute-done.9
  131.2 1.3 add_convert_fusion.3
  132.5 1.5 fusion.4
  134.9 0.8 pad_maximum_fusion.9
  135.7 1.4 collective-permute-start.10
  137.1 33.0 %collective-permute-done.10 = bf16[528,512]{1,0:T(8,128)(2,1)} collective-permute-done((bf16[528,512]{1,0:T(8,128)(2,1)}, bf16[528,512]{1,0:T(8,128)(2,1)}, u32[]{:S(2)}, u32[]{:S(2)}) %collective-permute-start.10) | collective-permute-done | bytes 540704 | tf_op jit(solution)/shard_map/ppermute | solution.py:323
  170.2 1.7 add_convert_fusion.2
  171.8 2.0 fusion.2
  174.0 1.3 collective-permute-start.11
  175.3 18.0 %collective-permute-done.11 = bf16[832,512]{1,0:T(8,128)(2,1)S(1)} collective-permute-done((bf16[832,512]{1,0:T(8,128)(2,1)S(1)}, bf16[832,512]{1,0:T(8,128)(2,1)S(1)}, u32[]{:S(2)}, u32[]{:S(2)}) %collective-permute-start.11) | collective-permute-done | bytes 852000 | tf_op jit(solution)/shard_map/ppermute | solution.py:327
  193.6 1.4 collective-permute-start.12
  194.9 7.9 %collective-permute-done.12 = bf16[416,512]{1,0:T(8,128)(2,1)S(1)} collective-permute-done((bf16[416,512]{1,0:T(8,128)(2,1)S(1)}, bf16[416,512]{1,0:T(8,128)(2,1)S(1)}, u32[]{:S(2)}, u32[]{:S(2)}) %collective-permute-start.12) | collective-permute-done | bytes 426016 | tf_op jit(solution)/shard_map/ppermute | solution.py:327
  203.0 2.4 collective-permute-start.13
  205.4 9.1 %collective-permute-done.13 = bf16[208,512]{1,0:T(8,128)(2,1)S(1)} collective-permute-done((bf16[208,512]{1,0:T(8,128)(2,1)S(1)}, bf16[208,512]{1,0:T(8,128)(2,1)S(1)}, u32[]{:S(2)}, u32[]{:S(2)}) %collective-permute-start.13) | collective-permute-done | bytes 213024 | tf_op jit(solution)/shard_map/ppermute | solution.py:327
  214.6 11.8 %collective-permute-done.14 = bf16[208,512]{1,0:T(8,128)(2,1)S(1)} collective-permute-done((bf16[208,512]{1,0:T(8,128)(2,1)S(1)}, bf16[208,512]{1,0:T(8,128)(2,1)S(1)}, u32[]{:S(2)}, u32[]{:S(2)}) %collective-permute-start.14) | collective-permute-done | bytes 213024 | tf_op jit(solution)/shard_map/ppermute | solution.py:327
  226.6 10.0 %collective-permute-done.15 = bf16[416,512]{1,0:T(8,128)(2,1)S(1)} collective-permute-done((bf16[416,512]{1,0:T(8,128)(2,1)S(1)}, bf16[416,512]{1,0:T(8,128)(2,1)S(1)}, u32[]{:S(2)}, u32[]{:S(2)}) %collective-permute-start.15) | collective-permute-done | bytes 426016 | tf_op jit(solution)/shard_map/ppermute | solution.py:327
  236.8 1.3 collective-permute-start.16
  238.1 17.0 %collective-permute-done.16 = bf16[832,512]{1,0:T(8,128)(2,1)S(1)} collective-permute-done((bf16[832,512]{1,0:T(8,128)(2,1)S(1)}, bf16[832,512]{1,0:T(8,128)(2,1)S(1)}, u32[]{:S(2)}, u32[]{:S(2)}) %collective-permute-start.16) | collective-permute-done | bytes 852000 | tf_op jit(solution)/shard_map/ppermute | solution.py:327
  255.4 1.3 pad_maximum_fusion.2
  256.7 3.1 %collective-permute-start.17 = (bf16[1664,512]{1,0:T(8,128)(2,1)}, bf16[1664,512]{1,0:T(8,128)(2,1)S(1)}, u32[]{:S(2)}, u32[]{:S(2)}) collective-permute-start(bf16[1664,512]{1,0:T(8,128)(2,1)} %pad_maximum_fusion.2), channel_id=1, source_target_pairs={{0,2},{2,0},{4,6},{6,4},{8,10},{10,8},{12,14},{14,12},{16,18},{18,... | collective-permute-start | bytes 5111816 | tf_op jit(solution)/shard_map/ppermute | solution.py:327
  259.9 7.4 %input_gradient.1 = f32[1024,512]{1,0:T(8,128)} custom-call(s32[2]{0:T(128)} %pad_add_fusion.scalars, f32[1024,512]{1,0:T(8,128)} %get-tuple-element.54.gz_ref, bf16[3,512,256]{2,1,0:T(8,128)(2,1)} %w_own.1, bf16[3,512,128]{2,1,0:T(8,128)(2,1)} %copy-done.6, bf16[3,512,128]{2,1,0:T(8,128)(2,1)} %copy-done.7, bf16[3,128,1024]{2,1,0:T(8,128)(2,1)} %get-tuple-element.59.g0, ...), custom_call_target="tpu_custom_call" | custom-call | flops 1600000000 | bytes 9000000 | tf_op jit(solution)/shard_map/input_gradient/pallas_call | solution.py:310
  267.3 1.0 select_convert_fusion.1
  268.2 0.9 slice.169
  269.2 0.9 slice.168
  271.5 1.5 fusion.19
  272.9 2.3 copy.45
  275.2 2.3 copy.44
  277.5 2.7 pad_maximum_fusion.3
  280.8 0.8 pad_maximum_fusion.10
  281.7 1.5 pad_maximum_fusion
  283.7 1.5 pad_maximum_fusion.1
  (112 shorter events, 11.1 us)
Async XLA Ops:
  0.6 2.1 copy-start.3
  4.7 0.7 copy-start.19
  4.7 0.7 copy-start.17
  4.7 0.8 copy-start.10
  4.7 2.0 copy-start.1
  4.9 27.1 %collective-permute-start.4 = (bf16[1152,512]{1,0:T(8,128)(2,1)S(1)}, bf16[1152,512]{1,0:T(8,128)(2,1)}, u32[]{:S(2)}, u32[]{:S(2)}) collective-permute-start(bf16[1152,512]{1,0:T(8,128)(2,1)S(1)} %pad_maximum_fusion.4), channel_id=1, source_target_pairs={{0,1},{1,0},{2,3},{3,2},{4,5},{5,4},{6,7},{7,6},{8,9},{9,8},{10,11... | collective-permute-start | bytes 3538952 | tf_op jit(solution)/shard_map/ppermute | solution.py:323
  5.5 26.5 %collective-permute-start = (f32[770]{0:T(1024)S(1)}, f32[770]{0:T(1024)S(1)}, u32[]{:S(2)}, u32[]{:S(2)}) collective-permute-start(f32[770]{0:T(1024)S(1)} %pad_maximum_fusion.16), channel_id=1, source_target_pairs={{0,1},{1,0},{2,3},{3,2},{4,5},{5,4},{6,7},{7,6},{8,9},{9,8},{10,11... | collective-permute-start | bytes 9248 | tf_op jit(solution)/shard_map/ppermute | solution.py:323
  6.9 2.9 %copy-start.20 = (s32[2]{0:T(128)S(1)}, s32[2]{0:T(128)}, u32[]{:S(2)}) copy-start(s32[2]{0:T(128)} %param.29) | copy-start | bytes 28
  7.8 32.5 %collective-permute-start.1 = (bf16[3,512,128]{2,1,0:T(8,128)(2,1)S(1)}, bf16[3,512,128]{2,1,0:T(8,128)(2,1)S(1)}, u32[]{:S(2)}, u32[]{:S(2)}) collective-permute-start(bf16[3,512,128]{2,1,0:T(8,128)(2,1)S(1)} %bitcast.69), channel_id=1, source_target_pairs={{0,1},{1,0},{2,3},{3,2},{4,5},{5,4},{6,7},{7,6},{8,9},{9,8},{10,11... | collective-permute-start | bytes 1179656 | tf_op jit(solution)/shard_map/ppermute | solution.py:323
  19.4 8.2 %copy-start.11 = (f32[512]{0:T(512)S(1)}, f32[512]{0:T(512)}, u32[]{:S(2)}) copy-start(f32[512]{0:T(512)} %param.20) | copy-start | bytes 6148
  19.4 8.2 %copy-start.12 = (f32[512]{0:T(512)S(1)}, f32[512]{0:T(512)}, u32[]{:S(2)}) copy-start(f32[512]{0:T(512)} %param.21) | copy-start | bytes 6148
  19.5 8.2 %copy-start.13 = (f32[512]{0:T(512)S(1)}, f32[512]{0:T(512)}, u32[]{:S(2)}) copy-start(f32[512]{0:T(512)} %param.22) | copy-start | bytes 6148
  19.5 8.2 %copy-start.14 = (f32[512]{0:T(512)S(1)}, f32[512]{0:T(512)}, u32[]{:S(2)}) copy-start(f32[512]{0:T(512)} %param.26) | copy-start | bytes 6148
  19.5 8.2 %copy-start.15 = (f32[512]{0:T(512)S(1)}, f32[512]{0:T(512)}, u32[]{:S(2)}) copy-start(f32[512]{0:T(512)} %param.27) | copy-start | bytes 6148
  19.5 8.2 %copy-start.16 = (f32[512]{0:T(512)S(1)}, f32[512]{0:T(512)}, u32[]{:S(2)}) copy-start(f32[512]{0:T(512)} %param.28) | copy-start | bytes 6148
  32.0 26.5 %collective-permute-start.5 = (bf16[1152,512]{1,0:T(8,128)(2,1)}, bf16[1152,512]{1,0:T(8,128)(2,1)S(1)}, u32[]{:S(2)}, u32[]{:S(2)}) collective-permute-start(bf16[1152,512]{1,0:T(8,128)(2,1)} %collective-permute-done.4.pack_m.wo_ref), channel_id=1, source_target_pairs={{0,2},{2,0},{4,6},{6,4},{8,10},{10,8},{12,14},{14,12},{16,18},{18,... | collective-permute-start | bytes 3538952 | tf_op jit(solution)/shard_map/ppermute | solution.py:327
  34.7 2.7 collective-permute-start.2
  40.4 4.2 %copy-start.6 = (bf16[3,512,128]{2,1,0:T(8,128)(2,1)}, bf16[3,512,128]{2,1,0:T(8,128)(2,1)S(1)}, u32[]{:S(2)}) copy-start(bf16[3,512,128]{2,1,0:T(8,128)(2,1)S(1)} %collective-permute-done.1.w_ref.w_m) | copy-start | bytes 1179652
  40.4 10.8 %collective-permute-start.3 = (bf16[3,512,128]{2,1,0:T(8,128)(2,1)S(1)}, bf16[3,512,128]{2,1,0:T(8,128)(2,1)S(1)}, u32[]{:S(2)}, u32[]{:S(2)}) collective-permute-start(bf16[3,512,128]{2,1,0:T(8,128)(2,1)S(1)} %collective-permute-done.1.w_ref.w_m), channel_id=1, source_target_pairs={{0,2},{2,0},{4,6},{6,4},{8,10},{10,8},{12,14},{14,12},{16,18},{18,... | collective-permute-start | bytes 1179656 | tf_op jit(solution)/shard_map/ppermute | solution.py:327
  51.2 0.7 copy-start.7
  58.6 1.0 copy-start.18
  91.6 8.7 %copy-start.9 = (f32[4,512]{1,0:T(4,128)S(1)}, f32[4,512]{1,0:T(4,128)}, u32[]{:S(2)}) copy-start(f32[4,512]{1,0:T(4,128)} %get-tuple-element.75) | copy-start | bytes 24580
  109.0 23.5 %collective-permute-start.6 = (bf16[2,1024,512]{2,1,0:T(8,128)(2,1)}, bf16[2,1024,512]{2,1,0:T(8,128)(2,1)}, u32[]{:S(2)}, u32[]{:S(2)}) collective-permute-start(bf16[2,1024,512]{2,1,0:T(8,128)(2,1)} %get-tuple-element.73), channel_id=1, source_target_pairs={{0,2},{2,0},{4,6},{6,4},{8,10},{10,8},{12,14},{14,12},{16,18},{18,... | collective-permute-start | bytes 6291464 | tf_op jit(solution)/shard_map/ppermute | solution.py:327
  117.9 8.8 %copy-start.8 = (f32[6,512]{1,0:T(8,128)S(1)}, f32[6,512]{1,0:T(8,128)}, u32[]{:S(2)}) copy-start(f32[6,512]{1,0:T(8,128)} %get-tuple-element.77) | copy-start | bytes 36868
  117.9 8.8 %copy-start.5 = (bf16[512,512]{1,0:T(8,128)(2,1)S(1)}, bf16[512,512]{1,0:T(8,128)(2,1)}, u32[]{:S(2)}) copy-start(bf16[512,512]{1,0:T(8,128)(2,1)} %get-tuple-element.78) | copy-start | bytes 1572868
  128.8 3.7 %copy-start.2 = (bf16[2,1024,512]{2,1,0:T(8,128)(2,1)S(1)}, bf16[2,1024,512]{2,1,0:T(8,128)(2,1)}, u32[]{:S(2)}) copy-start(bf16[2,1024,512]{2,1,0:T(8,128)(2,1)} %get-tuple-element.72) | copy-start | bytes 6291460
  128.9 2.3 collective-permute-start.9
  129.3 4.8 %collective-permute-start.8 = (bf16[528,512]{1,0:T(8,128)(2,1)}, bf16[528,512]{1,0:T(8,128)(2,1)}, u32[]{:S(2)}, u32[]{:S(2)}) collective-permute-start(bf16[528,512]{1,0:T(8,128)(2,1)} %get-tuple-element.110), channel_id=1, source_target_pairs={{0,2},{2,0},{4,6},{6,4},{8,10},{10,8},{12,14},{14,12},{16,18},{18,... | collective-permute-start | bytes 1622024 | tf_op jit(solution)/shard_map/ppermute | solution.py:327
  134.0 37.8 %collective-permute-start.7 = (bf16[1024,512]{1,0:T(8,128)(2,1)S(1)}, bf16[1024,512]{1,0:T(8,128)(2,1)}, u32[]{:S(2)}, u32[]{:S(2)}) collective-permute-start(bf16[1024,512]{1,0:T(8,128)(2,1)S(1)} %fusion.4), channel_id=1, source_target_pairs={{0,1},{1,0},{2,3},{3,2},{4,5},{5,4},{6,7},{7,6},{8,9},{9,8},{10,11... | collective-permute-start | bytes 3145736 | tf_op jit(solution)/shard_map/ppermute | solution.py:323
  135.7 34.5 %collective-permute-start.10 = (bf16[528,512]{1,0:T(8,128)(2,1)}, bf16[528,512]{1,0:T(8,128)(2,1)}, u32[]{:S(2)}, u32[]{:S(2)}) collective-permute-start(bf16[528,512]{1,0:T(8,128)(2,1)} %pad_maximum_fusion.9), channel_id=1, source_target_pairs={{0,1},{1,0},{2,3},{3,2},{4,5},{5,4},{6,7},{7,6},{8,9},{9,8},{10,11... | collective-permute-start | bytes 1622024 | tf_op jit(solution)/shard_map/ppermute | solution.py:323
  174.0 19.3 %collective-permute-start.11 = (bf16[832,512]{1,0:T(8,128)(2,1)S(1)}, bf16[832,512]{1,0:T(8,128)(2,1)S(1)}, u32[]{:S(2)}, u32[]{:S(2)}) collective-permute-start(bf16[832,512]{1,0:T(8,128)(2,1)S(1)} %constant_dynamic-slice_fusion.2), channel_id=1, source_target_pairs={{0,4},{2,6},{4,0},{6,2},{8,12},{10,14},{12,8},{14,10},{16,20},{18,... | collective-permute-start | bytes 2555912 | tf_op jit(solution)/shard_map/ppermute | solution.py:327
  193.6 9.3 %collective-permute-start.12 = (bf16[416,512]{1,0:T(8,128)(2,1)S(1)}, bf16[416,512]{1,0:T(8,128)(2,1)S(1)}, u32[]{:S(2)}, u32[]{:S(2)}) collective-permute-start(bf16[416,512]{1,0:T(8,128)(2,1)S(1)} %constant_dynamic-slice_fusion.1), channel_id=1, source_target_pairs={{0,8},{2,10},{4,12},{6,14},{8,0},{10,2},{12,4},{14,6},{16,24},{18,... | collective-permute-start | bytes 1277960 | tf_op jit(solution)/shard_map/ppermute | solution.py:327
  203.0 11.5 %collective-permute-start.13 = (bf16[208,512]{1,0:T(8,128)(2,1)S(1)}, bf16[208,512]{1,0:T(8,128)(2,1)S(1)}, u32[]{:S(2)}, u32[]{:S(2)}) collective-permute-start(bf16[208,512]{1,0:T(8,128)(2,1)S(1)} %constant_dynamic-slice_fusion), channel_id=1, source_target_pairs={{0,16},{2,18},{4,20},{6,22},{8,24},{10,26},{12,28},{14,30},{16,0},... | collective-permute-start | bytes 638984 | tf_op jit(solution)/shard_map/ppermute | solution.py:327
  214.6 11.9 %collective-permute-start.14 = (bf16[208,512]{1,0:T(8,128)(2,1)S(1)}, bf16[208,512]{1,0:T(8,128)(2,1)S(1)}, u32[]{:S(2)}, u32[]{:S(2)}) collective-permute-start(bf16[208,512]{1,0:T(8,128)(2,1)S(1)} %add_convert_fusion.5), channel_id=1, source_target_pairs={{0,16},{2,18},{4,20},{6,22},{8,24},{10,26},{12,28},{14,30},{16,0},... | collective-permute-start | bytes 638984 | tf_op jit(solution)/shard_map/ppermute | solution.py:327
  226.5 10.1 %collective-permute-start.15 = (bf16[416,512]{1,0:T(8,128)(2,1)S(1)}, bf16[416,512]{1,0:T(8,128)(2,1)S(1)}, u32[]{:S(2)}, u32[]{:S(2)}) collective-permute-start(bf16[416,512]{1,0:T(8,128)(2,1)S(1)} %pad_maximum_fusion.11), channel_id=1, source_target_pairs={{0,8},{2,10},{4,12},{6,14},{8,0},{10,2},{12,4},{14,6},{16,24},{18,... | collective-permute-start | bytes 1277960 | tf_op jit(solution)/shard_map/ppermute | solution.py:327
  236.8 18.3 %collective-permute-start.16 = (bf16[832,512]{1,0:T(8,128)(2,1)S(1)}, bf16[832,512]{1,0:T(8,128)(2,1)S(1)}, u32[]{:S(2)}, u32[]{:S(2)}) collective-permute-start(bf16[832,512]{1,0:T(8,128)(2,1)S(1)} %pad_maximum_fusion.8), channel_id=1, source_target_pairs={{0,4},{2,6},{4,0},{6,2},{8,12},{10,14},{12,8},{14,10},{16,20},{18,... | collective-permute-start | bytes 2555912 | tf_op jit(solution)/shard_map/ppermute | solution.py:327
  256.7 10.6 %collective-permute-start.17 = (bf16[1664,512]{1,0:T(8,128)(2,1)}, bf16[1664,512]{1,0:T(8,128)(2,1)S(1)}, u32[]{:S(2)}, u32[]{:S(2)}) collective-permute-start(bf16[1664,512]{1,0:T(8,128)(2,1)} %pad_maximum_fusion.2), channel_id=1, source_target_pairs={{0,2},{2,0},{4,6},{6,4},{8,10},{10,8},{12,14},{14,12},{16,18},{18,... | collective-permute-start | bytes 5111816 | tf_op jit(solution)/shard_map/ppermute | solution.py:327
  277.5 3.3 %copy-start.4 = (f32[128,512]{1,0:T(8,128)S(1)}, f32[128,512]{1,0:T(8,128)}, u32[]{:S(2)}) copy-start(f32[128,512]{1,0:T(8,128)} %slice.172) | copy-start | bytes 786436
  277.5 4.1 %copy-start = (f32[512,512]{1,0:T(8,128)S(1)}, f32[512,512]{1,0:T(8,128)}, u32[]{:S(2)}) copy-start(f32[512,512]{1,0:T(8,128)} %get-tuple-element.123) | copy-start | bytes 3145732

commit v3 on v2

v3 whole, which is shorter than its diff:
```python
import math
from functools import partial

import jax
import jax.numpy as jnp
from jax import lax
from jax.experimental import pallas as pl
from jax.experimental.pallas import tpu as pltpu
from jax.sharding import PartitionSpec as P

EPSILON = 1e-05
BF = jnp.bfloat16
F32 = jnp.float32
SMALL_ROWS = 64


def dot(a, b, ca, cb):
    return lax.dot_general(a, b, (((ca,), (cb,)), ((), ())), preferred_element_type=F32)


def place(index, size):
    return pl.ds(pl.multiple_of(index * size, size), size)


def whole(a):
    return pl.BlockSpec(a.shape, lambda *_: (0,) * len(a.shape))


def params(mebibytes):
    return pltpu.CompilerParams(vmem_limit_bytes=mebibytes * 1024 * 1024)


def cost(micros, size):
    return pl.CostEstimate(flops=int(micros * 1.1e9), bytes_accessed=size, transcendentals=0)


def forward_kernel(ids, x_ref, w_ref, bias_ref, *rest, slot):
    qkv_ref, e_ref, inv_ref, ctx_ref = rest[-4:]
    width, rows = qkv_ref.shape[1:]
    half = rows // 2
    heads = e_ref.shape[1]
    size = width // heads
    quarter = ids[0] ^ (slot % 2)
    i = pl.program_id(0)

    @pl.when(i == 0)
    def _():
        for c in range(3):
            part = dot(w_ref[c], x_ref[...], 0, 1)
            if c != 1:
                bias = bias_ref[c // 2: c // 2 + 1, place(quarter, width)]
                part = part + jnp.broadcast_to(bias, (width, width)).T[:, :1]
            qkv_ref[c] = part.astype(BF)

    mine = place(i, half)
    factor = math.log2(math.e) / math.sqrt(size)
    for h in range(heads):
        lanes = slice(h * size, (h + 1) * size)
        j = i ^ ids[4 + (slot // 2 * 2 + quarter) * heads + h]
        theirs = place(j, half)
        s = dot(qkv_ref[1, lanes, theirs], qkv_ref[0, lanes, mine], 0, 0)
        key = lax.broadcasted_iota(jnp.int32, (half, 1), 0) + j * half
        s = jnp.where(key < ids[1], s, -1e30)
        top = jnp.max(s, axis=0, keepdims=True)
        e = jnp.exp2((s - top) * factor)
        inv = 1.0 / jnp.sum(e, axis=0, keepdims=True)
        low = e.astype(BF)
        e_ref[0, h] = low
        inv_ref[0, h] = inv
        ctx = dot(qkv_ref[2, lanes, theirs], low, 1, 0) * inv
        ctx_ref[lanes, mine] = ctx.astype(BF)


def attend_forward(ids, x, w, bias, slot, heads, pair, waits=()):
    rows, width = x.shape
    half = rows // 2
    fixed = lambda *shape: pl.BlockSpec(shape, lambda i, *_: (0,) * len(shape))
    return pl.pallas_call(
        partial(forward_kernel, slot=slot),
        out_shape=(
            pltpu.HBM((3, pair, rows), BF),
            pltpu.HBM((2, heads, half, half), BF),
            pltpu.HBM((2, heads, 1, half), F32),
            pltpu.HBM((pair, rows), BF),
        ),
        grid_spec=pltpu.PrefetchScalarGridSpec(
            num_scalar_prefetch=1,
            grid=(2,),
            in_specs=[
                fixed(rows, width),
                pl.BlockSpec((3, width, pair), lambda i, s, *_: (0, 0, (s[0] ^ slot) if slot < 2 else 0)),
                fixed(*bias.shape),
                *[pl.BlockSpec(memory_space=pl.ANY) for _ in waits],
            ],
            out_specs=(
                fixed(3, pair, rows),
                pl.BlockSpec((1, heads, half, half), lambda i, *_: (i, 0, 0, 0)),
                pl.BlockSpec((1, heads, 1, half), lambda i, *_: (i, 0, 0, 0)),
                fixed(pair, rows),
            ),
        ),
        compiler_params=params(16),
        cost_estimate=cost(0.5, 400_000),
        name="attend_forward",
    )(ids, x, w, bias, *waits)


def backward_kernel(ids, x_ref, wo_ref, qkv_ref, e_ref, inv_ref, ctx_ref, ga_ref, small_ref, *rest, slot):
    g_ref, dw_ref, gc_ref = rest[-3:]
    width, rows = gc_ref.shape
    half = rows // 2
    heads = e_ref.shape[1]
    size = width // heads
    quarter = ids[0] ^ (slot % 2)
    i = pl.program_id(0)

    @pl.when(i == 0)
    def _():
        gc_ref[...] = dot(wo_ref[...], ga_ref[...], 1, 1).astype(BF)
        dw_ref[3 * width: 4 * width] = dot(ctx_ref[...], ga_ref[...], 1, 0).astype(BF)

    mine = place(i, half)
    scaling = 1.0 / math.sqrt(size)
    for h in range(heads):
        lanes = slice(h * size, (h + 1) * size)
        j = i ^ ids[4 + (slot // 2 * 2 + quarter) * heads + h]
        theirs = place(j, half)
        g = gc_ref[lanes, mine].astype(F32) * inv_ref[0, h]
        inner = jnp.sum(g * ctx_ref[lanes, mine].astype(F32), axis=0, keepdims=True)
        g = g.astype(BF)
        e = e_ref[0, h]
        dp = dot(qkv_ref[2, lanes, theirs], g, 0, 0)
        ds = (e.astype(F32) * (dp - inner)).astype(BF)
        g_ref[2, lanes, theirs] = dot(g, e, 1, 1).astype(BF)
        g_ref[1, lanes, theirs] = (dot(qkv_ref[0, lanes, mine], ds, 1, 1) * scaling).astype(BF)
        g_ref[0, lanes, mine] = (dot(qkv_ref[1, lanes, theirs], ds, 1, 0) * scaling).astype(BF)

    @pl.when(i == 1)
    def _():
        small = small_ref[0]
        row = lax.broadcasted_iota(jnp.int32, small.shape, 0)
        for c in range(3):
            dw_ref[c * width: (c + 1) * width] = dot(g_ref[c], x_ref[...], 1, 0).astype(BF)
        ones = jnp.ones((8, rows), BF)
        sums = jnp.concatenate([dot(ones, g_ref[c], 1, 1) for c in (0, 2)] * 2, axis=1)
        small = jnp.where(row == 1, sums, small)
        small = jnp.concatenate([small, jnp.zeros((SMALL_ROWS - 8, small.shape[1]), F32)], axis=0)
        dw_ref[4 * width:] = small.astype(BF)


def attend_backward(ids, x, wo, block, kept, g_attn, small, slot, waits=()):
    qkv, e, inv, ctx = kept
    rows, width = x.shape
    heads = e.shape[1]
    pair = ctx.shape[0]
    half = rows // 2
    fixed = lambda *shape: pl.BlockSpec(shape, lambda i, *_: (0,) * len(shape))
    return pl.pallas_call(
        partial(backward_kernel, slot=slot),
        out_shape=(
            jax.ShapeDtypeStruct((3, pair, rows), BF),
            jax.ShapeDtypeStruct((4 * pair + SMALL_ROWS, width), BF),
        ),
        grid_spec=pltpu.PrefetchScalarGridSpec(
            num_scalar_prefetch=1,
            grid=(2,),
            in_specs=[
                fixed(rows, width),
                pl.BlockSpec((pair, width), lambda i, s: (block(s[0]), 0)),
                fixed(3, pair, rows),
                pl.BlockSpec((1, heads, half, half), lambda i, *_: (i, 0, 0, 0)),
                pl.BlockSpec((1, heads, 1, half), lambda i, *_: (i, 0, 0, 0)),
                fixed(pair, rows),
                fixed(rows, width),
                pl.BlockSpec((1, 8, width), lambda i, *_: (slot, 0, 0)),
                *[pl.BlockSpec(memory_space=pl.ANY) for _ in waits],
            ],
            out_specs=(fixed(3, pair, rows), fixed(4 * pair + SMALL_ROWS, width)),
            scratch_shapes=[pltpu.VMEM((pair, rows), BF)],
        ),
        compiler_params=params(16),
        cost_estimate=cost(7.8, 4_000_000),
        name="attend_backward",
    )(ids, x, wo, qkv, e, inv, ctx, g_attn, small, *waits)


def normed(v):
    centre = v - jnp.mean(v, axis=-1, keepdims=True)
    inv = lax.rsqrt(jnp.mean(centre * centre, axis=-1, keepdims=True) + EPSILON)
    return centre * inv, inv


def norm_back(g, hat, inv, gain):
    g = g * gain
    return (g - jnp.mean(g, axis=-1, keepdims=True) - hat * jnp.mean(g * hat, axis=-1, keepdims=True)) * inv


def gelu_parts(v):
    t = 1.0 / (1.0 + (0.3275911 * math.sqrt(0.5)) * jnp.abs(v))
    bell = jnp.exp2(v * v * (-0.5 * math.log2(math.e)))
    poly = ((((0.5 * 1.061405429 * t - 0.5 * 1.453152027) * t + 0.5 * 1.421413741) * t
             - 0.5 * 0.284496736) * t + 0.5 * 0.254829592) * t
    tail = poly * bell
    cdf = jnp.where(v < 0, tail, 1.0 - tail)
    return v * cdf, cdf + v * bell * (1.0 / math.sqrt(2.0 * math.pi))


def dense_kernel(ids, x_ref, cot_ref, c0, c1, c2, c3, out_bias, gain1, shift1, down_bias, gain2, shift2,
                 wo_own, wu_own, wd_own, ub_own, wo_m, wu_m, wd_m, ub_other, wo_p, wu_p, wd_p,
                 out_ref, gz_ref, ga_ref, gm_ref, gp_ref, small_ref,
                 wo_all, n1_all, gf_all, act_all, gp_all, tile):
    rows, width = x_ref.shape
    pair = c0.shape[0]
    units = ub_own.shape[1] // 2
    core, length = ids[0], ids[1]

    wo_all[0:pair] = wo_own[place(core, pair)]
    wo_all[pair: 2 * pair] = wo_own[place(1 - core, pair)]
    wo_all[2 * pair: 3 * pair] = wo_m[...]
    wo_all[3 * pair:] = wo_p[...]
    near, far = place(core, units), place(1 - core, units)
    ups = [wu_own.at[:, near], wu_own.at[:, far], wu_m, wu_p]
    downs = [wd_own.at[near], wd_own.at[far], wd_m, wd_p]
    biases = [ub_own.at[:, near], ub_own.at[:, far],
              ub_other.at[:, near], ub_other.at[:, far]]
    small_ref[...] = jnp.zeros_like(small_ref)

    @pl.loop(0, rows // tile)
    def _(r):
        here = place(r, tile)
        ctx = jnp.concatenate([c[:, here] for c in (c0, c1, c2, c3)], axis=0)
        z1 = x_ref[here].astype(F32) + dot(ctx, wo_all[...], 0, 0) + out_bias[...]
        hat1, inv1 = normed(z1)
        n1 = hat1 * gain1[...] + shift1[...]
        low = n1.astype(BF)
        n1_all[here] = low
        z2 = n1 + down_bias[...]
        for k in range(4):
            cols = slice(k * units, (k + 1) * units)
            act, slope = gelu_parts(dot(low, ups[k][...], 1, 0) + biases[k][...])
            act = act.astype(BF)
            act_all[here, cols] = act
            gp_all[here, cols] = slope.astype(BF)
            z2 = z2 + dot(act, downs[k][...], 1, 0)
        hat2, inv2 = normed(z2)
        row = lax.broadcasted_iota(jnp.int32, (tile, 1), 0) + r * tile
        valid = (row < length).astype(F32)
        out_ref[here] = ((hat2 * gain2[...] + shift2[...]) * valid).astype(BF)
        g_out = cot_ref[here].astype(F32) * valid
        g_z2 = norm_back(g_out, hat2, inv2, gain2[...])
        g_ffn = g_z2.astype(BF)
        gf_all[here] = g_ffn
        g_n1 = g_z2
        for k in range(4):
            cols = slice(k * units, (k + 1) * units)
            g_pre = (dot(g_ffn, downs[k][...], 1, 1) * gp_all[here, cols].astype(F32)).astype(BF)
            gp_all[here, cols] = g_pre
            small_ref[k, 0:1] += jnp.sum(g_pre.astype(F32), axis=0, keepdims=True)
            g_n1 = g_n1 + dot(g_pre, ups[k][...], 1, 1)
        g_z1 = norm_back(g_n1, hat1, inv1, gain1[...])
        gz_ref[here] = g_z1
        g_attn = g_z1.astype(BF)
        ga_ref[here] = g_attn
        sums = (g_attn.astype(F32), g_n1 * hat1, g_n1, g_ffn.astype(F32), g_out * hat2, g_out)
        for k, v in enumerate(sums):
            small_ref[0, 2 + k: 3 + k] += jnp.sum(v, axis=0, keepdims=True)

    for k in range(1, 4):
        small_ref[k, 2:8] = small_ref[0, 2:8]
    flipped = n1_all[...].T
    for k in range(4):
        cols = slice(k * units, (k + 1) * units)
        to = (gm_ref, gp_ref)[k % 2].at[k // 2]
        to[:width] = dot(flipped, gp_all[:, cols], 1, 0).astype(BF)
        to[width:] = dot(act_all[:, cols], gf_all[...], 0, 0).astype(BF)


def dense(ids, x, cot, ctxs, vecs, own, other):
    rows, width = x.shape
    pair = ctxs[0].shape[0]
    units = own[3].shape[1] // 2
    args = [x, cot, *ctxs, *vecs, *own, *other]
    outs = (
        jax.ShapeDtypeStruct((rows, width), BF),
        jax.ShapeDtypeStruct((rows, width), F32),
        jax.ShapeDtypeStruct((rows, width), BF),
        jax.ShapeDtypeStruct((2, width + units, width), BF),
        jax.ShapeDtypeStruct((2, width + units, width), BF),
        jax.ShapeDtypeStruct((4, 8, width), F32),
    )
    return pl.pallas_call(
        partial(dense_kernel, tile=256),
        out_shape=outs,
        grid_spec=pltpu.PrefetchScalarGridSpec(
            num_scalar_prefetch=1,
            grid=(1,),
            in_specs=[whole(a) for a in args],
            out_specs=tuple(whole(a) for a in outs),
            scratch_shapes=[
                pltpu.VMEM((4 * pair, width), BF),
                pltpu.VMEM((rows, width), BF),
                pltpu.VMEM((rows, width), BF),
                pltpu.VMEM((rows, 4 * units), BF),
                pltpu.VMEM((rows, 4 * units), BF),
            ],
        ),
        compiler_params=params(36),
        cost_estimate=cost(31, 20_000_000),
        name="dense",
    )(ids, *args)


def input_kernel(ids, gz_ref, w_own, w_m, w_p, g0, g1, g2, g3, *rest, tile):
    out_ref = rest[-1]
    rows, width = gz_ref.shape
    pair = g0.shape[1]
    core = ids[0]

    @pl.loop(0, rows // tile)
    def _(r):
        here = place(r, tile)
        total = gz_ref[here]
        for c in range(3):
            g = jnp.concatenate([g0[c, :, here], g1[c, :, here], g2[c, :, here], g3[c, :, here]], axis=0)
            w = jnp.concatenate([w_own[c, :, place(core, pair)], w_own[c, :, place(1 - core, pair)], w_m[c], w_p[c]], axis=1)
            total = total + dot(g, w, 0, 1)
        out_ref[here] = total


def input_gradient(ids, gz, w_own, w_m, w_p, gs, waits=()):
    args = [gz, w_own, w_m, w_p, *gs]
    return pl.pallas_call(
        partial(input_kernel, tile=256),
        out_shape=jax.ShapeDtypeStruct(gz.shape, F32),
        grid_spec=pltpu.PrefetchScalarGridSpec(
            num_scalar_prefetch=1, grid=(1,),
            in_specs=[whole(a) for a in args] + [pl.BlockSpec(memory_space=pl.ANY) for _ in waits],
            out_specs=whole(gz)),
        compiler_params=params(20),
        cost_estimate=cost(7, 9_000_000),
        name="input_gradient",
    )(ids, *args, *waits)


def attention_kernel(ids, mine_near, mine_far, mate_near, mate_far, dwq_ref, dqb_ref, dwo_ref, dub_ref,
                     v0, v1, v2, v3, v4, v5, both):
    core, side = ids[0], ids[2]
    part = mine_near.shape[0]
    pair = dwo_ref.shape[0] // 2
    units = dub_ref.shape[1] // 2
    for c, near, far in ((core, mine_near, mine_far), (1 - core, mate_near, mate_far)):
        both[c, pl.ds(pl.multiple_of(side * part, 8), part)] = near[...].astype(F32)
        both[c, pl.ds(pl.multiple_of((1 - side) * part, 8), part)] = far[...].astype(F32)
    for m in range(2):
        cols = slice(m * pair, (m + 1) * pair)
        for c in range(3):
            dwq_ref[c, :, cols] = both[m, c * pair: (c + 1) * pair].T
        dwo_ref[cols] = both[m, 3 * pair: 4 * pair]
        dub_ref[:, m * units: (m + 1) * units] = both[m, 4 * pair: 4 * pair + 1]
        for c in range(2):
            dqb_ref[c: c + 1, cols] = both[m, 4 * pair + 1: 4 * pair + 2, c * pair: (c + 1) * pair]
    for k, ref in enumerate((v0, v1, v2, v3, v4, v5)):
        ref[...] = both[0, 4 * pair + 2 + k: 4 * pair + 3 + k]


def assemble_attention(ids, parts, pair, units):
    width = parts[0].shape[1]
    outs = [(3, width, 2 * pair), (2, 2 * pair), (2 * pair, width), (1, 2 * units)] + [(1, width)] * 6
    outs = tuple(jax.ShapeDtypeStruct(s, F32) for s in outs)
    return pl.pallas_call(
        attention_kernel,
        out_shape=outs,
        grid_spec=pltpu.PrefetchScalarGridSpec(
            num_scalar_prefetch=1, grid=(1,), in_specs=[whole(a) for a in parts],
            out_specs=tuple(whole(a) for a in outs),
            scratch_shapes=[pltpu.VMEM((2, 2 * parts[0].shape[0], width), F32)]),
        compiler_params=params(16),
        cost_estimate=cost(3, 4_000_000),
        name="assemble_attention",
    )(ids, *parts)


def dense_out_kernel(ids, mine_near, mine_far, mate_near, mate_far, dwu_ref, dwd_ref):
    core, side = ids[0], ids[2]
    units = mine_near.shape[1]
    part = mine_near.shape[0] // 2
    width = dwu_ref.shape[0]
    for c, near, far in ((core, mine_near, mine_far), (1 - core, mate_near, mate_far)):
        for s, ref in ((side, near), (1 - side, far)):
            dwu_ref[place(s, part), place(c, units)] = ref[:part].astype(F32)
            dwd_ref[pl.ds(pl.multiple_of(c * width + s * part, part), part)] = ref[part:].astype(F32)


def assemble_dense(ids, parts, units):
    width = parts[0].shape[1]
    outs = tuple(jax.ShapeDtypeStruct(s, F32) for s in ((width, 2 * units), (2 * units, width)))
    return pl.pallas_call(
        dense_out_kernel,
        out_shape=outs,
        grid_spec=pltpu.PrefetchScalarGridSpec(
            num_scalar_prefetch=1, grid=(1,), in_specs=[whole(a) for a in parts],
            out_specs=tuple(whole(a) for a in outs)),
        compiler_params=params(20),
        cost_estimate=cost(3, 6_000_000),
        name="assemble_dense",
    )(ids, *parts)


def send_tensor(a):
    n = lax.axis_size("tensor")
    return lax.ppermute(a, "tensor", [(i, (i + 1) % n) for i in range(n)])


def send_bit(a, bit):
    return lax.ppermute(a, "dp", [(i, i ^ (1 << bit)) for i in range(lax.axis_size("dp"))])


def plus(*members):
    return sum(m.astype(F32) for m in members).astype(BF)


def tie(*arrays):
    return lax.optimization_barrier(arrays)


def half_of(a, side, axis=0):
    n = a.shape[axis] // 2
    return lax.dynamic_slice_in_dim(a, side * n, n, axis)


def joined(mine, got, side, axis=0):
    return jnp.concatenate([jnp.where(side == 0, mine, got), jnp.where(side == 0, got, mine)], axis=axis)


def local(hidden_in, w_qkv, qv_bias, w_out, out_bias, gain1, shift1, w_up, up_bias, w_down,
          down_bias, gain2, shift2, lengths, head_perm, cotangent):
    rows, width = hidden_in.shape
    me = lax.axis_index("dp")
    core, xside, zside = me & 1, (me >> 1) & 1, (me >> 2) & 1
    upper_bits = range(3, lax.axis_size("dp").bit_length() - 1)
    pair = w_qkv.shape[2] // 2
    heads = head_perm.shape[0] // 2
    units = up_bias.shape[0] // 2
    row = lambda v: v.reshape(1, -1)
    def fetch(a, axis, rows_axis):
        sizes = list(a.shape)
        starts = [0] * a.ndim
        for dim, index in ((axis, core), (rows_axis, xside)):
            sizes[dim] //= 2
            starts[dim] += index * sizes[dim]
        return lax.dynamic_slice(a, starts, sizes)

    def forward(slot, w, bias, waits=()):
        return attend_forward(ids, hidden_in, w, bias, slot, heads, pair, waits)

    perm_other, bias_other, ub_other = send_tensor(head_perm), send_tensor(qv_bias), send_tensor(up_bias)
    pieces = [fetch(w_qkv, 2, 1), fetch(w_up, 1, 0), fetch(w_down, 0, 0), fetch(w_out, 0, 0)]
    *pieces, perm_other, bias_other, ub_other = tie(*pieces, perm_other, bias_other, ub_other)
    wq_m, wu_m, wd_m, wo_m = (send_tensor(a) for a in pieces)
    ids = jnp.concatenate([core.reshape(1), lax.dynamic_slice_in_dim(lengths, lax.axis_index("tensor"), 1, 0),
                             xside.reshape(1), zside.reshape(1), head_perm, perm_other])
    kept = [forward(0, w_qkv, qv_bias, pieces)]
    wq_m, ctx = tie(wq_m, kept[0][3])
    wq_got = send_bit(wq_m, 1)
    kept.append(forward(1, w_qkv, qv_bias))
    wq_got, wu_m, ctx1 = tie(wq_got, wu_m, kept[1][3])
    wu_got = send_bit(wu_m, 1)
    wq_m = joined(wq_m, wq_got, xside, 1)
    wq_p = send_bit(wq_m, 0)
    kept.append(forward(2, wq_m, bias_other))
    wd_m, wo_m, wu_got, ctx2 = tie(wd_m, wo_m, wu_got, kept[2][3])
    wd_got, wo_got = send_bit(wd_m, 1), send_bit(wo_m, 1)
    wu_m = joined(wu_m, wu_got, xside)
    wu_p = send_bit(wu_m, 0)
    kept.append(forward(3, wq_p, bias_other))
    wd_got, wo_got, wu_p, ctx3 = tie(wd_got, wo_got, wu_p, kept[3][3])
    wd_m, wo_m = joined(wd_m, wd_got, xside), joined(wo_m, wo_got, xside)
    ctxs = [ctx, ctx1, ctx2, ctx3]
    wo_p, wd_p = send_bit(wo_m, 0), send_bit(wd_m, 0)
    out, g_z1, g_attn, ffn_m, ffn_p, smalls = dense(
        ids, hidden_in, cotangent, ctxs,
        [row(v) for v in (out_bias, gain1, shift1, down_bias, gain2, shift2)],
        [w_out, w_up, w_down, row(up_bias)], [wo_m, wu_m, wd_m, row(ub_other), wo_p, wu_p, wd_p])

    def backward(k, waits=()):
        if k < 2:
            wo, block = w_out, lambda c: c ^ k
        else:
            wo, block = (wo_m, wo_p)[k - 2], lambda c: 0
        return attend_backward(ids, hidden_in, wo, block, kept[k], g_attn, smalls, k, waits)

    ffn_got = send_bit(ffn_p, 0)
    up = [(ffn_m[t, :width], ffn_got[t, :width]) for t in range(2)]
    down = [(ffn_m[t, width:], ffn_got[t, width:]) for t in range(2)]
    up_other = plus(*up[1])
    up_got = send_tensor(up_other)
    down_away = jnp.stack([plus(*[half_of(v, 1 - xside) for v in down[t]]) for t in range(2)])
    down_got = send_bit(down_away, 1)
    g3, d3 = backward(3, (up_other, down_away))
    d3_got = send_bit(d3, 0)
    g2, d2 = backward(2, (d3,))
    other_away = plus(*[half_of(v, 1 - xside) for v in (d2, d3_got)])
    other_got = send_bit(other_away, 1)
    g1, d1 = backward(1, (other_away,))
    d1, up_got, down_got = tie(d1, up_got, down_got)
    d1_got = send_bit(d1, 0)
    up_away = plus(*[half_of(v, 1 - xside) for v in (*up[0], up_got)])
    down_other = plus(*[half_of(v, xside) for v in down[1]], down_got[1])
    up_away, down_other, other_got = tie(up_away, down_other, other_got)
    att_other = plus(*[half_of(v, xside) for v in (d2, d3_got)], other_got)
    up_got2 = send_bit(up_away, 1)
    down_got2 = send_tensor(down_other)
    att_got = send_tensor(att_other)
    g0, d0 = backward(0, (up_away, down_other, att_other))
    att_away = plus(*[half_of(v, 1 - xside) for v in (d0, d1_got)])
    att_got2 = send_bit(att_away, 1)
    att_away, up_got2, down_got2 = tie(att_away, up_got2, down_got2)
    ffn = jnp.concatenate([
        plus(*[half_of(v, xside) for v in (*up[0], up_got)], up_got2),
        plus(*[half_of(v, xside) for v in down[0]], down_got[0], down_got2)], axis=0)
    ffn_away = half_of(ffn, 1 - zside)
    ffn_got2 = send_bit(ffn_away, 2)
    x_grad = input_gradient(ids, g_z1, w_qkv, wq_m, wq_p, [g0, g1, g2, g3], (att_away, ffn_away))
    x_grad, att_got, att_got2, ffn_got2 = tie(x_grad, att_got, att_got2, ffn_got2)
    att = plus(*[half_of(v, xside) for v in (d0, d1_got)], att_got, att_got2)
    att_got3 = send_bit(half_of(att, 1 - zside), 2)
    ffn = plus(half_of(ffn, zside), ffn_got2)
    att = plus(half_of(att, zside), att_got3)
    for bit in upper_bits:
        ffn, att = plus(ffn, send_bit(ffn, bit)), plus(att, send_bit(att, bit))
    ffn = joined(ffn, send_bit(ffn, 2), zside)
    att = joined(att, send_bit(att, 2), zside)
    ffn_far = send_bit(ffn, 1)
    att_far = send_bit(att, 1)
    d_wu, d_wd = assemble_dense(ids, [ffn, ffn_far, send_bit(ffn, 0), send_bit(ffn_far, 0)], units)
    d_wu, att_far = tie(d_wu, att_far)
    d_wq, d_qb, d_wo, d_ub, *vecs = assemble_attention(
        ids, [att, att_far, send_bit(att, 0), send_bit(att_far, 0)], pair, units)
    v = [a.reshape(-1) for a in vecs]
    return (out, x_grad, d_wq, d_qb, d_wo, v[0], v[1], v[2], d_wu, d_ub.reshape(-1), d_wd, v[3], v[4], v[5])


def solution(mesh):
    every = P()
    rows = P(("dp", "tensor"), None)
    return jax.shard_map(
        local,
        mesh=mesh,
        in_specs=(rows, P(None, None, "tensor"), P(None, "tensor"), P("tensor", None), every, every, every,
                  P(None, "tensor"), P("tensor"), P("tensor", None), every, every, every, P("dp"), P("tensor"), rows),
        out_specs=(rows, rows, P(None, None, "tensor"), P(None, "tensor"), P("tensor", None), every, every, every,
                   P(None, "tensor"), P("tensor"), P("tensor", None), every, every, every),
        check_vma=False,
    )
```

time: 288 us -> 180 us (0.62)
  waiting for transfers between devices: 115 us -> 41.3 us
  other arithmetic: 31.5 us -> 5.56 us
  Pallas kernels: 96.7 us -> 75.9 us
  starting transfers between devices: 17.6 us -> 38.4 us
  local copies, waits for them, and re-layouts: 22.6 us -> 15.4 us
    ppermute x5 -> x10, waiting for transfers between devices: 39.8 us -> 0.03 us  [send_tensor(): return lax.ppermute(a, 'tensor', [(i, (i + 1) % n) for i in range(n)])]
    ppermute x13 -> x27, waiting for transfers between devices: 75.7 us -> 41.3 us  [send_bit(): lax.ppermute(a, 'dp', [(i, i ^ 1 << bit) for i in range(lax.axis_size('dp...]
    pallas_call x9 -> x11, Pallas kernels: 89.3 us -> 71.6 us  [the longest x1 28.8 us: dense(): pl.pallas_call(partial(dense_kernel, tile=256), out_shape=outs, grid_spec...]
    concatenate x19 -> x7, other arithmetic: 17.2 us -> 0.52 us  [the longest x1 0.35 us: local(): jnp.concatenate([plus(*[half_of(v, xside) for v in (*up[0], up_got)], up_...]
    ppermute x13 -> x27, starting transfers between devices: 14.4 us -> 30.9 us  [send_bit(): lax.ppermute(a, 'dp', [(i, i ^ 1 << bit) for i in range(lax.axis_size('dp...]
    reshape x15 -> x0, local copies, waits for them, and re-layouts: 7.31 us -> none  [the longest x2 4.59 us: local(): turn = lambda v: jnp.swapaxes(v[at[2]:at[3]].reshape(3, pair, width), 1, 2)]
    another operation x7 -> x1, other arithmetic: 5.27 us -> 0.05 us  [local(): jnp.stack([plus(*[half_of(v, 1 - xside) for v in down[t]]) for t in range...]
    unnamed x44 -> x92, local copies, waits for them, and re-layouts: 2.33 us -> 7.27 us
  transfers between devices with their start and end apart: 18 -> 37, of which waited for: 10 -> 13; matrix products, arithmetic and copies ran while one was open for 8% -> 6% of each run, Pallas kernels for 17% -> 25%
where the time goes in v3:
time: 180 us; the launch traced here: 178 us
  Pallas kernels  75.9 us (42%)
  waiting for transfers between devices  41.3 us (23%)
  starting transfers between devices  38.4 us (21%)
  local copies, waits for them, and re-layouts  15.4 us (9%)
  other arithmetic  5.56 us (3%)
    ppermute x27, waiting for transfers between devices, send_bit(): lax.ppermute(a, 'dp', [(i, i ^ 1 << bit) for i in range(lax.axis_size('dp...  41.3 us
    ppermute x27, starting transfers between devices, send_bit(): lax.ppermute(a, 'dp', [(i, i ^ 1 << bit) for i in range(lax.axis_size('dp...  30.9 us
    pallas_call x1, Pallas kernels, dense(): pl.pallas_call(partial(dense_kernel, tile=256), out_shape=outs, grid_spec...  28.8 us
    pallas_call x4, Pallas kernels, attend_forward(): pl.pallas_call(partial(forward_kernel, slot=slot), out_shape=(pltpu.HBM((...  20.5 us
    pallas_call x4, Pallas kernels, attend_backward(): pl.pallas_call(partial(backward_kernel, slot=slot), out_shape=(jax.ShapeD...  17 us
    ppermute x10, starting transfers between devices, send_tensor(): return lax.ppermute(a, 'tensor', [(i, (i + 1) % n) for i in range(n)])  7.46 us
    unnamed x92, local copies, waits for them, and re-layouts  7.27 us
    pallas_call x1, Pallas kernels, input_gradient(): pl.pallas_call(partial(input_kernel, tile=256), out_shape=jax.ShapeDtypeS...  4.34 us
  transfers between devices with their start and end apart: 37, of which 13 were waited for; matrix products, arithmetic and copies ran while one was open for 6% of the time, Pallas kernels for 25%

profile of v3, /device:TPU:5, one launch (start us, length us, event | category | flops | bytes accessed | tf_op | source)
XLA Modules:
  0.0 177.9 jit_solution(17752293809024471252)
XLA Ops:
  0.7 1.5 collective-permute-start.1
  2.3 1.0 constant_dynamic-slice_fusion.2.rest_2_
  3.2 1.0 constant_dynamic-slice_fusion.3.rest_0_
  4.2 0.9 constant_dynamic-slice_fusion.1.rest_3_
  5.0 1.0 dynamic_slice.95.rest_1_
  6.0 1.5 collective-permute-start.3
  7.6 1.2 dynamic_slice.93
  8.8 1.4 concatenate.24.ids
  10.2 1.2 copy-done.1
  11.4 0.7 copy-done.8
  12.1 5.2 %attend_forward.4 = (bf16[3,128,1024]{2,1,0:T(8,128)(2,1)}, bf16[2,2,512,512]{3,2,1,0:T(8,128)(2,1)}, f32[2,2,1,512]{3,2,1,0:T(1,128)}, bf16[128,1024]{1,0:T(8,128)(2,1)}) custom-call(s32[12]{0:T(128)S(1)} %concatenate.24.ids, bf16[1024,512]{1,0:T(8,128)(2,1)S(1)} %copy-done.1, bf16[3,512,256]{2,1,0:T(8,128)(2,1)S(1)} %copy-done, f32[2,256]{1,0:T(2,128)S(1)} %copy-done.8, ...), custom_call_target="tpu_custom_call" | custom-call | flops 550000000 | bytes 400000 | tf_op jit(solution)/shard_map/attend_forward/pallas_call | solution.py:78
  17.3 1.4 collective-permute-start.4
  18.7 1.2 collective-permute-start.6
  20.2 5.2 %attend_forward.5 = (bf16[3,128,1024]{2,1,0:T(8,128)(2,1)}, bf16[2,2,512,512]{3,2,1,0:T(8,128)(2,1)}, f32[2,2,1,512]{3,2,1,0:T(1,128)}, bf16[128,1024]{1,0:T(8,128)(2,1)}) custom-call(s32[12]{0:T(128)S(1)} %concatenate.24.ids, bf16[1024,512]{1,0:T(8,128)(2,1)S(1)} %copy-done.1, bf16[3,512,256]{2,1,0:T(8,128)(2,1)S(1)} %copy-done, f32[2,256]{1,0:T(2,128)S(1)} %copy-done.8), custom_call_target="tpu_custom_call" | custom-call | flops 550000000 | bytes 400000 | tf_op jit(solution)/shard_map/attend_forward/pallas_call | solution.py:78
  25.6 5.1 %attend_forward.6 = (bf16[3,128,1024]{2,1,0:T(8,128)(2,1)}, bf16[2,2,512,512]{3,2,1,0:T(8,128)(2,1)}, f32[2,2,1,512]{3,2,1,0:T(1,128)}, bf16[128,1024]{1,0:T(8,128)(2,1)}) custom-call(s32[12]{0:T(128)S(1)} %concatenate.24.ids, bf16[1024,512]{1,0:T(8,128)(2,1)S(1)} %copy-done.1, bf16[3,512,128]{2,1,0:T(8,128)(2,1)S(1)} %pad_maximum_fusion.4.w_ref.w_m, ...), custom_call_target="tpu_custom_call" | custom-call | flops 550000000 | bytes 400000 | tf_op jit(solution)/shard_map/attend_forward/pallas_call | solution.py:78
  30.8 1.0 broadcast_select_fusion.5
  32.1 4.1 %collective-permute-start.11 = (bf16[512,512]{1,0:T(8,128)(2,1)S(1)}, bf16[512,512]{1,0:T(8,128)(2,1)S(1)}, u32[]{:S(2)}, u32[]{:S(2)}) collective-permute-start(bf16[512,512]{1,0:T(8,128)(2,1)S(1)} %pad_maximum_fusion.wu_m), channel_id=1, source_target_pairs={{0,2},{2,0},{4,6},{6,4},{8,10},{10,8},{12,14},{14,12},{16,18},{18,... | collective-permute-start | bytes 1572872 | tf_op jit(solution)/shard_map/ppermute | solution.py:415
  36.6 1.1 collective-permute-start.10
  37.7 0.6 collective-permute-done.12.w_ref.w_p
  38.3 5.1 %attend_forward.7 = (bf16[3,128,1024]{2,1,0:T(8,128)(2,1)}, bf16[2,2,512,512]{3,2,1,0:T(8,128)(2,1)}, f32[2,2,1,512]{3,2,1,0:T(1,128)}, bf16[128,1024]{1,0:T(8,128)(2,1)}) custom-call(s32[12]{0:T(128)S(1)} %concatenate.24.ids, bf16[1024,512]{1,0:T(8,128)(2,1)S(1)} %copy-done.1, bf16[3,512,128]{2,1,0:T(8,128)(2,1)S(1)} %collective-permute-done.12.w_ref.w_p, ...), custom_call_target="tpu_custom_call" | custom-call | flops 550000000 | bytes 400000 | tf_op jit(solution)/shard_map/attend_forward/pallas_call | solution.py:78
  43.4 1.7 collective-permute-done.10
  45.2 1.3 collective-permute-start.14
  46.7 1.6 collective-permute-done.13.wo_p.wo_ref
  48.4 0.9 copy-done.34
  49.4 28.8 %dense.1 = (bf16[1024,512]{1,0:T(8,128)(2,1)}, f32[1024,512]{1,0:T(8,128)S(1)}, bf16[1024,512]{1,0:T(8,128)(2,1)S(1)}, bf16[2,1024,512]{2,1,0:T(8,128)(2,1)S(1)}...) custom-call(s32[12]{0:T(128)S(1)} %concatenate.24.ids, bf16[1024,512]{1,0:T(8,128)(2,1)S(1)} %copy-done.2, ...), custom_call_target="tpu_custom_call" | custom-call | flops 34100000768 | bytes 20000000 | tf_op jit(solution)/shard_map/dense/pallas_call | solution.py:291
  78.2 1.3 copy-done.39
  79.5 1.0 copy-done.41
  80.5 0.6 copy-done.43
  81.6 4.0 %collective-permute-done.15 = bf16[2,1024,512]{2,1,0:T(8,128)(2,1)} collective-permute-done((bf16[2,1024,512]{2,1,0:T(8,128)(2,1)}, bf16[2,1024,512]{2,1,0:T(8,128)(2,1)}, u32[]{:S(2)}, u32[]{:S(2)}) %collective-permute-start.15) | collective-permute-done | bytes 2097184 | tf_op jit(solution)/shard_map/ppermute | solution.py:415
  85.6 1.2 fusion.rest_0_
  86.8 1.3 collective-permute-start.17
  88.1 1.6 fusion.9
  90.0 0.4 collective-permute-start.18
  90.4 0.7 copy-done.3
  91.4 4.2 %attend_backward.4 = (bf16[3,128,1024]{2,1,0:T(8,128)(2,1)S(1)}, bf16[576,512]{1,0:T(8,128)(2,1)S(1)}) custom-call(s32[12]{0:T(128)S(1)} %concatenate.24.ids, bf16[1024,512]{1,0:T(8,128)(2,1)S(1)} %copy-done.3, bf16[128,512]{1,0:T(8,128)(2,1)S(1)} %collective-permute-done.13.wo_p.wo_ref, bf16[3,128,1024]{2,1,0:T(8,128)(2,1)S(1)} %copy-done.31, ...), custom_call_target="tpu_custom_call" | custom-call | flops 8579999744 | bytes 4000000 | tf_op jit(solution)/shard_map/attend_backward/pallas_call | solution.py:158
  95.6 0.7 collective-permute-start.16
  96.4 4.4 %attend_backward.5 = (bf16[3,128,1024]{2,1,0:T(8,128)(2,1)S(1)}, bf16[576,512]{1,0:T(8,128)(2,1)S(1)}) custom-call(s32[12]{0:T(128)S(1)} %concatenate.24.ids, bf16[1024,512]{1,0:T(8,128)(2,1)S(1)} %copy-done.3, bf16[128,512]{1,0:T(8,128)(2,1)S(1)} %pad_maximum_fusion.6.wo_m.wo_ref, bf16[3,128,1024]{2,1,0:T(8,128)(2,1)S(1)} %copy-done.30, ...), custom_call_target="tpu_custom_call" | custom-call | flops 8579999744 | bytes 4000000 | tf_op jit(solution)/shard_map/attend_backward/pallas_call | solution.py:158
  100.9 0.5 collective-permute-start.19
  101.4 4.2 %attend_backward.6 = (bf16[3,128,1024]{2,1,0:T(8,128)(2,1)S(1)}, bf16[576,512]{1,0:T(8,128)(2,1)S(1)}) custom-call(s32[12]{0:T(128)S(1)} %concatenate.24.ids, bf16[1024,512]{1,0:T(8,128)(2,1)S(1)} %copy-done.3, bf16[256,512]{1,0:T(8,128)(2,1)S(1)} %copy-done.7, bf16[3,128,1024]{2,1,0:T(8,128)(2,1)S(1)} %copy-done.25, ...), custom_call_target="tpu_custom_call" | custom-call | flops 8579999744 | bytes 4000000 | tf_op jit(solution)/shard_map/attend_backward/pallas_call | solution.py:158
  106.2 3.8 %collective-permute-done.19 = bf16[288,512]{1,0:T(8,128)(2,1)S(1)} collective-permute-done((bf16[288,512]{1,0:T(8,128)(2,1)S(1)}, bf16[288,512]{1,0:T(8,128)(2,1)S(1)}, u32[]{:S(2)}, u32[]{:S(2)}) %collective-permute-start.19) | collective-permute-done | bytes 294944 | tf_op jit(solution)/shard_map/ppermute | solution.py:415
  110.7 1.3 collective-permute-start.23
  112.0 4.2 %attend_backward.7 = (bf16[3,128,1024]{2,1,0:T(8,128)(2,1)S(1)}, bf16[576,512]{1,0:T(8,128)(2,1)S(1)}) custom-call(s32[12]{0:T(128)S(1)} %concatenate.24.ids, bf16[1024,512]{1,0:T(8,128)(2,1)S(1)} %copy-done.3, bf16[256,512]{1,0:T(8,128)(2,1)S(1)} %copy-done.7, bf16[3,128,1024]{2,1,0:T(8,128)(2,1)S(1)} %copy-done.11, bf16[2,2,512,512]{3,2,1,0:T(8,128)(2,1)S(1)} %copy-done.9, ...), custom_call_target="tpu_custom_call" | custom-call | flops 8579999744 | bytes 4000000 | tf_op jit(solution)/shard_map/attend_backward/pallas_call | solution.py:158
  116.3 1.2 collective-permute-start.24
  118.2 1.4 collective-permute-start.25
  119.5 4.3 %input_gradient.1 = f32[1024,512]{1,0:T(8,128)} custom-call(s32[12]{0:T(128)S(1)} %concatenate.24.ids, f32[1024,512]{1,0:T(8,128)S(1)} %copy-done.40, bf16[3,512,256]{2,1,0:T(8,128)(2,1)S(1)} %copy-done, bf16[3,512,128]{2,1,0:T(8,128)(2,1)S(1)} %pad_maximum_fusion.4.w_ref.w_m, bf16[3,512,128]{2,1,0:T(8,128)(2,1)S(1)} %copy-done.13, ...), custom_call_target="tpu_custom_call" | custom-call | flops 7699999744 | bytes 9000000 | tf_op jit(solution)/shard_map/input_gradient/pallas_call | solution.py:332
  124.6 2.3 %collective-permute-start.29 = (bf16[256,512]{1,0:T(8,128)(2,1)S(1)}, bf16[256,512]{1,0:T(8,128)(2,1)S(1)}, u32[]{:S(2)}, u32[]{:S(2)}) collective-permute-start(bf16[256,512]{1,0:T(8,128)(2,1)S(1)} %add_convert_fusion.6), channel_id=1, source_target_pairs={{0,16},{2,18},{4,20},{6,22},{8,24},{10,26},{12,28},{14,30},{16,0},... | collective-permute-start | bytes 786440 | tf_op jit(solution)/shard_map/ppermute | solution.py:415
  126.9 11.4 %collective-permute-done.29 = bf16[256,512]{1,0:T(8,128)(2,1)S(1)} collective-permute-done((bf16[256,512]{1,0:T(8,128)(2,1)S(1)}, bf16[256,512]{1,0:T(8,128)(2,1)S(1)}, u32[]{:S(2)}, u32[]{:S(2)}) %collective-permute-start.29) | collective-permute-done | bytes 262176 | tf_op jit(solution)/shard_map/ppermute | solution.py:415
  138.4 1.2 add_convert_fusion.1
  139.6 1.5 collective-permute-start.26
  141.2 3.4 %collective-permute-done.30 = bf16[256,512]{1,0:T(8,128)(2,1)S(1)} collective-permute-done((bf16[256,512]{1,0:T(8,128)(2,1)S(1)}, bf16[256,512]{1,0:T(8,128)(2,1)S(1)}, u32[]{:S(2)}, u32[]{:S(2)}) %collective-permute-start.30) | collective-permute-done | bytes 262176 | tf_op jit(solution)/shard_map/ppermute | solution.py:415
  144.7 0.4 collective-permute-start.31
  145.1 2.7 %collective-permute-done.26 = bf16[144,512]{1,0:T(8,128)(2,1)S(1)} collective-permute-done((bf16[144,512]{1,0:T(8,128)(2,1)S(1)}, bf16[144,512]{1,0:T(8,128)(2,1)S(1)}, u32[]{:S(2)}, u32[]{:S(2)}) %collective-permute-start.26) | collective-permute-done | bytes 147488 | tf_op jit(solution)/shard_map/ppermute | solution.py:415
  147.8 1.8 collective-permute-start.27
  149.6 2.7 %collective-permute-start.32 = (bf16[512,512]{1,0:T(8,128)(2,1)S(1)}, bf16[512,512]{1,0:T(8,128)(2,1)S(1)}, u32[]{:S(2)}, u32[]{:S(2)}) collective-permute-start(bf16[512,512]{1,0:T(8,128)(2,1)S(1)} %pad_maximum_fusion.3.mine_near), channel_id=1, source_target_pairs={{0,2},{2,0},{4,6},{6,4},{8,10},{10,8},{12,14},{14,12},{16,18},{18,... | collective-permute-start | bytes 1572872 | tf_op jit(solution)/shard_map/ppermute | solution.py:415
  152.3 1.8 collective-permute-done.31.mine_far
  154.1 5.0 %collective-permute-start.33 = (bf16[512,512]{1,0:T(8,128)(2,1)S(1)}, bf16[512,512]{1,0:T(8,128)(2,1)S(1)}, u32[]{:S(2)}, u32[]{:S(2)}) collective-permute-start(bf16[512,512]{1,0:T(8,128)(2,1)S(1)} %collective-permute-done.31.mine_far), channel_id=1, source_target_pairs={{0,2},{2,0},{4,6},{6,4},{8,10},{10,8},{12,14},{14,12},{16,18},{18,... | collective-permute-start | bytes 1572872 | tf_op jit(solution)/shard_map/ppermute | solution.py:415
  159.2 5.5 %collective-permute-done.28 = bf16[144,512]{1,0:T(8,128)(2,1)S(1)} collective-permute-done((bf16[144,512]{1,0:T(8,128)(2,1)S(1)}, bf16[144,512]{1,0:T(8,128)(2,1)S(1)}, u32[]{:S(2)}, u32[]{:S(2)}) %collective-permute-start.28) | collective-permute-done | bytes 147488 | tf_op jit(solution)/shard_map/ppermute | solution.py:415
  164.7 0.4 collective-permute-start.34
  165.2 1.1 collective-permute-start.35
  166.2 2.8 %assemble_dense.1 = (f32[512,1024]{1,0:T(8,128)}, f32[1024,512]{1,0:T(8,128)}) custom-call(s32[12]{0:T(128)S(1)} %concatenate.24.ids, bf16[512,512]{1,0:T(8,128)(2,1)S(1)} %pad_maximum_fusion.3.mine_near, bf16[512,512]{1,0:T(8,128)(2,1)S(1)} %collective-permute-done.31.mine_far, bf16[512,512]{1,0:T(8,128)(2,1)S(1)} %collective-permute-done.32.mate_near, ...), custom_call_target="tpu_custom_call" | custom-call | flops 3300000000 | bytes 6000000 | tf_op jit(solution)/shard_map/assemble_dense/pallas_call | solution.py:397
  169.0 3.5 %collective-permute-done.34.mine_far = bf16[288,512]{1,0:T(8,128)(2,1)S(1)} collective-permute-done((bf16[288,512]{1,0:T(8,128)(2,1)S(1)}, bf16[288,512]{1,0:T(8,128)(2,1)S(1)}, u32[]{:S(2)}, u32[]{:S(2)}) %collective-permute-start.34) | collective-permute-done | bytes 294944 | tf_op jit(solution)/shard_map/ppermute | solution.py:415
  172.6 1.7 collective-permute-start.36
  174.2 1.2 collective-permute-done.36.mate_far
  175.4 2.5 %assemble_attention.1 = (f32[3,512,256]{2,1,0:T(8,128)}, f32[2,256]{1,0:T(2,128)}, f32[256,512]{1,0:T(8,128)}, f32[1,1024]{1,0:T(1,128)}, f32[1,512]{1,0:T(1,128...) custom-call(s32[12]{0:T(128)S(1)} %concatenate.24.ids, ...), custom_call_target="tpu_custom_call" | custom-call | flops 3300000000 | bytes 4000000 | tf_op jit(solution)/shard_map/assemble_attention/pallas_call | solution.py:370
  (151 shorter events, 5.9 us)
Async XLA Ops:
  0.6 9.6 %copy-start = (bf16[3,512,256]{2,1,0:T(8,128)(2,1)S(1)}, bf16[3,512,256]{2,1,0:T(8,128)(2,1)}, u32[]{:S(2)}) copy-start(bf16[3,512,256]{2,1,0:T(8,128)(2,1)} %w_own.1) | copy-start | bytes 2359300
  0.7 5.4 %collective-permute-start = (s32[4]{0:T(128)}, s32[4]{0:T(128)S(1)}, u32[]{:S(2)}, u32[]{:S(2)}) collective-permute-start(s32[4]{0:T(128)} %param.30), channel_id=1, source_target_pairs={{0,1},{1,0},{2,3},{3,2},{4,5},{5,4},{6,7},{7,6},{8,9},{9,8},{10,11... | collective-permute-start | bytes 56 | tf_op jit(solution)/shard_map/ppermute | solution.py:411
  0.7 5.3 %collective-permute-start.1 = (f32[2,256]{1,0:T(2,128)}, f32[2,256]{1,0:T(2,128)S(1)}, u32[]{:S(2)}, u32[]{:S(2)}) collective-permute-start(f32[2,256]{1,0:T(2,128)} %bias_ref.3), channel_id=1, source_target_pairs={{0,1},{1,0},{2,3},{3,2},{4,5},{5,4},{6,7},{7,6},{8,9},{9,8},{10,11... | collective-permute-start | bytes 6152 | tf_op jit(solution)/shard_map/ppermute | solution.py:411
  2.2 3.9 %collective-permute-start.2 = (f32[1024]{0:T(1024)}, f32[1024]{0:T(1024)S(1)}, u32[]{:S(2)}, u32[]{:S(2)}) collective-permute-start(f32[1024]{0:T(1024)} %param.24), channel_id=1, source_target_pairs={{0,1},{1,0},{2,3},{3,2},{4,5},{5,4},{6,7},{7,6},{8,9},{9,8},{10,11... | collective-permute-start | bytes 12296 | tf_op jit(solution)/shard_map/ppermute | solution.py:411
  6.0 11.2 %collective-permute-start.3 = (bf16[3,256,128]{2,1,0:T(8,128)(2,1)S(1)}, bf16[3,256,128]{2,1,0:T(8,128)(2,1)S(1)}, u32[]{:S(2)}, u32[]{:S(2)}) collective-permute-start(bf16[3,256,128]{2,1,0:T(8,128)(2,1)S(1)} %constant_dynamic-slice_fusion.3.rest_0_), channel_id=1, source_target_pairs={{0,1},{1,0},{2,3},{3,2},{4,5},{5,4},{6,7},{7,6},{8,9},{9,8},{10,11... | collective-permute-start | bytes 589832 | tf_op jit(solution)/shard_map/ppermute | solution.py:411
  7.5 17.8 %collective-permute-start.5 = (bf16[256,512]{1,0:T(8,128)(2,1)S(1)}, bf16[256,512]{1,0:T(8,128)(2,1)}, u32[]{:S(2)}, u32[]{:S(2)}) collective-permute-start(bf16[256,512]{1,0:T(8,128)(2,1)S(1)} %dynamic_slice.95.rest_1_), channel_id=1, source_target_pairs={{0,1},{1,0},{2,3},{3,2},{4,5},{5,4},{6,7},{7,6},{8,9},{9,8},{10,11... | collective-permute-start | bytes 786440 | tf_op jit(solution)/shard_map/ppermute | solution.py:411
  17.3 8.0 %collective-permute-start.4 = (bf16[3,256,128]{2,1,0:T(8,128)(2,1)S(1)}, bf16[3,256,128]{2,1,0:T(8,128)(2,1)S(1)}, u32[]{:S(2)}, u32[]{:S(2)}) collective-permute-start(bf16[3,256,128]{2,1,0:T(8,128)(2,1)S(1)} %collective-permute-done.3), channel_id=1, source_target_pairs={{0,4},{2,6},{4,0},{6,2},{8,12},{10,14},{12,8},{14,10},{16,20},{18,... | collective-permute-start | bytes 589832 | tf_op jit(solution)/shard_map/ppermute | solution.py:415
  18.7 12.0 %collective-permute-start.6 = (bf16[256,512]{1,0:T(8,128)(2,1)S(1)}, bf16[256,512]{1,0:T(8,128)(2,1)S(1)}, u32[]{:S(2)}, u32[]{:S(2)}) collective-permute-start(bf16[256,512]{1,0:T(8,128)(2,1)S(1)} %constant_dynamic-slice_fusion.2.rest_2_), channel_id=1, source_target_pairs={{0,1},{1,0},{2,3},{3,2},{4,5},{5,4},{6,7},{7,6},{8,9},{9,8},{10,11... | collective-permute-start | bytes 786440 | tf_op jit(solution)/shard_map/ppermute | solution.py:411
  19.9 10.7 %collective-permute-start.7 = (bf16[64,512]{1,0:T(8,128)(2,1)S(1)}, bf16[64,512]{1,0:T(8,128)(2,1)S(1)}, u32[]{:S(2)}, u32[]{:S(2)}) collective-permute-start(bf16[64,512]{1,0:T(8,128)(2,1)S(1)} %constant_dynamic-slice_fusion.1.rest_3_), channel_id=1, source_target_pairs={{0,1},{1,0},{2,3},{3,2},{4,5},{5,4},{6,7},{7,6},{8,9},{9,8},{10,11... | collective-permute-start | bytes 196616 | tf_op jit(solution)/shard_map/ppermute | solution.py:411
  25.3 5.5 %collective-permute-start.8 = (bf16[256,512]{1,0:T(8,128)(2,1)}, bf16[256,512]{1,0:T(8,128)(2,1)S(1)}, u32[]{:S(2)}, u32[]{:S(2)}) collective-permute-start(bf16[256,512]{1,0:T(8,128)(2,1)} %collective-permute-done.5), channel_id=1, source_target_pairs={{0,4},{2,6},{4,0},{6,2},{8,12},{10,14},{12,8},{14,10},{16,20},{18,... | collective-permute-start | bytes 786440 | tf_op jit(solution)/shard_map/ppermute | solution.py:415
  31.9 16.4 %copy-start.14 = (bf16[128,1024]{1,0:T(8,128)(2,1)S(1)}, bf16[128,1024]{1,0:T(8,128)(2,1)}, u32[]{:S(2)}) copy-start(bf16[128,1024]{1,0:T(8,128)(2,1)} %get-tuple-element.97.c0.ctx_ref) | copy-start | bytes 786436
  31.9 16.4 %copy-start.26 = (bf16[128,1024]{1,0:T(8,128)(2,1)S(1)}, bf16[128,1024]{1,0:T(8,128)(2,1)}, u32[]{:S(2)}) copy-start(bf16[128,1024]{1,0:T(8,128)(2,1)} %get-tuple-element.100.c1.ctx_ref) | copy-start | bytes 786436
  31.9 16.4 %copy-start.32 = (bf16[128,1024]{1,0:T(8,128)(2,1)S(1)}, bf16[128,1024]{1,0:T(8,128)(2,1)}, u32[]{:S(2)}) copy-start(bf16[128,1024]{1,0:T(8,128)(2,1)} %get-tuple-element.105.c2.ctx_ref) | copy-start | bytes 786436
  31.9 16.4 %copy-start.2 = (bf16[1024,512]{1,0:T(8,128)(2,1)S(1)}, bf16[1024,512]{1,0:T(8,128)(2,1)}, u32[]{:S(2)}) copy-start(bf16[1024,512]{1,0:T(8,128)(2,1)} %x_ref.17) | copy-start | bytes 3145732
  31.9 16.4 %copy-start.4 = (bf16[1024,512]{1,0:T(8,128)(2,1)S(1)}, bf16[1024,512]{1,0:T(8,128)(2,1)}, u32[]{:S(2)}) copy-start(bf16[1024,512]{1,0:T(8,128)(2,1)} %wd_own.1) | copy-start | bytes 3145732
  31.9 16.4 %copy-start.5 = (bf16[512,1024]{1,0:T(8,128)(2,1)S(1)}, bf16[512,1024]{1,0:T(8,128)(2,1)}, u32[]{:S(2)}) copy-start(bf16[512,1024]{1,0:T(8,128)(2,1)} %wu_own.1) | copy-start | bytes 3145732
  32.0 16.4 %copy-start.6 = (bf16[256,512]{1,0:T(8,128)(2,1)S(1)}, bf16[256,512]{1,0:T(8,128)(2,1)}, u32[]{:S(2)}) copy-start(bf16[256,512]{1,0:T(8,128)(2,1)} %wo_ref.3) | copy-start | bytes 786436
  32.0 16.4 %copy-start.10 = (bf16[1024,512]{1,0:T(8,128)(2,1)S(1)}, bf16[1024,512]{1,0:T(8,128)(2,1)}, u32[]{:S(2)}) copy-start(bf16[1024,512]{1,0:T(8,128)(2,1)} %cot_ref.1) | copy-start | bytes 3145732
  32.0 16.4 %copy-start.17 = (f32[1024]{0:T(1024)S(1)}, f32[1024]{0:T(1024)}, u32[]{:S(2)}) copy-start(f32[1024]{0:T(1024)} %param.24) | copy-start | bytes 12292
  32.0 16.4 %copy-start.18 = (f32[512]{0:T(512)S(1)}, f32[512]{0:T(512)}, u32[]{:S(2)}) copy-start(f32[512]{0:T(512)} %param.20) | copy-start | bytes 6148
  32.0 16.4 %copy-start.19 = (f32[512]{0:T(512)S(1)}, f32[512]{0:T(512)}, u32[]{:S(2)}) copy-start(f32[512]{0:T(512)} %param.21) | copy-start | bytes 6148
  32.0 16.4 %copy-start.20 = (f32[512]{0:T(512)S(1)}, f32[512]{0:T(512)}, u32[]{:S(2)}) copy-start(f32[512]{0:T(512)} %param.22) | copy-start | bytes 6148
  32.0 16.4 %copy-start.21 = (f32[512]{0:T(512)S(1)}, f32[512]{0:T(512)}, u32[]{:S(2)}) copy-start(f32[512]{0:T(512)} %param.26) | copy-start | bytes 6148
  32.0 16.4 %copy-start.22 = (f32[512]{0:T(512)S(1)}, f32[512]{0:T(512)}, u32[]{:S(2)}) copy-start(f32[512]{0:T(512)} %param.27) | copy-start | bytes 6148
  32.1 16.4 %copy-start.23 = (f32[512]{0:T(512)S(1)}, f32[512]{0:T(512)}, u32[]{:S(2)}) copy-start(f32[512]{0:T(512)} %param.28) | copy-start | bytes 6148
  32.1 13.1 %collective-permute-start.11 = (bf16[512,512]{1,0:T(8,128)(2,1)S(1)}, bf16[512,512]{1,0:T(8,128)(2,1)S(1)}, u32[]{:S(2)}, u32[]{:S(2)}) collective-permute-start(bf16[512,512]{1,0:T(8,128)(2,1)S(1)} %pad_maximum_fusion.wu_m), channel_id=1, source_target_pairs={{0,2},{2,0},{4,6},{6,4},{8,10},{10,8},{12,14},{14,12},{16,18},{18,... | collective-permute-start | bytes 1572872 | tf_op jit(solution)/shard_map/ppermute | solution.py:415
  36.2 2.1 %collective-permute-start.12 = (bf16[3,512,128]{2,1,0:T(8,128)(2,1)S(1)}, bf16[3,512,128]{2,1,0:T(8,128)(2,1)S(1)}, u32[]{:S(2)}, u32[]{:S(2)}) collective-permute-start(bf16[3,512,128]{2,1,0:T(8,128)(2,1)S(1)} %pad_maximum_fusion.4.w_ref.w_m), channel_id=1, source_target_pairs={{0,2},{2,0},{4,6},{6,4},{8,10},{10,8},{12,14},{14,12},{16,18},{18,... | collective-permute-start | bytes 1179656 | tf_op jit(solution)/shard_map/ppermute | solution.py:415
  36.3 8.9 %collective-permute-start.9 = (bf16[256,512]{1,0:T(8,128)(2,1)S(1)}, bf16[256,512]{1,0:T(8,128)(2,1)S(1)}, u32[]{:S(2)}, u32[]{:S(2)}) collective-permute-start(bf16[256,512]{1,0:T(8,128)(2,1)S(1)} %collective-permute-done.6), channel_id=1, source_target_pairs={{0,4},{2,6},{4,0},{6,2},{8,12},{10,14},{12,8},{14,10},{16,20},{18,... | collective-permute-start | bytes 786440 | tf_op jit(solution)/shard_map/ppermute | solution.py:415
  36.6 8.5 %collective-permute-start.10 = (bf16[64,512]{1,0:T(8,128)(2,1)S(1)}, bf16[64,512]{1,0:T(8,128)(2,1)S(1)}, u32[]{:S(2)}, u32[]{:S(2)}) collective-permute-start(bf16[64,512]{1,0:T(8,128)(2,1)S(1)} %collective-permute-done.7), channel_id=1, source_target_pairs={{0,4},{2,6},{4,0},{6,2},{8,12},{10,14},{12,8},{14,10},{16,20},{18,... | collective-permute-start | bytes 196616 | tf_op jit(solution)/shard_map/ppermute | solution.py:415
  38.3 8.3 %copy-start.12 = (bf16[3,512,128]{2,1,0:T(8,128)(2,1)}, bf16[3,512,128]{2,1,0:T(8,128)(2,1)S(1)}, u32[]{:S(2)}) copy-start(bf16[3,512,128]{2,1,0:T(8,128)(2,1)S(1)} %collective-permute-done.12.w_ref.w_p) | copy-start | bytes 1179652
  45.2 3.1 %collective-permute-start.14 = (bf16[512,512]{1,0:T(8,128)(2,1)S(1)}, bf16[512,512]{1,0:T(8,128)(2,1)S(1)}, u32[]{:S(2)}, u32[]{:S(2)}) collective-permute-start(bf16[512,512]{1,0:T(8,128)(2,1)S(1)} %pad_maximum_fusion.1.wd_m), channel_id=1, source_target_pairs={{0,2},{2,0},{4,6},{6,4},{8,10},{10,8},{12,14},{14,12},{16,18},{18,... | collective-permute-start | bytes 1572872 | tf_op jit(solution)/shard_map/ppermute | solution.py:415
  46.6 1.7 collective-permute-start.13
  81.1 4.5 %collective-permute-start.15 = (bf16[2,1024,512]{2,1,0:T(8,128)(2,1)}, bf16[2,1024,512]{2,1,0:T(8,128)(2,1)}, u32[]{:S(2)}, u32[]{:S(2)}) collective-permute-start(bf16[2,1024,512]{2,1,0:T(8,128)(2,1)} %get-tuple-element.123), channel_id=1, source_target_pairs={{0,2},{2,0},{4,6},{6,4},{8,10},{10,8},{12,14},{14,12},{16,18},{18,... | collective-permute-start | bytes 6291464 | tf_op jit(solution)/shard_map/ppermute | solution.py:415
  86.8 18.9 %collective-permute-start.17 = (bf16[512,512]{1,0:T(8,128)(2,1)S(1)}, bf16[512,512]{1,0:T(8,128)(2,1)S(1)}, u32[]{:S(2)}, u32[]{:S(2)}) collective-permute-start(bf16[512,512]{1,0:T(8,128)(2,1)S(1)} %fusion.rest_0_), channel_id=1, source_target_pairs={{0,1},{1,0},{2,3},{3,2},{4,5},{5,4},{6,7},{7,6},{8,9},{9,8},{10,11... | collective-permute-start | bytes 1572872 | tf_op jit(solution)/shard_map/ppermute | solution.py:411
  90.0 15.7 %collective-permute-start.18 = (bf16[2,256,512]{2,1,0:T(8,128)(2,1)S(1)}, bf16[2,256,512]{2,1,0:T(8,128)(2,1)S(1)}, u32[]{:S(2)}, u32[]{:S(2)}) collective-permute-start(bf16[2,256,512]{2,1,0:T(8,128)(2,1)S(1)} %pad_maximum_fusion.2.rest_1_), channel_id=1, source_target_pairs={{0,4},{2,6},{4,0},{6,2},{8,12},{10,14},{12,8},{14,10},{16,20},{18,... | collective-permute-start | bytes 1572872 | tf_op jit(solution)/shard_map/ppermute | solution.py:415
  91.4 4.9 %copy-start.30 = (bf16[3,128,1024]{2,1,0:T(8,128)(2,1)S(1)}, bf16[3,128,1024]{2,1,0:T(8,128)(2,1)}, u32[]{:S(2)}) copy-start(bf16[3,128,1024]{2,1,0:T(8,128)(2,1)} %get-tuple-element.127.qkv_ref) | copy-start | bytes 2359300
  95.6 5.1 %collective-permute-start.16 = (bf16[576,512]{1,0:T(8,128)(2,1)S(1)}, bf16[576,512]{1,0:T(8,128)(2,1)S(1)}, u32[]{:S(2)}, u32[]{:S(2)}) collective-permute-start(bf16[576,512]{1,0:T(8,128)(2,1)S(1)} %get-tuple-element.133.rest_0_), channel_id=1, source_target_pairs={{0,2},{2,0},{4,6},{6,4},{8,10},{10,8},{12,14},{14,12},{16,18},{18,... | collective-permute-start | bytes 1769480 | tf_op jit(solution)/shard_map/ppermute | solution.py:415
  96.3 5.1 %copy-start.7 = (bf16[256,512]{1,0:T(8,128)(2,1)S(1)}, bf16[256,512]{1,0:T(8,128)(2,1)}, u32[]{:S(2)}) copy-start(bf16[256,512]{1,0:T(8,128)(2,1)} %wo_ref.3) | copy-start | bytes 786436
  96.3 5.1 %copy-start.24 = (bf16[2,2,512,512]{3,2,1,0:T(8,128)(2,1)S(1)}, bf16[2,2,512,512]{3,2,1,0:T(8,128)(2,1)}, u32[]{:S(2)}) copy-start(bf16[2,2,512,512]{3,2,1,0:T(8,128)(2,1)} %get-tuple-element.125.e_ref) | copy-start | bytes 6291460
  96.3 5.1 %copy-start.25 = (bf16[3,128,1024]{2,1,0:T(8,128)(2,1)S(1)}, bf16[3,128,1024]{2,1,0:T(8,128)(2,1)}, u32[]{:S(2)}) copy-start(bf16[3,128,1024]{2,1,0:T(8,128)(2,1)} %get-tuple-element.124.qkv_ref) | copy-start | bytes 2359300
  96.3 5.0 %copy-start.27 = (bf16[128,1024]{1,0:T(8,128)(2,1)S(1)}, bf16[128,1024]{1,0:T(8,128)(2,1)}, u32[]{:S(2)}) copy-start(bf16[128,1024]{1,0:T(8,128)(2,1)} %get-tuple-element.100.c1.ctx_ref) | copy-start | bytes 786436
  96.3 5.0 %copy-start.36 = (f32[2,2,1,512]{3,2,1,0:T(1,128)S(1)}, f32[2,2,1,512]{3,2,1,0:T(1,128)}, u32[]{:S(2)}) copy-start(f32[2,2,1,512]{3,2,1,0:T(1,128)} %get-tuple-element.126.inv_ref) | copy-start | bytes 24580
  100.9 9.2 %collective-permute-start.19 = (bf16[288,512]{1,0:T(8,128)(2,1)S(1)}, bf16[288,512]{1,0:T(8,128)(2,1)S(1)}, u32[]{:S(2)}, u32[]{:S(2)}) collective-permute-start(bf16[288,512]{1,0:T(8,128)(2,1)S(1)} %add_convert_fusion.4.rest_0_), channel_id=1, source_target_pairs={{0,4},{2,6},{4,0},{6,2},{8,12},{10,14},{12,8},{14,10},{16,20},{18,... | collective-permute-start | bytes 884744 | tf_op jit(solution)/shard_map/ppermute | solution.py:415
  105.6 6.4 %copy-start.9 = (bf16[2,2,512,512]{3,2,1,0:T(8,128)(2,1)S(1)}, bf16[2,2,512,512]{3,2,1,0:T(8,128)(2,1)}, u32[]{:S(2)}) copy-start(bf16[2,2,512,512]{3,2,1,0:T(8,128)(2,1)} %get-tuple-element.118.e_ref) | copy-start | bytes 6291460
  105.6 6.4 %copy-start.11 = (bf16[3,128,1024]{2,1,0:T(8,128)(2,1)S(1)}, bf16[3,128,1024]{2,1,0:T(8,128)(2,1)}, u32[]{:S(2)}) copy-start(bf16[3,128,1024]{2,1,0:T(8,128)(2,1)} %get-tuple-element.117.qkv_ref) | copy-start | bytes 2359300
  105.6 6.4 %copy-start.15 = (bf16[128,1024]{1,0:T(8,128)(2,1)S(1)}, bf16[128,1024]{1,0:T(8,128)(2,1)}, u32[]{:S(2)}) copy-start(bf16[128,1024]{1,0:T(8,128)(2,1)} %get-tuple-element.97.c0.ctx_ref) | copy-start | bytes 786436
  105.6 6.4 %copy-start.16 = (f32[2,2,1,512]{3,2,1,0:T(1,128)S(1)}, f32[2,2,1,512]{3,2,1,0:T(1,128)}, u32[]{:S(2)}) copy-start(f32[2,2,1,512]{3,2,1,0:T(1,128)} %get-tuple-element.119.inv_ref) | copy-start | bytes 24580
  105.7 10.6 %collective-permute-start.20 = (bf16[576,512]{1,0:T(8,128)(2,1)S(1)}, bf16[576,512]{1,0:T(8,128)(2,1)S(1)}, u32[]{:S(2)}, u32[]{:S(2)}) collective-permute-start(bf16[576,512]{1,0:T(8,128)(2,1)S(1)} %get-tuple-element.146), channel_id=1, source_target_pairs={{0,2},{2,0},{4,6},{6,4},{8,10},{10,8},{12,14},{14,12},{16,18},{18,... | collective-permute-start | bytes 1769480 | tf_op jit(solution)/shard_map/ppermute | solution.py:415
  110.0 7.5 %collective-permute-start.21 = (bf16[256,512]{1,0:T(8,128)(2,1)S(1)}, bf16[256,512]{1,0:T(8,128)(2,1)S(1)}, u32[]{:S(2)}, u32[]{:S(2)}) collective-permute-start(bf16[256,512]{1,0:T(8,128)(2,1)S(1)} %fusion.4.rest_0_), channel_id=1, source_target_pairs={{0,4},{2,6},{4,0},{6,2},{8,12},{10,14},{12,8},{14,10},{16,20},{18,... | collective-permute-start | bytes 786440 | tf_op jit(solution)/shard_map/ppermute | solution.py:415
  110.4 7.2 %collective-permute-start.22 = (bf16[256,512]{1,0:T(8,128)(2,1)S(1)}, bf16[256,512]{1,0:T(8,128)(2,1)S(1)}, u32[]{:S(2)}, u32[]{:S(2)}) collective-permute-start(bf16[256,512]{1,0:T(8,128)(2,1)S(1)} %fusion.5.rest_1_), channel_id=1, source_target_pairs={{0,1},{1,0},{2,3},{3,2},{4,5},{5,4},{6,7},{7,6},{8,9},{9,8},{10,11... | collective-permute-start | bytes 786440 | tf_op jit(solution)/shard_map/ppermute | solution.py:411
  110.7 13.2 %collective-permute-start.23 = (bf16[288,512]{1,0:T(8,128)(2,1)S(1)}, bf16[288,512]{1,0:T(8,128)(2,1)S(1)}, u32[]{:S(2)}, u32[]{:S(2)}) collective-permute-start(bf16[288,512]{1,0:T(8,128)(2,1)S(1)} %add_convert_fusion.3.rest_2_), channel_id=1, source_target_pairs={{0,1},{1,0},{2,3},{3,2},{4,5},{5,4},{6,7},{7,6},{8,9},{9,8},{10,11... | collective-permute-start | bytes 884744 | tf_op jit(solution)/shard_map/ppermute | solution.py:411
  116.3 7.6 %collective-permute-start.24 = (bf16[288,512]{1,0:T(8,128)(2,1)S(1)}, bf16[288,512]{1,0:T(8,128)(2,1)}, u32[]{:S(2)}, u32[]{:S(2)}) collective-permute-start(bf16[288,512]{1,0:T(8,128)(2,1)S(1)} %add_convert_fusion.2.rest_0_), channel_id=1, source_target_pairs={{0,4},{2,6},{4,0},{6,2},{8,12},{10,14},{12,8},{14,10},{16,20},{18,... | collective-permute-start | bytes 884744 | tf_op jit(solution)/shard_map/ppermute | solution.py:415
  118.2 5.7 %collective-permute-start.25 = (bf16[256,512]{1,0:T(8,128)(2,1)S(1)}, bf16[256,512]{1,0:T(8,128)(2,1)S(1)}, u32[]{:S(2)}, u32[]{:S(2)}) collective-permute-start(bf16[256,512]{1,0:T(8,128)(2,1)S(1)} %fusion.7.rest_1_), channel_id=1, source_target_pairs={{0,8},{2,10},{4,12},{6,14},{8,0},{10,2},{12,4},{14,6},{16,24},{18,... | collective-permute-start | bytes 786440 | tf_op jit(solution)/shard_map/ppermute | solution.py:415
  124.6 13.7 %collective-permute-start.29 = (bf16[256,512]{1,0:T(8,128)(2,1)S(1)}, bf16[256,512]{1,0:T(8,128)(2,1)S(1)}, u32[]{:S(2)}, u32[]{:S(2)}) collective-permute-start(bf16[256,512]{1,0:T(8,128)(2,1)S(1)} %add_convert_fusion.6), channel_id=1, source_target_pairs={{0,16},{2,18},{4,20},{6,22},{8,24},{10,26},{12,28},{14,30},{16,0},... | collective-permute-start | bytes 786440 | tf_op jit(solution)/shard_map/ppermute | solution.py:415
  138.3 6.3 %collective-permute-start.30 = (bf16[256,512]{1,0:T(8,128)(2,1)S(1)}, bf16[256,512]{1,0:T(8,128)(2,1)S(1)}, u32[]{:S(2)}, u32[]{:S(2)}) collective-permute-start(bf16[256,512]{1,0:T(8,128)(2,1)S(1)} %add_convert_fusion.5), channel_id=1, source_target_pairs={{0,8},{2,10},{4,12},{6,14},{8,0},{10,2},{12,4},{14,6},{16,24},{18,... | collective-permute-start | bytes 786440 | tf_op jit(solution)/shard_map/ppermute | solution.py:415
  139.6 8.1 %collective-permute-start.26 = (bf16[144,512]{1,0:T(8,128)(2,1)S(1)}, bf16[144,512]{1,0:T(8,128)(2,1)S(1)}, u32[]{:S(2)}, u32[]{:S(2)}) collective-permute-start(bf16[144,512]{1,0:T(8,128)(2,1)S(1)} %constant_dynamic-slice_fusion), channel_id=1, source_target_pairs={{0,8},{2,10},{4,12},{6,14},{8,0},{10,2},{12,4},{14,6},{16,24},{18,... | collective-permute-start | bytes 442376 | tf_op jit(solution)/shard_map/ppermute | solution.py:415
  144.7 9.4 %collective-permute-start.31 = (bf16[512,512]{1,0:T(8,128)(2,1)S(1)}, bf16[512,512]{1,0:T(8,128)(2,1)S(1)}, u32[]{:S(2)}, u32[]{:S(2)}) collective-permute-start(bf16[512,512]{1,0:T(8,128)(2,1)S(1)} %pad_maximum_fusion.3.mine_near), channel_id=1, source_target_pairs={{0,4},{2,6},{4,0},{6,2},{8,12},{10,14},{12,8},{14,10},{16,20},{18,... | collective-permute-start | bytes 1572872 | tf_op jit(solution)/shard_map/ppermute | solution.py:415
  147.8 11.3 %collective-permute-start.27 = (bf16[144,512]{1,0:T(8,128)(2,1)S(1)}, bf16[144,512]{1,0:T(8,128)(2,1)S(1)}, u32[]{:S(2)}, u32[]{:S(2)}) collective-permute-start(bf16[144,512]{1,0:T(8,128)(2,1)S(1)} %add_convert_fusion.11), channel_id=1, source_target_pairs={{0,16},{2,18},{4,20},{6,22},{8,24},{10,26},{12,28},{14,30},{16,0},... | collective-permute-start | bytes 442376 | tf_op jit(solution)/shard_map/ppermute | solution.py:415
  149.6 16.6 %collective-permute-start.32 = (bf16[512,512]{1,0:T(8,128)(2,1)S(1)}, bf16[512,512]{1,0:T(8,128)(2,1)S(1)}, u32[]{:S(2)}, u32[]{:S(2)}) collective-permute-start(bf16[512,512]{1,0:T(8,128)(2,1)S(1)} %pad_maximum_fusion.3.mine_near), channel_id=1, source_target_pairs={{0,2},{2,0},{4,6},{6,4},{8,10},{10,8},{12,14},{14,12},{16,18},{18,... | collective-permute-start | bytes 1572872 | tf_op jit(solution)/shard_map/ppermute | solution.py:415
  154.1 12.1 %collective-permute-start.33 = (bf16[512,512]{1,0:T(8,128)(2,1)S(1)}, bf16[512,512]{1,0:T(8,128)(2,1)S(1)}, u32[]{:S(2)}, u32[]{:S(2)}) collective-permute-start(bf16[512,512]{1,0:T(8,128)(2,1)S(1)} %collective-permute-done.31.mine_far), channel_id=1, source_target_pairs={{0,2},{2,0},{4,6},{6,4},{8,10},{10,8},{12,14},{14,12},{16,18},{18,... | collective-permute-start | bytes 1572872 | tf_op jit(solution)/shard_map/ppermute | solution.py:415
  159.1 5.5 %collective-permute-start.28 = (bf16[144,512]{1,0:T(8,128)(2,1)S(1)}, bf16[144,512]{1,0:T(8,128)(2,1)S(1)}, u32[]{:S(2)}, u32[]{:S(2)}) collective-permute-start(bf16[144,512]{1,0:T(8,128)(2,1)S(1)} %add_convert_fusion.10), channel_id=1, source_target_pairs={{0,8},{2,10},{4,12},{6,14},{8,0},{10,2},{12,4},{14,6},{16,24},{18,... | collective-permute-start | bytes 442376 | tf_op jit(solution)/shard_map/ppermute | solution.py:415
  164.7 7.8 %collective-permute-start.34 = (bf16[288,512]{1,0:T(8,128)(2,1)S(1)}, bf16[288,512]{1,0:T(8,128)(2,1)S(1)}, u32[]{:S(2)}, u32[]{:S(2)}) collective-permute-start(bf16[288,512]{1,0:T(8,128)(2,1)S(1)} %pad_maximum_fusion.5.mine_near), channel_id=1, source_target_pairs={{0,4},{2,6},{4,0},{6,2},{8,12},{10,14},{12,8},{14,10},{16,20},{18,... | collective-permute-start | bytes 884744 | tf_op jit(solution)/shard_map/ppermute | solution.py:415
  165.2 9.1 %collective-permute-start.35 = (bf16[288,512]{1,0:T(8,128)(2,1)S(1)}, bf16[288,512]{1,0:T(8,128)(2,1)S(1)}, u32[]{:S(2)}, u32[]{:S(2)}) collective-permute-start(bf16[288,512]{1,0:T(8,128)(2,1)S(1)} %pad_maximum_fusion.5.mine_near), channel_id=1, source_target_pairs={{0,2},{2,0},{4,6},{6,4},{8,10},{10,8},{12,14},{14,12},{16,18},{18,... | collective-permute-start | bytes 884744 | tf_op jit(solution)/shard_map/ppermute | solution.py:415
  172.6 2.9 %collective-permute-start.36 = (bf16[288,512]{1,0:T(8,128)(2,1)S(1)}, bf16[288,512]{1,0:T(8,128)(2,1)S(1)}, u32[]{:S(2)}, u32[]{:S(2)}) collective-permute-start(bf16[288,512]{1,0:T(8,128)(2,1)S(1)} %collective-permute-done.34.mine_far), channel_id=1, source_target_pairs={{0,2},{2,0},{4,6},{6,4},{8,10},{10,8},{12,14},{14,12},{16,18},{18,... | collective-permute-start | bytes 884744 | tf_op jit(solution)/shard_map/ppermute | solution.py:415
  (19 other events, 40.4 us)
